TPU v7x, 256 devices: a whole 4x4x8 slice. The times are simulated.
256 devices in a mesh: section: 2 (over z_hi), dp: 8 (over y, core), mp: 16 (over z_lo, x).
Axes of the slice: x: 4, y: 4, z: 8 (z_hi: 2, z_lo: 4; z = z_hi * 4 + z_lo), core: 2. Of those that a mesh axis runs over, the one named last changes fastest.
Arguments:
- loss_sensitivity_outgoing: bfloat16 [2, 1536, 8192], P('section', ('dp', 'mp')), may hold values from -6 to 6
- expansion_factor: bfloat16 [2, 8192, 32768], P('section', 'dp', 'mp'), may hold values from -0.0508233 to 0.0508233
- contraction_factor: bfloat16 [2, 32768, 8192], P('section', 'mp', 'dp'), may hold values from -0.03125 to 0.03125
- intermediate_affine_values: bfloat16 [2, 1536, 32768], P('section', 'dp', 'mp'), may hold values from -6 to 6
- centered_unscaled_entry: bfloat16 [2, 1536, 8192], P('section', 'mp', 'dp'), may hold values from -4.5 to 4.5
- inverse_spread_per_position: float32 [2, 1536], P('section', 'mp'), may hold values from 0.3 to 3
- layernorm_multiplier: float32 [2, 8192], P('section', 'dp'), may hold values from 0.25 to 3
Outputs:
- grad_out: bfloat16 [2, 1536, 8192], P('section', 'mp', 'dp')
All inputs are finite; a program needn't handle non-finite values.
Results may differ from a plain program's by a relative error of at most 0.02.
Values may be sent and summed in bfloat16 or wider, within the bound.
No kernel may reach another device: no remote copies, remote signals or barrier semaphores. Data moves between devices by JAX's collectives and lax.ppermute only.
A program may use at most 64 MiB of HBM per device.

v0:
```python
import functools
import math

import jax
import jax.numpy as jnp
from jax import lax
from jax.experimental import pallas as pl
from jax.experimental.pallas import tpu as pltpu
from jax.sharding import Mesh, PartitionSpec as P

BF = jnp.bfloat16
F32 = jnp.float32
CHUNKS = 3
ROWS = 12 // CHUNKS


def near(core):
    return 1 + 2 * core


def wide(core):
    return 3 - 2 * core


def move_ring(array, axis, flip):
    pairs = [(c, i, c, i ^ flip(c)) for c in range(2) for i in range(4)]
    if axis == "y":
        return lax.ppermute(array, ("y", "core"), [(2 * i + c, 2 * j + d) for c, i, d, j in pairs])
    return lax.ppermute(array, ("core", axis), [(4 * c + i, 4 * d + j) for c, i, d, j in pairs])


def move_y(array, flip):
    return lax.ppermute(array, "y", [(y, y ^ flip) for y in range(4)])


def move_z(array, flip):
    return lax.ppermute(array, "z", [(z, z ^ flip) for z in range(4)])


def move_mirror(array):
    return lax.ppermute(array, ("section", "z"), [(i, 7 - i) for i in range(8)])


def move_core(array):
    return lax.ppermute(array, "core", [(0, 1), (1, 0)])


def flips(chunk):
    return (near, wide) if chunk % 2 == 0 else (wide, near)


def ring_order(chunk, core):
    first, second = flips(chunk)
    return 0, first(core), second(core), 2


def gelu_slope(u):
    c = math.sqrt(2.0 / math.pi)
    t = jnp.tanh(c * (u + 0.044715 * u * u * u))
    return 0.5 * (1.0 + t) + 0.5 * u * (1.0 - t * t) * c * (1.0 + 3.0 * 0.044715 * u * u)


def nt_dot(left, right):
    return lax.dot_general(left, right, (((1,), (1,)), ((), ())), preferred_element_type=F32)


def full(shape):
    return pl.BlockSpec(shape, lambda i: (0,) * len(shape))


SMEM = pl.BlockSpec(memory_space=pltpu.SMEM)


def slope_kernel(u, *outs):
    values = gelu_slope(u[...].astype(F32))
    for k in range(CHUNKS):
        pieces = []
        for x in range(4):
            for z in range(4):
                start = (4 * z + x) * 12 + ROWS * k
                pieces.append(values[start : start + ROWS])
        outs[k][...] = jnp.concatenate(pieces, axis=0)


def slope_rows(u):
    rows, width = u.shape
    tile = min(512, width)
    return pl.pallas_call(
        slope_kernel,
        grid=(width // tile,),
        in_specs=[pl.BlockSpec((rows, tile), lambda i: (0, i))],
        out_specs=[pl.BlockSpec((rows // CHUNKS, tile), lambda i: (0, i))] * CHUNKS,
        out_shape=[jax.ShapeDtypeStruct((rows // CHUNKS, width), F32)] * CHUNKS,
        compiler_params=pltpu.CompilerParams(vmem_limit_bytes=16 * 2**20),
        cost_estimate=pl.CostEstimate(flops=20 * rows * width, bytes_accessed=6 * rows * width, transcendentals=rows * width),
    )(u)


def hidden_kernel(chunk, pos, near_pair, wide_pair, weight, keep, send, mine, lhs):
    x, y, z, c = pos[0], pos[1], pos[2], pos[3]

    @pl.when(pl.program_id(0) == 0)
    def _():
        for c_rel in range(2):
            core = jnp.bitwise_xor(c, c_rel)
            for j, flip in enumerate(ring_order(chunk, core)):
                source = 2 * jnp.bitwise_xor(y, flip) + core
                for x_rel, x_flip in enumerate(ring_order(chunk, c)):
                    ref = near_pair if x_rel < 2 else wide_pair
                    lhs[4 * c_rel + j, jnp.bitwise_xor(x, x_flip)] = ref[x_rel % 2, source]
        source = 2 * z + x // 2
        for x_rel, x_flip in enumerate(ring_order(chunk, c)):
            ref = near_pair if x_rel < 2 else wide_pair
            rows = ref[x_rel % 2, source].astype(F32)
            picked = jnp.where(lax.rem(x, 2) == 0, rows[:8], rows[8:])
            mine[jnp.bitwise_xor(x, x_flip)] = picked

    rows = lhs[...].reshape(512, -1)
    product = nt_dot(rows, weight[...]).astype(BF)
    keep[...] = product[:256].reshape(keep.shape)
    send[...] = product[256:].reshape(send.shape)


def hidden_product(chunk, pos, near_pair, wide_pair, weight):
    width, depth = weight.shape
    tile = min(256, width)
    out_block = pl.BlockSpec((4, 64, tile), lambda i: (0, 0, i))
    return pl.pallas_call(
        functools.partial(hidden_kernel, chunk),
        grid=(width // tile,),
        in_specs=[
            SMEM,
            full(near_pair.shape),
            full(wide_pair.shape),
            pl.BlockSpec((tile, depth), lambda i: (i, 0)),
        ],
        out_specs=[out_block, out_block, full((4, 8, depth))],
        out_shape=[
            jax.ShapeDtypeStruct((4, 64, width), BF),
            jax.ShapeDtypeStruct((4, 64, width), BF),
            jax.ShapeDtypeStruct((4, 8, depth), F32),
        ],
        scratch_shapes=[pltpu.VMEM((8, 4, 16, depth), BF)],
        compiler_params=pltpu.CompilerParams(vmem_limit_bytes=16 * 2**20),
        cost_estimate=pl.CostEstimate(
            flops=2 * 512 * width * depth, bytes_accessed=2 * (width * depth + 512 * (width + depth)), transcendentals=0
        ),
    )(pos, near_pair, wide_pair, weight)


def feature_kernel(chunk, pos, near_same, wide_same, other, weight, keep, send, lhs, result):
    x, y, z, c = pos[0], pos[1], pos[2], pos[3]

    @pl.when(pl.program_id(0) == 0)
    def _():
        for j, flip in enumerate(ring_order(chunk, c)):
            lhs[2 * jnp.bitwise_xor(y, flip) + c] = (near_same if j < 2 else wide_same)[j % 2]
        for j, flip in enumerate(ring_order(chunk, 1 - c)):
            lhs[2 * jnp.bitwise_xor(y, flip) + 1 - c] = other[j]

    rows = lhs[...].reshape(512, -1)
    result[...] = nt_dot(rows, weight[...]).reshape(result.shape)
    for x_rel, x_flip in enumerate(ring_order(chunk, c)):
        to = jnp.bitwise_xor(x, x_flip)
        out = keep if x_rel < 2 else send
        for z_rel, z_flip in enumerate((0, 2, 1, 3)):
            rows = result[2 * jnp.bitwise_xor(z, z_flip) + to // 2, :, lax.rem(to, 2)]
            out[x_rel % 2, z_rel] = rows.reshape(32, -1).astype(BF)


def feature_product(chunk, pos, pairs, weight):
    width, depth = weight.shape
    tile = min(256, width)
    out_block = pl.BlockSpec((2, 4, 32, tile), lambda i: (0, 0, 0, i))
    return pl.pallas_call(
        functools.partial(feature_kernel, chunk),
        grid=(width // tile,),
        in_specs=[SMEM] + [full(pair.shape) for pair in pairs] + [pl.BlockSpec((tile, depth), lambda i: (i, 0))],
        out_specs=[out_block, out_block],
        out_shape=[jax.ShapeDtypeStruct((2, 4, 32, width), BF)] * 2,
        scratch_shapes=[pltpu.VMEM((8, 64, depth), BF), pltpu.VMEM((8, 4, 2, 8, tile), F32)],
        compiler_params=pltpu.CompilerParams(vmem_limit_bytes=20 * 2**20),
        cost_estimate=pl.CostEstimate(
            flops=2 * 512 * width * depth, bytes_accessed=2 * (width * depth + 512 * (width + depth)), transcendentals=0
        ),
    )(pos, *pairs, weight)


def add(*terms):
    return functools.reduce(jnp.add, [term.astype(F32) for term in terms])


def sort_flips(pieces, at):
    a0, a1, a2, a3 = pieces
    odd, high = at % 2 == 1, at >= 2
    a0, a1 = jnp.where(odd, a1, a0), jnp.where(odd, a0, a1)
    a2, a3 = jnp.where(odd, a3, a2), jnp.where(odd, a2, a3)
    a0, a2 = jnp.where(high, a2, a0), jnp.where(high, a0, a2)
    a1, a3 = jnp.where(high, a3, a1), jnp.where(high, a1, a3)
    return a0, a1, a2, a3


def own_features(rows, y, c):
    depth = rows.shape[1] // 8
    parts = [jnp.stack([rows[:, (2 * i + core) * depth :][:, :depth] for i in range(4)]) for core in range(2)]
    low = c == 0
    mine = jnp.where(low, parts[0], parts[1])
    other = move_core(jnp.where(low, parts[1], parts[0]))
    both = jnp.stack([jnp.where(low, mine, other), jnp.where(low, other, mine)], axis=1)

    def blocks(*flips_y):
        return jnp.stack([lax.dynamic_index_in_dim(both, y ^ flip, 0, keepdims=False) for flip in flips_y])

    moved = move_y(blocks(1, 2), 1)
    kept = blocks(0, 3)
    far = move_y(jnp.stack([kept[1], moved[1]]), 3)
    return jnp.concatenate(sort_flips((kept[0], moved[0], far[1], far[0]), y)).transpose(1, 0, 2)


def gather_z(rows, z):
    a3 = move_mirror(rows)
    a1 = move_z(a3, 2)
    a2, a0 = move_z(jnp.stack([a3, a1]), 1)
    pieces = sort_flips((a0, a1, a2, a3), z)
    starts = range(0, rows.shape[0], ROWS)
    return [jnp.concatenate([piece[at : at + ROWS] for piece in pieces]).transpose(1, 0, 2) for at in starts]


def gather_ring(chunk, block, axis):
    first, second = flips(chunk)
    pair = jnp.stack([block, move_ring(block, axis, first)])
    return pair, move_ring(pair, axis, second)


def reduce_hidden(chunk, keep, send):
    second, first = flips(chunk)
    other = move_core(send)
    far = move_ring(add(keep[2:], other[2:]).astype(BF), "y", first)
    last = move_ring(add(keep[1], other[1], far[1]).astype(BF), "y", second)
    return add(keep[0], other[0], far[0], last)


def reduce_x(chunk, keep, send):
    second, first = flips(chunk)
    far = move_ring(send, "x", first)
    last = move_ring(add(keep[1], far[1]).astype(BF), "x", second)
    return add(keep[0], far[0], last)


def reduce_z(totals):
    total = jnp.stack(totals, axis=1)
    far = move_z(total[2:].astype(BF), 1)
    last = move_z(add(total[1], far[1]).astype(BF), 2)
    return list(add(total[0], far[0], last))


def sum_over_dp(array):
    array = array + move_core(array)
    array = array + move_y(array, 1)
    return array + move_y(array, 3)


def per_device(
    loss_sensitivity_outgoing,
    expansion_factor,
    contraction_factor,
    intermediate_affine_values,
    centered_unscaled_entry,
    inverse_spread_per_position,
    layernorm_multiplier,
):
    x, y, z, c = (lax.axis_index(name) for name in ("x", "y", "z", "core"))
    pos = jnp.stack([x, y, z, c]).astype(jnp.int32)
    model = 8 * expansion_factor.shape[1]
    rows = own_features(loss_sensitivity_outgoing[0], y, c)
    slope = slope_rows(intermediate_affine_values[0])

    def by_chunk(array):
        rest = array.shape[1:]
        array = array.reshape(2, 4, CHUNKS, ROWS, *rest)
        array = array.transpose(2, 1, 0, 3, *range(4, array.ndim))
        return array.reshape(CHUNKS, 32, *rest)

    entry = by_chunk(centered_unscaled_entry[0]).astype(F32)
    spread = by_chunk(inverse_spread_per_position[0])
    gain = layernorm_multiplier[0]

    rows, slope = lax.optimization_barrier((rows, slope))
    parts = gather_z(rows[:ROWS], z) + gather_z(rows[ROWS:], z)
    mine, totals = [], []
    for k in range(CHUNKS):
        keep, send, own_rows = hidden_product(k, pos, *gather_ring(k, parts[k], "x"), contraction_factor[0])
        block = (reduce_hidden(k, keep, send) * slope[k]).astype(BF)
        near_pair, wide_pair = gather_ring(k, block, "y")
        other = move_core(jnp.concatenate([near_pair, wide_pair]))
        keep, send = feature_product(k, pos, (near_pair, wide_pair, other), expansion_factor[0])
        mine.append(own_rows.reshape(32, -1))
        totals.append(reduce_x(k, keep, send))
    scaled = [gain * total for total in reduce_z(totals[:2]) + reduce_z(totals[2:])]
    scaled = jnp.stack(scaled)
    upstream = jnp.stack(mine)
    sums = sum_over_dp(jnp.stack([jnp.sum(scaled, axis=2), jnp.sum(scaled * entry, axis=2)]))
    result = upstream + spread[:, :, None] * (
        scaled - sums[0][:, :, None] / model - entry * sums[1][:, :, None] / model
    )
    result = result.reshape(CHUNKS, 4, 2, ROWS, -1).transpose(2, 1, 0, 3, 4)
    return result.reshape(1, 96, -1).astype(BF)


def solution(mesh):
    split = Mesh(mesh.devices.reshape(2, 4, 2, 4, 4), ("section", "y", "core", "z", "x"))
    dp, mp = ("y", "core"), ("z", "x")
    in_specs = (
        P("section", dp + mp, None),
        P("section", dp, mp),
        P("section", mp, dp),
        P("section", dp, mp),
        P("section", mp, dp),
        P("section", mp),
        P("section", dp),
    )
    out_specs = P("section", mp, dp)
    return jax.shard_map(per_device, mesh=split, in_specs=in_specs, out_specs=out_specs, check_vma=False)
```

profile of v0, /device:TPU:1, one launch (start us, length us, event | category | flops | bytes accessed | tf_op | source)
XLA Modules:
  0.0 213.7 jit_solution(2096072233657679753)
XLA Ops:
  1.0 3.3 %collective-permute-start = (bf16[4,12,1024]{2,1,0:T(8,128)(2,1)S(1)}, bf16[4,12,1024]{2,1,0:T(8,128)(2,1)S(1)}, u32[]{:S(2)}, u32[]{:S(2)}) collective-permute-start(bf16[4,12,1024]{2,1,0:T(8,128)(2,1)S(1)} %broadcast_select_fusion.8), channel_id=1, source_target_pairs={{0,16},{16,0},{1,17},{17,1},{2,18},{18,2},{3,19},{19,3},{4,20},{20... | collective-permute-start | bytes 294920 | tf_op jit(solution)/shard_map/ppermute | solution.py:45
  5.5 4.7 %collective-permute-done.1 = bf16[2,2,12,1024]{3,2,1,0:T(8,128)(2,1)S(1)} collective-permute-done((bf16[2,2,12,1024]{3,2,1,0:T(8,128)(2,1)S(1)}, bf16[2,2,12,1024]{3,2,1,0:T(8,128)(2,1)S(1)}, u32[]{:S(2)}, u32[]{:S(2)}) %collective-permute-start.1) | collective-permute-done | bytes 98336 | tf_op jit(solution)/shard_map/ppermute | solution.py:33
  15.5 4.1 %collective-permute-start.3 = (bf16[4,8,1024]{2,0,1:T(4,128)(2,1)S(1)}, bf16[4,8,1024]{2,0,1:T(4,128)(2,1)S(1)}, u32[]{:S(2)}, u32[]{:S(2)}) collective-permute-start(bf16[4,8,1024]{2,0,1:T(4,128)(2,1)S(1)} %slice.239), channel_id=1, source_target_pairs={{0,140},{4,136},{8,132},{12,128},{128,12},{132,8},{136,4},{140,0},... | collective-permute-start | bytes 196616 | tf_op jit(solution)/shard_map/ppermute | solution.py:41
  23.5 3.5 %collective-permute-start.8 = (bf16[8,8,1024]{2,0,1:T(8,128)(2,1)S(1)}, bf16[8,8,1024]{2,0,1:T(8,128)(2,1)S(1)}, u32[]{:S(2)}, u32[]{:S(2)}) collective-permute-start(bf16[8,8,1024]{2,0,1:T(8,128)(2,1)S(1)} %slice.240), channel_id=1, source_target_pairs={{0,140},{4,136},{8,132},{12,128},{128,12},{132,8},{136,4},{140,0},... | collective-permute-start | bytes 393224 | tf_op jit(solution)/shard_map/ppermute | solution.py:41
  27.7 3.1 %collective-permute-done.8 = bf16[8,8,1024]{2,0,1:T(8,128)(2,1)S(1)} collective-permute-done((bf16[8,8,1024]{2,0,1:T(8,128)(2,1)S(1)}, bf16[8,8,1024]{2,0,1:T(8,128)(2,1)S(1)}, u32[]{:S(2)}, u32[]{:S(2)}) %collective-permute-start.8) | collective-permute-done | bytes 131104 | tf_op jit(solution)/shard_map/ppermute | solution.py:41
  39.0 4.6 %collective-permute-done.10 = bf16[2,8,8,1024]{3,1,2,0:T(8,128)(2,1)S(1)} collective-permute-done((bf16[2,8,8,1024]{3,1,2,0:T(8,128)(2,1)S(1)}, bf16[2,8,8,1024]{3,1,2,0:T(8,128)(2,1)S(1)}, u32[]{:S(2)}, u32[]{:S(2)}) %collective-permute-start.10) | collective-permute-done | bytes 262176 | tf_op jit(solution)/shard_map/ppermute | solution.py:37
  49.0 3.8 %collective-permute-done.11 = bf16[8,16,1024]{2,1,0:T(8,128)(2,1)S(1)} collective-permute-done((bf16[8,16,1024]{2,1,0:T(8,128)(2,1)S(1)}, bf16[8,16,1024]{2,1,0:T(8,128)(2,1)S(1)}, u32[]{:S(2)}, u32[]{:S(2)}) %collective-permute-start.11) | collective-permute-done | bytes 262176 | tf_op jit(solution)/shard_map/ppermute | solution.py:29
  57.5 4.8 %shard_map.74 = (bf16[4,64,2048]{2,1,0:T(8,128)(2,1)S(1)}, bf16[4,64,2048]{2,1,0:T(8,128)(2,1)S(1)}, f32[4,8,1024]{2,1,0:T(8,128)S(1)}) custom-call(s32[4]{0:T(128)S(1)} %pad_add_fusion.pos, bf16[2,8,16,1024]{3,2,1,0:T(8,128)(2,1)S(1)} %pad_maximum_fusion.3.near_pair, bf16[2,8,16,1024]{3,2,1,0:T(8,128)(2,1)S(1)} %collective-permute-done.7.wide_pair, ...), custom_call_target="tpu_custom_call" | custom-call | flops 2147483648 | bytes 7340032 | tf_op jit(solution)/shard_map/pallas_call | solution.py:128
  62.4 13.0 %collective-permute-start.15 = (bf16[4,64,2048]{2,1,0:T(8,128)(2,1)S(1)}, bf16[4,64,2048]{2,1,0:T(8,128)(2,1)S(1)}, u32[]{:S(2)}, u32[]{:S(2)}) collective-permute-start(bf16[4,64,2048]{2,1,0:T(8,128)(2,1)S(1)} %get-tuple-element.35), channel_id=1, source_target_pairs={{0,16},{16,0},{1,17},{17,1},{2,18},{18,2},{3,19},{19,3},{4,20},{20... | collective-permute-start | bytes 3145736 | tf_op jit(solution)/shard_map/ppermute | solution.py:45
  77.3 4.8 %shard_map.75 = (bf16[4,64,2048]{2,1,0:T(8,128)(2,1)S(1)}, bf16[4,64,2048]{2,1,0:T(8,128)(2,1)S(1)}, f32[4,8,1024]{2,1,0:T(8,128)S(1)}) custom-call(s32[4]{0:T(128)S(1)} %pad_add_fusion.pos, bf16[2,8,16,1024]{3,2,1,0:T(8,128)(2,1)S(1)} %pad_maximum_fusion.4.near_pair, bf16[2,8,16,1024]{3,2,1,0:T(8,128)(2,1)S(1)} %collective-permute-done.12.wide_pair, ...), custom_call_target="tpu_custom_call" | custom-call | flops 2147483648 | bytes 7340032 | tf_op jit(solution)/shard_map/pallas_call | solution.py:128
  84.1 4.8 %shard_map.76 = (bf16[4,64,2048]{2,1,0:T(8,128)(2,1)S(1)}, bf16[4,64,2048]{2,1,0:T(8,128)(2,1)S(1)}, f32[4,8,1024]{2,1,0:T(8,128)S(1)}) custom-call(s32[4]{0:T(128)S(1)} %pad_add_fusion.pos, bf16[2,8,16,1024]{3,2,1,0:T(8,128)(2,1)S(1)} %pad_maximum_fusion.5.near_pair, bf16[2,8,16,1024]{3,2,1,0:T(8,128)(2,1)S(1)} %collective-permute-done.14.wide_pair, ...), custom_call_target="tpu_custom_call" | custom-call | flops 2147483648 | bytes 7340032 | tf_op jit(solution)/shard_map/pallas_call | solution.py:128
  93.7 7.9 %collective-permute-done.16 = bf16[2,64,2048]{2,1,0:T(8,128)(2,1)S(1)} collective-permute-done((bf16[2,64,2048]{2,1,0:T(8,128)(2,1)S(1)}, bf16[2,64,2048]{2,1,0:T(8,128)(2,1)S(1)}, u32[]{:S(2)}, u32[]{:S(2)}) %collective-permute-start.16) | collective-permute-done | bytes 524320 | tf_op jit(solution)/shard_map/ppermute | solution.py:28
  101.7 4.5 %collective-permute-start.17 = (bf16[64,2048]{1,0:T(8,128)(2,1)S(1)}, bf16[64,2048]{1,0:T(8,128)(2,1)S(1)}, u32[]{:S(2)}, u32[]{:S(2)}) collective-permute-start(bf16[64,2048]{1,0:T(8,128)(2,1)S(1)} %fusion.15), channel_id=1, source_target_pairs={{0,32},{32,0},{64,96},{96,64},{16,112},{48,80},{80,48},{112,16},{1... | collective-permute-start | bytes 786440 | tf_op jit(solution)/shard_map/ppermute | solution.py:28
  106.5 3.5 %collective-permute-done.17 = bf16[64,2048]{1,0:T(8,128)(2,1)S(1)} collective-permute-done((bf16[64,2048]{1,0:T(8,128)(2,1)S(1)}, bf16[64,2048]{1,0:T(8,128)(2,1)S(1)}, u32[]{:S(2)}, u32[]{:S(2)}) %collective-permute-start.17) | collective-permute-done | bytes 262176 | tf_op jit(solution)/shard_map/ppermute | solution.py:28
  113.2 4.5 %collective-permute-done.34 = bf16[2,64,2048]{2,1,0:T(8,128)(2,1)S(1)} collective-permute-done((bf16[2,64,2048]{2,1,0:T(8,128)(2,1)S(1)}, bf16[2,64,2048]{2,1,0:T(8,128)(2,1)S(1)}, u32[]{:S(2)}, u32[]{:S(2)}) %collective-permute-start.34) | collective-permute-done | bytes 524320 | tf_op jit(solution)/shard_map/ppermute | solution.py:28
  121.8 4.7 %collective-permute-done.35 = bf16[64,2048]{1,0:T(8,128)(2,1)S(1)} collective-permute-done((bf16[64,2048]{1,0:T(8,128)(2,1)S(1)}, bf16[64,2048]{1,0:T(8,128)(2,1)S(1)}, u32[]{:S(2)}, u32[]{:S(2)}) %collective-permute-start.35) | collective-permute-done | bytes 262176 | tf_op jit(solution)/shard_map/ppermute | solution.py:28
  127.3 8.1 %collective-permute-done.26 = bf16[64,2048]{1,0:T(8,128)(2,1)S(1)} collective-permute-done((bf16[64,2048]{1,0:T(8,128)(2,1)S(1)}, bf16[64,2048]{1,0:T(8,128)(2,1)S(1)}, u32[]{:S(2)}, u32[]{:S(2)}) %collective-permute-start.26) | collective-permute-done | bytes 262176 | tf_op jit(solution)/shard_map/ppermute | solution.py:28
  137.1 6.2 %collective-permute-start.20 = (bf16[4,64,2048]{2,1,0:T(8,128)(2,1)S(1)}, bf16[4,64,2048]{2,1,0:T(8,128)(2,1)S(1)}, u32[]{:S(2)}, u32[]{:S(2)}) collective-permute-start(bf16[4,64,2048]{2,1,0:T(8,128)(2,1)S(1)} %pad_maximum_fusion), channel_id=1, source_target_pairs={{0,16},{16,0},{1,17},{17,1},{2,18},{18,2},{3,19},{19,3},{4,20},{20... | collective-permute-start | bytes 3145736 | tf_op jit(solution)/shard_map/ppermute | solution.py:45
  145.7 5.8 %collective-permute-start.28 = (bf16[4,64,2048]{2,1,0:T(8,128)(2,1)S(1)}, bf16[4,64,2048]{2,1,0:T(8,128)(2,1)S(1)}, u32[]{:S(2)}, u32[]{:S(2)}) collective-permute-start(bf16[4,64,2048]{2,1,0:T(8,128)(2,1)S(1)} %pad_maximum_fusion.1), channel_id=1, source_target_pairs={{0,16},{16,0},{1,17},{17,1},{2,18},{18,2},{3,19},{19,3},{4,20},{20... | collective-permute-start | bytes 3145736 | tf_op jit(solution)/shard_map/ppermute | solution.py:45
  151.7 4.0 %shard_map.77 = (bf16[2,4,32,1024]{3,2,1,0:T(8,128)(2,1)S(1)}, bf16[2,4,32,1024]{3,2,1,0:T(8,128)(2,1)S(1)}) custom-call(s32[4]{0:T(128)S(1)} %pad_add_fusion.pos, bf16[2,64,2048]{2,1,0:T(8,128)(2,1)S(1)} %pad_maximum_fusion.6.near_same, bf16[2,64,2048]{2,1,0:T(8,128)(2,1)S(1)} %collective-permute-done.19.wide_same, ...), custom_call_target="tpu_custom_call" | custom-call | flops 2147483648 | bytes 7340032 | tf_op jit(solution)/shard_map/pallas_call | solution.py:175
  156.6 4.0 %shard_map.78 = (bf16[2,4,32,1024]{3,2,1,0:T(8,128)(2,1)S(1)}, bf16[2,4,32,1024]{3,2,1,0:T(8,128)(2,1)S(1)}) custom-call(s32[4]{0:T(128)S(1)} %pad_add_fusion.pos, bf16[2,64,2048]{2,1,0:T(8,128)(2,1)S(1)} %pad_maximum_fusion.7.near_same, bf16[2,64,2048]{2,1,0:T(8,128)(2,1)S(1)} %collective-permute-done.27.wide_same, ...), custom_call_target="tpu_custom_call" | custom-call | flops 2147483648 | bytes 7340032 | tf_op jit(solution)/shard_map/pallas_call | solution.py:175
  162.7 4.6 %shard_map.79 = (bf16[2,4,32,1024]{3,2,1,0:T(8,128)(2,1)S(1)}, bf16[2,4,32,1024]{3,2,1,0:T(8,128)(2,1)}) custom-call(s32[4]{0:T(128)S(1)} %pad_add_fusion.pos, bf16[2,64,2048]{2,1,0:T(8,128)(2,1)S(1)} %pad_maximum_fusion.8.near_same, bf16[2,64,2048]{2,1,0:T(8,128)(2,1)S(1)} %collective-permute-done.37.wide_same, ...), custom_call_target="tpu_custom_call" | custom-call | flops 2147483648 | bytes 7340032 | tf_op jit(solution)/shard_map/pallas_call | solution.py:175
  173.1 7.2 %collective-permute-done.39 = bf16[2,4,32,1024]{3,2,1,0:T(8,128)(2,1)} collective-permute-done((bf16[2,4,32,1024]{3,2,1,0:T(8,128)(2,1)}, bf16[2,4,32,1024]{3,2,1,0:T(8,128)(2,1)}, u32[]{:S(2)}, u32[]{:S(2)}) %collective-permute-start.39) | collective-permute-done | bytes 524320 | tf_op jit(solution)/shard_map/ppermute | solution.py:29
  197.0 6.0 %collective-permute-done.42 = bf16[1,32,1024]{2,1,0:T(8,128)(2,1)S(1)} collective-permute-done((bf16[1,32,1024]{2,1,0:T(8,128)(2,1)S(1)}, bf16[1,32,1024]{2,1,0:T(8,128)(2,1)S(1)}, u32[]{:S(2)}, u32[]{:S(2)}) %collective-permute-start.42) | collective-permute-done | bytes 65568 | tf_op jit(solution)/shard_map/ppermute | solution.py:37
  (170 shorter events, 87.2 us)
Async XLA Ops:
  38.9 16.5 %collective-permute-start.7 = (bf16[2,8,16,1024]{3,2,1,0:T(8,128)(2,1)S(1)}, bf16[2,8,16,1024]{3,2,1,0:T(8,128)(2,1)S(1)}, u32[]{:S(2)}, u32[]{:S(2)}) collective-permute-start(bf16[2,8,16,1024]{3,2,1,0:T(8,128)(2,1)S(1)} %pad_maximum_fusion.3.near_pair), channel_id=1, source_target_pairs={{0,3},{1,2},{2,1},{3,0},{16,17},{17,16},{18,19},{19,18},{4,7},{5,6... | collective-permute-start | bytes 1572872 | tf_op jit(solution)/shard_map/ppermute | solution.py:29
  47.1 28.4 %collective-permute-start.13 = (bf16[8,16,1024]{2,1,0:T(8,128)(2,1)S(1)}, bf16[8,16,1024]{2,1,0:T(8,128)(2,1)S(1)}, u32[]{:S(2)}, u32[]{:S(2)}) collective-permute-start(bf16[8,16,1024]{2,1,0:T(8,128)(2,1)S(1)} %get-tuple-element.63), channel_id=1, source_target_pairs={{0,1},{1,0},{2,3},{3,2},{16,19},{17,18},{18,17},{19,16},{4,5},{5,4... | collective-permute-start | bytes 786440 | tf_op jit(solution)/shard_map/ppermute | solution.py:29
  52.8 24.5 %collective-permute-start.12 = (bf16[2,8,16,1024]{3,2,1,0:T(8,128)(2,1)S(1)}, bf16[2,8,16,1024]{3,2,1,0:T(8,128)(2,1)S(1)}, u32[]{:S(2)}, u32[]{:S(2)}) collective-permute-start(bf16[2,8,16,1024]{3,2,1,0:T(8,128)(2,1)S(1)} %pad_maximum_fusion.4.near_pair), channel_id=1, source_target_pairs={{0,1},{1,0},{2,3},{3,2},{16,19},{17,18},{18,17},{19,16},{4,5},{5,4... | collective-permute-start | bytes 1572872 | tf_op jit(solution)/shard_map/ppermute | solution.py:29
  62.4 28.5 %collective-permute-start.15 = (bf16[4,64,2048]{2,1,0:T(8,128)(2,1)S(1)}, bf16[4,64,2048]{2,1,0:T(8,128)(2,1)S(1)}, u32[]{:S(2)}, u32[]{:S(2)}) collective-permute-start(bf16[4,64,2048]{2,1,0:T(8,128)(2,1)S(1)} %get-tuple-element.35), channel_id=1, source_target_pairs={{0,16},{16,0},{1,17},{17,1},{2,18},{18,2},{3,19},{19,3},{4,20},{20... | collective-permute-start | bytes 3145736 | tf_op jit(solution)/shard_map/ppermute | solution.py:45
  82.1 9.0 %collective-permute-start.23 = (bf16[4,64,2048]{2,1,0:T(8,128)(2,1)S(1)}, bf16[4,64,2048]{2,1,0:T(8,128)(2,1)S(1)}, u32[]{:S(2)}, u32[]{:S(2)}) collective-permute-start(bf16[4,64,2048]{2,1,0:T(8,128)(2,1)S(1)} %get-tuple-element.40), channel_id=1, source_target_pairs={{0,16},{16,0},{1,17},{17,1},{2,18},{18,2},{3,19},{19,3},{4,20},{20... | collective-permute-start | bytes 3145736 | tf_op jit(solution)/shard_map/ppermute | solution.py:45
  89.0 17.3 %collective-permute-start.33 = (bf16[4,64,2048]{2,1,0:T(8,128)(2,1)S(1)}, bf16[4,64,2048]{2,1,0:T(8,128)(2,1)S(1)}, u32[]{:S(2)}, u32[]{:S(2)}) collective-permute-start(bf16[4,64,2048]{2,1,0:T(8,128)(2,1)S(1)} %get-tuple-element.45), channel_id=1, source_target_pairs={{0,16},{16,0},{1,17},{17,1},{2,18},{18,2},{3,19},{19,3},{4,20},{20... | collective-permute-start | bytes 3145736 | tf_op jit(solution)/shard_map/ppermute | solution.py:45
  91.0 10.6 %collective-permute-start.16 = (bf16[2,64,2048]{2,1,0:T(8,128)(2,1)S(1)}, bf16[2,64,2048]{2,1,0:T(8,128)(2,1)S(1)}, u32[]{:S(2)}, u32[]{:S(2)}) collective-permute-start(bf16[2,64,2048]{2,1,0:T(8,128)(2,1)S(1)} %add_convert_fusion.2), channel_id=1, source_target_pairs={{0,96},{32,64},{64,32},{96,0},{16,48},{48,16},{80,112},{112,80},{1... | collective-permute-start | bytes 1572872 | tf_op jit(solution)/shard_map/ppermute | solution.py:28
  91.3 21.7 %collective-permute-start.24 = (bf16[2,64,2048]{2,1,0:T(8,128)(2,1)S(1)}, bf16[2,64,2048]{2,1,0:T(8,128)(2,1)S(1)}, u32[]{:S(2)}, u32[]{:S(2)}) collective-permute-start(bf16[2,64,2048]{2,1,0:T(8,128)(2,1)S(1)} %add_convert_fusion.1), channel_id=1, source_target_pairs={{0,32},{32,0},{64,96},{96,64},{16,112},{48,80},{80,48},{112,16},{1... | collective-permute-start | bytes 1572872 | tf_op jit(solution)/shard_map/ppermute | solution.py:28
  106.4 11.2 %collective-permute-start.34 = (bf16[2,64,2048]{2,1,0:T(8,128)(2,1)S(1)}, bf16[2,64,2048]{2,1,0:T(8,128)(2,1)S(1)}, u32[]{:S(2)}, u32[]{:S(2)}) collective-permute-start(bf16[2,64,2048]{2,1,0:T(8,128)(2,1)S(1)} %add_convert_fusion), channel_id=1, source_target_pairs={{0,96},{32,64},{64,32},{96,0},{16,48},{48,16},{80,112},{112,80},{1... | collective-permute-start | bytes 1572872 | tf_op jit(solution)/shard_map/ppermute | solution.py:28
  110.2 9.7 %collective-permute-start.18 = (bf16[64,2048]{1,0:T(8,128)(2,1)S(1)}, bf16[64,2048]{1,0:T(8,128)(2,1)S(1)}, u32[]{:S(2)}, u32[]{:S(2)}) collective-permute-start(bf16[64,2048]{1,0:T(8,128)(2,1)S(1)} %fusion.9), channel_id=1, source_target_pairs={{0,32},{32,0},{64,96},{96,64},{16,112},{48,80},{80,48},{112,16},{1... | collective-permute-start | bytes 786440 | tf_op jit(solution)/shard_map/ppermute | solution.py:28
  117.7 8.7 %collective-permute-start.35 = (bf16[64,2048]{1,0:T(8,128)(2,1)S(1)}, bf16[64,2048]{1,0:T(8,128)(2,1)S(1)}, u32[]{:S(2)}, u32[]{:S(2)}) collective-permute-start(bf16[64,2048]{1,0:T(8,128)(2,1)S(1)} %fusion.19), channel_id=1, source_target_pairs={{0,32},{32,0},{64,96},{96,64},{16,112},{48,80},{80,48},{112,16},{1... | collective-permute-start | bytes 786440 | tf_op jit(solution)/shard_map/ppermute | solution.py:28
  120.0 17.0 %collective-permute-start.19 = (bf16[2,64,2048]{2,1,0:T(8,128)(2,1)S(1)}, bf16[2,64,2048]{2,1,0:T(8,128)(2,1)S(1)}, u32[]{:S(2)}, u32[]{:S(2)}) collective-permute-start(bf16[2,64,2048]{2,1,0:T(8,128)(2,1)S(1)} %pad_maximum_fusion.6.near_same), channel_id=1, source_target_pairs={{0,96},{32,64},{64,32},{96,0},{16,48},{48,16},{80,112},{112,80},{1... | collective-permute-start | bytes 1572872 | tf_op jit(solution)/shard_map/ppermute | solution.py:28
  121.3 14.1 %collective-permute-start.26 = (bf16[64,2048]{1,0:T(8,128)(2,1)S(1)}, bf16[64,2048]{1,0:T(8,128)(2,1)S(1)}, u32[]{:S(2)}, u32[]{:S(2)}) collective-permute-start(bf16[64,2048]{1,0:T(8,128)(2,1)S(1)} %fusion.6), channel_id=1, source_target_pairs={{0,96},{32,64},{64,32},{96,0},{16,48},{48,16},{80,112},{112,80},{1... | collective-permute-start | bytes 786440 | tf_op jit(solution)/shard_map/ppermute | solution.py:28
  126.6 10.2 %collective-permute-start.36 = (bf16[64,2048]{1,0:T(8,128)(2,1)S(1)}, bf16[64,2048]{1,0:T(8,128)(2,1)S(1)}, u32[]{:S(2)}, u32[]{:S(2)}) collective-permute-start(bf16[64,2048]{1,0:T(8,128)(2,1)S(1)} %fusion.3), channel_id=1, source_target_pairs={{0,32},{32,0},{64,96},{96,64},{16,112},{48,80},{80,48},{112,16},{1... | collective-permute-start | bytes 786440 | tf_op jit(solution)/shard_map/ppermute | solution.py:28
  135.4 10.2 %collective-permute-start.27 = (bf16[2,64,2048]{2,1,0:T(8,128)(2,1)S(1)}, bf16[2,64,2048]{2,1,0:T(8,128)(2,1)S(1)}, u32[]{:S(2)}, u32[]{:S(2)}) collective-permute-start(bf16[2,64,2048]{2,1,0:T(8,128)(2,1)S(1)} %pad_maximum_fusion.7.near_same), channel_id=1, source_target_pairs={{0,32},{32,0},{64,96},{96,64},{16,112},{48,80},{80,48},{112,16},{1... | collective-permute-start | bytes 1572872 | tf_op jit(solution)/shard_map/ppermute | solution.py:28
  136.9 14.6 %collective-permute-start.37 = (bf16[2,64,2048]{2,1,0:T(8,128)(2,1)S(1)}, bf16[2,64,2048]{2,1,0:T(8,128)(2,1)S(1)}, u32[]{:S(2)}, u32[]{:S(2)}) collective-permute-start(bf16[2,64,2048]{2,1,0:T(8,128)(2,1)S(1)} %pad_maximum_fusion.8.near_same), channel_id=1, source_target_pairs={{0,96},{32,64},{64,32},{96,0},{16,48},{48,16},{80,112},{112,80},{1... | collective-permute-start | bytes 1572872 | tf_op jit(solution)/shard_map/ppermute | solution.py:28
  137.1 14.6 %collective-permute-start.20 = (bf16[4,64,2048]{2,1,0:T(8,128)(2,1)S(1)}, bf16[4,64,2048]{2,1,0:T(8,128)(2,1)S(1)}, u32[]{:S(2)}, u32[]{:S(2)}) collective-permute-start(bf16[4,64,2048]{2,1,0:T(8,128)(2,1)S(1)} %pad_maximum_fusion), channel_id=1, source_target_pairs={{0,16},{16,0},{1,17},{17,1},{2,18},{18,2},{3,19},{19,3},{4,20},{20... | collective-permute-start | bytes 3145736 | tf_op jit(solution)/shard_map/ppermute | solution.py:45
  145.7 10.9 %collective-permute-start.28 = (bf16[4,64,2048]{2,1,0:T(8,128)(2,1)S(1)}, bf16[4,64,2048]{2,1,0:T(8,128)(2,1)S(1)}, u32[]{:S(2)}, u32[]{:S(2)}) collective-permute-start(bf16[4,64,2048]{2,1,0:T(8,128)(2,1)S(1)} %pad_maximum_fusion.1), channel_id=1, source_target_pairs={{0,16},{16,0},{1,17},{17,1},{2,18},{18,2},{3,19},{19,3},{4,20},{20... | collective-permute-start | bytes 3145736 | tf_op jit(solution)/shard_map/ppermute | solution.py:45
  151.6 11.1 %collective-permute-start.38 = (bf16[4,64,2048]{2,1,0:T(8,128)(2,1)S(1)}, bf16[4,64,2048]{2,1,0:T(8,128)(2,1)S(1)}, u32[]{:S(2)}, u32[]{:S(2)}) collective-permute-start(bf16[4,64,2048]{2,1,0:T(8,128)(2,1)S(1)} %pad_maximum_fusion.2), channel_id=1, source_target_pairs={{0,16},{16,0},{1,17},{17,1},{2,18},{18,2},{3,19},{19,3},{4,20},{20... | collective-permute-start | bytes 3145736 | tf_op jit(solution)/shard_map/ppermute | solution.py:45
  155.7 13.3 %collective-permute-start.21 = (bf16[2,4,32,1024]{3,2,1,0:T(8,128)(2,1)S(1)}, bf16[2,4,32,1024]{3,2,1,0:T(8,128)(2,1)}, u32[]{:S(2)}, u32[]{:S(2)}) collective-permute-start(bf16[2,4,32,1024]{3,2,1,0:T(8,128)(2,1)S(1)} %get-tuple-element.38), channel_id=1, source_target_pairs={{0,3},{1,2},{2,1},{3,0},{16,17},{17,16},{18,19},{19,18},{4,7},{5,6... | collective-permute-start | bytes 1572872 | tf_op jit(solution)/shard_map/ppermute | solution.py:29
  160.6 11.4 %collective-permute-start.29 = (bf16[2,4,32,1024]{3,2,1,0:T(8,128)(2,1)S(1)}, bf16[2,4,32,1024]{3,2,1,0:T(8,128)(2,1)}, u32[]{:S(2)}, u32[]{:S(2)}) collective-permute-start(bf16[2,4,32,1024]{3,2,1,0:T(8,128)(2,1)S(1)} %get-tuple-element.43), channel_id=1, source_target_pairs={{0,1},{1,0},{2,3},{3,2},{16,19},{17,18},{18,17},{19,16},{4,5},{5,4... | collective-permute-start | bytes 1572872 | tf_op jit(solution)/shard_map/ppermute | solution.py:29
  167.3 13.0 %collective-permute-start.39 = (bf16[2,4,32,1024]{3,2,1,0:T(8,128)(2,1)}, bf16[2,4,32,1024]{3,2,1,0:T(8,128)(2,1)}, u32[]{:S(2)}, u32[]{:S(2)}) collective-permute-start(bf16[2,4,32,1024]{3,2,1,0:T(8,128)(2,1)} %get-tuple-element.48), channel_id=1, source_target_pairs={{0,3},{1,2},{2,1},{3,0},{16,17},{17,16},{18,19},{19,18},{4,7},{5,6... | collective-permute-start | bytes 1572872 | tf_op jit(solution)/shard_map/ppermute | solution.py:29
  170.0 11.6 %collective-permute-start.22 = (bf16[4,32,1024]{2,1,0:T(8,128)(2,1)S(1)}, bf16[4,32,1024]{2,1,0:T(8,128)(2,1)S(1)}, u32[]{:S(2)}, u32[]{:S(2)}) collective-permute-start(bf16[4,32,1024]{2,1,0:T(8,128)(2,1)S(1)} %fusion.16), channel_id=1, source_target_pairs={{0,1},{1,0},{2,3},{3,2},{16,19},{17,18},{18,17},{19,16},{4,5},{5,4... | collective-permute-start | bytes 786440 | tf_op jit(solution)/shard_map/ppermute | solution.py:29
  173.0 10.0 %collective-permute-start.30 = (bf16[4,32,1024]{2,1,0:T(8,128)(2,1)S(1)}, bf16[4,32,1024]{2,1,0:T(8,128)(2,1)S(1)}, u32[]{:S(2)}, u32[]{:S(2)}) collective-permute-start(bf16[4,32,1024]{2,1,0:T(8,128)(2,1)S(1)} %fusion.18), channel_id=1, source_target_pairs={{0,3},{1,2},{2,1},{3,0},{16,17},{17,16},{18,19},{19,18},{4,7},{5,6... | collective-permute-start | bytes 786440 | tf_op jit(solution)/shard_map/ppermute | solution.py:29
  (30 other events, 246.3 us)
where the time goes:
time: 215 us; the launch traced here: 214 us
  waiting for transfers between devices  84.6 us (39%)
  starting transfers between devices  80.6 us (37%)
  Pallas kernels  28.5 us (13%)
  other arithmetic  11.5 us (5%)
  local copies, waits for them, and re-layouts  7.99 us (4%)
    ppermute x12, waiting for transfers between devices, move_ring(): lax.ppermute(array, ('y', 'core'), [(2 * i + c, 2 * j + d) for c, i, d, j...  34.1 us
    ppermute x8, starting transfers between devices, move_core(): return lax.ppermute(array, 'core', [(0, 1), (1, 0)])  32.8 us
    ppermute x12, waiting for transfers between devices, move_ring(): lax.ppermute(array, ('core', axis), [(4 * c + i, 4 * d + j) for c, i, d,...  18.2 us
    ppermute x8, waiting for transfers between devices, move_z(): return lax.ppermute(array, 'z', [(z, z ^ flip) for z in range(4)])  15.6 us
    ppermute x12, starting transfers between devices, move_ring(): lax.ppermute(array, ('core', axis), [(4 * c + i, 4 * d + j) for c, i, d,...  15.1 us
    pallas_call x3, Pallas kernels, hidden_product(): pl.pallas_call(functools.partial(hidden_kernel, chunk), grid=(width // ti...  14.5 us
    ppermute x12, starting transfers between devices, move_ring(): lax.ppermute(array, ('y', 'core'), [(2 * i + c, 2 * j + d) for c, i, d, j...  12.8 us
    pallas_call x3, Pallas kernels, feature_product(): pl.pallas_call(functools.partial(feature_kernel, chunk), grid=(width // t...  12.6 us
  transfers between devices with their start and end apart: 46, of which 29 were waited for; matrix products, arithmetic and copies ran while one was open for 6% of the time, Pallas kernels for 13%

commit v1 on v0

--- a/solution.py
+++ b/solution.py
@@ -84,7 +84,7 @@
 
 def slope_rows(u):
     rows, width = u.shape
-    tile = min(512, width)
+    tile = min(256, width)
     return pl.pallas_call(
         slope_kernel,
         grid=(width // tile,),
@@ -115,15 +115,19 @@
             picked = jnp.where(lax.rem(x, 2) == 0, rows[:8], rows[8:])
             mine[jnp.bitwise_xor(x, x_flip)] = picked
 
-    rows = lhs[...].reshape(512, -1)
-    product = nt_dot(rows, weight[...]).astype(BF)
-    keep[...] = product[:256].reshape(keep.shape)
-    send[...] = product[256:].reshape(send.shape)
+    part = 256
+
+    @pl.loop(0, weight.shape[0] // part)
+    def _(index):
+        columns = pl.ds(pl.multiple_of(index * part, part), part)
+        product = nt_dot(lhs[...].reshape(512, -1), weight[columns, :]).astype(BF)
+        keep[:, :, columns] = product[:256].reshape(4, 64, part)
+        send[:, :, columns] = product[256:].reshape(4, 64, part)
 
 
 def hidden_product(chunk, pos, near_pair, wide_pair, weight):
     width, depth = weight.shape
-    tile = min(256, width)
+    tile = min(512, width)
     out_block = pl.BlockSpec((4, 64, tile), lambda i: (0, 0, i))
     return pl.pallas_call(
         functools.partial(hidden_kernel, chunk),
@@ -158,8 +162,12 @@
         for j, flip in enumerate(ring_order(chunk, 1 - c)):
             lhs[2 * jnp.bitwise_xor(y, flip) + 1 - c] = other[j]
 
-    rows = lhs[...].reshape(512, -1)
-    result[...] = nt_dot(rows, weight[...]).reshape(result.shape)
+
+    @pl.loop(0, 2)
+    def _(index):
+        part = pl.ds(4 * index, 4)
+        result[part] = nt_dot(lhs[part].reshape(256, -1), weight[...]).reshape(4, *result.shape[1:])
+
     for x_rel, x_flip in enumerate(ring_order(chunk, c)):
         to = jnp.bitwise_xor(x, x_flip)
         out = keep if x_rel < 2 else send
@@ -208,22 +216,18 @@
     other = move_core(jnp.where(low, parts[1], parts[0]))
     both = jnp.stack([jnp.where(low, mine, other), jnp.where(low, other, mine)], axis=1)
 
-    def blocks(*flips_y):
-        return jnp.stack([lax.dynamic_index_in_dim(both, y ^ flip, 0, keepdims=False) for flip in flips_y])
-
-    moved = move_y(blocks(1, 2), 1)
-    kept = blocks(0, 3)
-    far = move_y(jnp.stack([kept[1], moved[1]]), 3)
-    return jnp.concatenate(sort_flips((kept[0], moved[0], far[1], far[0]), y)).transpose(1, 0, 2)
-
-
-def gather_z(rows, z):
-    a3 = move_mirror(rows)
+    def block(flip):
+        return lax.dynamic_index_in_dim(both, y ^ flip, 0, keepdims=False)
+
+    pieces = [block(0)] + [move_y(block(flip), flip) for flip in (1, 2, 3)]
+    return jnp.concatenate(sort_flips(pieces, y)).transpose(1, 0, 2)
+
+
+def gather_rows(chunk, a3, z):
     a1 = move_z(a3, 2)
     a2, a0 = move_z(jnp.stack([a3, a1]), 1)
-    pieces = sort_flips((a0, a1, a2, a3), z)
-    starts = range(0, rows.shape[0], ROWS)
-    return [jnp.concatenate([piece[at : at + ROWS] for piece in pieces]).transpose(1, 0, 2) for at in starts]
+    own = jnp.concatenate(sort_flips((a0, a1, a2, a3), z)).transpose(1, 0, 2)
+    return gather_ring(chunk, own, "x")
 
 
 def gather_ring(chunk, block, axis):
@@ -285,18 +289,19 @@
     spread = by_chunk(inverse_spread_per_position[0])
     gain = layernorm_multiplier[0]
 
-    rows, slope = lax.optimization_barrier((rows, slope))
-    parts = gather_z(rows[:ROWS], z) + gather_z(rows[ROWS:], z)
+    rows = [move_mirror(rows[: 2 * ROWS]), move_mirror(rows[2 * ROWS :])]
+    rows = [rows[0][:ROWS], rows[0][ROWS:], rows[1]]
     mine, totals = [], []
     for k in range(CHUNKS):
-        keep, send, own_rows = hidden_product(k, pos, *gather_ring(k, parts[k], "x"), contraction_factor[0])
+        gathered = gather_rows(k, rows[k], z)
+        keep, send, own_rows = hidden_product(k, pos, *gathered, contraction_factor[0])
         block = (reduce_hidden(k, keep, send) * slope[k]).astype(BF)
         near_pair, wide_pair = gather_ring(k, block, "y")
-        other = move_core(jnp.concatenate([near_pair, wide_pair]))
-        keep, send = feature_product(k, pos, (near_pair, wide_pair, other), expansion_factor[0])
+        pairs = (near_pair, wide_pair, move_core(jnp.concatenate([near_pair, wide_pair])))
+        keep, send = feature_product(k, pos, pairs, expansion_factor[0])
         mine.append(own_rows.reshape(32, -1))
         totals.append(reduce_x(k, keep, send))
-    scaled = [gain * total for total in reduce_z(totals[:2]) + reduce_z(totals[2:])]
+    scaled = [gain * total for total in reduce_z(totals[:1]) + reduce_z(totals[1:])]
     scaled = jnp.stack(scaled)
     upstream = jnp.stack(mine)
     sums = sum_over_dp(jnp.stack([jnp.sum(scaled, axis=2), jnp.sum(scaled * entry, axis=2)]))

time: 215 us -> 210 us (0.977)
  waiting for transfers between devices: 84.6 us -> 75.2 us
  starting transfers between devices: 80.6 us -> 86.8 us
  local copies, waits for them, and re-layouts: 7.99 us -> 4.85 us
    ppermute x12, waiting for transfers between devices: 34.1 us -> 25.7 us  [move_ring(): lax.ppermute(array, ('y', 'core'), [(2 * i + c, 2 * j + d) for c, i, d, j...]
    ppermute x12, waiting for transfers between devices: 18.2 us -> 12.1 us  [move_ring(): lax.ppermute(array, ('core', axis), [(4 * c + i, 4 * d + j) for c, i, d,...]
    ppermute x8 -> x10, waiting for transfers between devices: 15.6 us -> 20.4 us  [move_z(): return lax.ppermute(array, 'z', [(z, z ^ flip) for z in range(4)])]
    ppermute x8, starting transfers between devices: 32.8 us -> 37.2 us  [move_core(): return lax.ppermute(array, 'core', [(0, 1), (1, 0)])]
    ppermute x12, starting transfers between devices: 15.1 us -> 10.8 us  [move_ring(): lax.ppermute(array, ('core', axis), [(4 * c + i, 4 * d + j) for c, i, d,...]
    ppermute x12, starting transfers between devices: 12.8 us -> 16.5 us  [move_ring(): lax.ppermute(array, ('y', 'core'), [(2 * i + c, 2 * j + d) for c, i, d, j...]
    ppermute x8 -> x10, starting transfers between devices: 9.59 us -> 13.2 us  [move_z(): return lax.ppermute(array, 'z', [(z, z ^ flip) for z in range(4)])]
    unnamed x19 -> x16, local copies, waits for them, and re-layouts: 3.89 us -> 0.59 us
  transfers between devices with their start and end apart: 46 -> 49, of which waited for: 29 -> 27; matrix products, arithmetic and copies ran while one was open for 6% -> 6% of each run, Pallas kernels for 13% -> 14%
where the time goes in v1:
time: 210 us; the launch traced here: 209 us
  starting transfers between devices  86.8 us (41%)
  waiting for transfers between devices  75.2 us (36%)
  Pallas kernels  30.1 us (14%)
  other arithmetic  11 us (5%)
  local copies, waits for them, and re-layouts  4.85 us (2%)
    ppermute x8, starting transfers between devices, move_core(): return lax.ppermute(array, 'core', [(0, 1), (1, 0)])  37.2 us
    ppermute x12, waiting for transfers between devices, move_ring(): lax.ppermute(array, ('y', 'core'), [(2 * i + c, 2 * j + d) for c, i, d, j...  25.7 us
    ppermute x10, waiting for transfers between devices, move_z(): return lax.ppermute(array, 'z', [(z, z ^ flip) for z in range(4)])  20.4 us
    ppermute x12, starting transfers between devices, move_ring(): lax.ppermute(array, ('y', 'core'), [(2 * i + c, 2 * j + d) for c, i, d, j...  16.5 us
    pallas_call x3, Pallas kernels, feature_product(): pl.pallas_call(functools.partial(feature_kernel, chunk), grid=(width // t...  14.4 us
    pallas_call x3, Pallas kernels, hidden_product(): pl.pallas_call(functools.partial(hidden_kernel, chunk), grid=(width // ti...  14.2 us
    ppermute x10, starting transfers between devices, move_z(): return lax.ppermute(array, 'z', [(z, z ^ flip) for z in range(4)])  13.2 us
    ppermute x12, waiting for transfers between devices, move_ring(): lax.ppermute(array, ('core', axis), [(4 * c + i, 4 * d + j) for c, i, d,...  12.1 us
  transfers between devices with their start and end apart: 49, of which 27 were waited for; matrix products, arithmetic and copies ran while one was open for 6% of the time, Pallas kernels for 14%

profile of v1, /device:TPU:1, one launch (start us, length us, event | category | flops | bytes accessed | tf_op | source)
XLA Modules:
  0.0 208.6 jit_solution(3535282401341789336)
XLA Ops:
  1.0 3.3 %collective-permute-start = (bf16[4,12,1024]{2,1,0:T(8,128)(2,1)S(1)}, bf16[4,12,1024]{2,1,0:T(8,128)(2,1)S(1)}, u32[]{:S(2)}, u32[]{:S(2)}) collective-permute-start(bf16[4,12,1024]{2,1,0:T(8,128)(2,1)S(1)} %broadcast_select_fusion), channel_id=1, source_target_pairs={{0,16},{16,0},{1,17},{17,1},{2,18},{18,2},{3,19},{19,3},{4,20},{20... | collective-permute-start | bytes 294920 | tf_op jit(solution)/shard_map/ppermute | solution.py:45
  12.3 4.5 %collective-permute-start.4 = (bf16[8,8,1024]{2,0,1:T(8,128)(2,1)S(1)}, bf16[8,8,1024]{2,0,1:T(8,128)(2,1)S(1)}, u32[]{:S(2)}, u32[]{:S(2)}) collective-permute-start(bf16[8,8,1024]{2,0,1:T(8,128)(2,1)S(1)} %slice.265), channel_id=1, source_target_pairs={{0,140},{4,136},{8,132},{12,128},{128,12},{132,8},{136,4},{140,0},... | collective-permute-start | bytes 393224 | tf_op jit(solution)/shard_map/ppermute | solution.py:41
  16.9 8.2 %collective-permute-done.13 = bf16[4,8,1024]{2,0,1:T(4,128)(2,1)S(1)} collective-permute-done((bf16[4,8,1024]{2,0,1:T(4,128)(2,1)S(1)}, bf16[4,8,1024]{2,0,1:T(4,128)(2,1)S(1)}, u32[]{:S(2)}, u32[]{:S(2)}) %collective-permute-start.13) | collective-permute-done | bytes 65568 | tf_op jit(solution)/shard_map/ppermute | solution.py:41
  31.3 2.8 %collective-permute-done.15 = bf16[2,4,8,1024]{3,1,2,0:T(4,128)(2,1)S(1)} collective-permute-done((bf16[2,4,8,1024]{3,1,2,0:T(4,128)(2,1)S(1)}, bf16[2,4,8,1024]{3,1,2,0:T(4,128)(2,1)S(1)}, u32[]{:S(2)}, u32[]{:S(2)}) %collective-permute-start.15) | collective-permute-done | bytes 131104 | tf_op jit(solution)/shard_map/ppermute | solution.py:37
  38.2 3.7 %collective-permute-done.5 = bf16[4,8,1024]{2,0,1:T(4,128)(2,1)S(1)} collective-permute-done((bf16[4,8,1024]{2,0,1:T(4,128)(2,1)S(1)}, bf16[4,8,1024]{2,0,1:T(4,128)(2,1)S(1)}, u32[]{:S(2)}, u32[]{:S(2)}) %collective-permute-start.5) | collective-permute-done | bytes 65568 | tf_op jit(solution)/shard_map/ppermute | solution.py:37
  42.4 4.1 %collective-permute-done.6 = bf16[2,4,8,1024]{3,1,2,0:T(4,128)(2,1)S(1)} collective-permute-done((bf16[2,4,8,1024]{3,1,2,0:T(4,128)(2,1)S(1)}, bf16[2,4,8,1024]{3,1,2,0:T(4,128)(2,1)S(1)}, u32[]{:S(2)}, u32[]{:S(2)}) %collective-permute-start.6) | collective-permute-done | bytes 131104 | tf_op jit(solution)/shard_map/ppermute | solution.py:37
  52.2 4.7 %shard_map.75 = (bf16[4,64,2048]{2,1,0:T(8,128)(2,1)S(1)}, bf16[4,64,2048]{2,1,0:T(8,128)(2,1)S(1)}, f32[4,8,1024]{2,1,0:T(8,128)S(1)}) custom-call(s32[4]{0:T(128)S(1)} %pad_add_fusion.pos, bf16[2,8,16,1024]{3,2,1,0:T(8,128)(2,1)S(1)} %pad_maximum_fusion.6.near_pair, bf16[2,8,16,1024]{3,2,1,0:T(8,128)(2,1)S(1)} %collective-permute-done.17.wide_pair, ...), custom_call_target="tpu_custom_call" | custom-call | flops 2147483648 | bytes 7340032 | tf_op jit(solution)/shard_map/pallas_call | solution.py:132
  56.9 11.2 %collective-permute-start.36 = (bf16[4,64,2048]{2,1,0:T(8,128)(2,1)S(1)}, bf16[4,64,2048]{2,1,0:T(8,128)(2,1)S(1)}, u32[]{:S(2)}, u32[]{:S(2)}) collective-permute-start(bf16[4,64,2048]{2,1,0:T(8,128)(2,1)S(1)} %get-tuple-element.37), channel_id=1, source_target_pairs={{0,16},{16,0},{1,17},{17,1},{2,18},{18,2},{3,19},{19,3},{4,20},{20... | collective-permute-start | bytes 3145736 | tf_op jit(solution)/shard_map/ppermute | solution.py:45
  68.4 4.7 %shard_map.74 = (bf16[4,64,2048]{2,1,0:T(8,128)(2,1)S(1)}, bf16[4,64,2048]{2,1,0:T(8,128)(2,1)S(1)}, f32[4,8,1024]{2,1,0:T(8,128)S(1)}) custom-call(s32[4]{0:T(128)S(1)} %pad_add_fusion.pos, bf16[2,8,16,1024]{3,2,1,0:T(8,128)(2,1)S(1)} %pad_maximum_fusion.5.near_pair, bf16[2,8,16,1024]{3,2,1,0:T(8,128)(2,1)S(1)} %collective-permute-done.12.wide_pair, ...), custom_call_target="tpu_custom_call" | custom-call | flops 2147483648 | bytes 7340032 | tf_op jit(solution)/shard_map/pallas_call | solution.py:132
  76.6 4.7 %shard_map.73 = (bf16[4,64,2048]{2,1,0:T(8,128)(2,1)S(1)}, bf16[4,64,2048]{2,1,0:T(8,128)(2,1)S(1)}, f32[4,8,1024]{2,1,0:T(8,128)S(1)}) custom-call(s32[4]{0:T(128)S(1)} %pad_add_fusion.pos, bf16[2,8,16,1024]{3,2,1,0:T(8,128)(2,1)S(1)} %pad_maximum_fusion.4.near_pair, bf16[2,8,16,1024]{3,2,1,0:T(8,128)(2,1)S(1)} %collective-permute-done.8.wide_pair, ...), custom_call_target="tpu_custom_call" | custom-call | flops 2147483648 | bytes 7340032 | tf_op jit(solution)/shard_map/pallas_call | solution.py:132
  89.5 7.8 %collective-permute-done.37 = bf16[2,64,2048]{2,1,0:T(8,128)(2,1)S(1)} collective-permute-done((bf16[2,64,2048]{2,1,0:T(8,128)(2,1)S(1)}, bf16[2,64,2048]{2,1,0:T(8,128)(2,1)S(1)}, u32[]{:S(2)}, u32[]{:S(2)}) %collective-permute-start.37) | collective-permute-done | bytes 524320 | tf_op jit(solution)/shard_map/ppermute | solution.py:28
  97.4 4.2 %collective-permute-start.38 = (bf16[64,2048]{1,0:T(8,128)(2,1)S(1)}, bf16[64,2048]{1,0:T(8,128)(2,1)S(1)}, u32[]{:S(2)}, u32[]{:S(2)}) collective-permute-start(bf16[64,2048]{1,0:T(8,128)(2,1)S(1)} %fusion.17), channel_id=1, source_target_pairs={{0,32},{32,0},{64,96},{96,64},{16,112},{48,80},{80,48},{112,16},{1... | collective-permute-start | bytes 786440 | tf_op jit(solution)/shard_map/ppermute | solution.py:28
  102.9 5.6 %collective-permute-done.38 = bf16[64,2048]{1,0:T(8,128)(2,1)S(1)} collective-permute-done((bf16[64,2048]{1,0:T(8,128)(2,1)S(1)}, bf16[64,2048]{1,0:T(8,128)(2,1)S(1)}, u32[]{:S(2)}, u32[]{:S(2)}) %collective-permute-start.38) | collective-permute-done | bytes 262176 | tf_op jit(solution)/shard_map/ppermute | solution.py:28
  108.7 2.8 %collective-permute-start.39 = (bf16[64,2048]{1,0:T(8,128)(2,1)S(1)}, bf16[64,2048]{1,0:T(8,128)(2,1)S(1)}, u32[]{:S(2)}, u32[]{:S(2)}) collective-permute-start(bf16[64,2048]{1,0:T(8,128)(2,1)S(1)} %fusion.2), channel_id=1, source_target_pairs={{0,32},{32,0},{64,96},{96,64},{16,112},{48,80},{80,48},{112,16},{1... | collective-permute-start | bytes 786440 | tf_op jit(solution)/shard_map/ppermute | solution.py:28
  115.9 3.3 %collective-permute-done.20 = bf16[64,2048]{1,0:T(8,128)(2,1)S(1)} collective-permute-done((bf16[64,2048]{1,0:T(8,128)(2,1)S(1)}, bf16[64,2048]{1,0:T(8,128)(2,1)S(1)}, u32[]{:S(2)}, u32[]{:S(2)}) %collective-permute-start.20) | collective-permute-done | bytes 262176 | tf_op jit(solution)/shard_map/ppermute | solution.py:28
  123.0 5.3 %collective-permute-done.21 = bf16[64,2048]{1,0:T(8,128)(2,1)S(1)} collective-permute-done((bf16[64,2048]{1,0:T(8,128)(2,1)S(1)}, bf16[64,2048]{1,0:T(8,128)(2,1)S(1)}, u32[]{:S(2)}, u32[]{:S(2)}) %collective-permute-start.21) | collective-permute-done | bytes 262176 | tf_op jit(solution)/shard_map/ppermute | solution.py:28
  128.6 8.4 %collective-permute-start.41 = (bf16[4,64,2048]{2,1,0:T(8,128)(2,1)S(1)}, bf16[4,64,2048]{2,1,0:T(8,128)(2,1)S(1)}, u32[]{:S(2)}, u32[]{:S(2)}) collective-permute-start(bf16[4,64,2048]{2,1,0:T(8,128)(2,1)S(1)} %pad_maximum_fusion.3), channel_id=1, source_target_pairs={{0,16},{16,0},{1,17},{17,1},{2,18},{18,2},{3,19},{19,3},{4,20},{20... | collective-permute-start | bytes 3145736 | tf_op jit(solution)/shard_map/ppermute | solution.py:45
  137.2 5.0 %collective-permute-start.33 = (bf16[4,64,2048]{2,1,0:T(8,128)(2,1)S(1)}, bf16[4,64,2048]{2,1,0:T(8,128)(2,1)S(1)}, u32[]{:S(2)}, u32[]{:S(2)}) collective-permute-start(bf16[4,64,2048]{2,1,0:T(8,128)(2,1)S(1)} %pad_maximum_fusion.2), channel_id=1, source_target_pairs={{0,16},{16,0},{1,17},{17,1},{2,18},{18,2},{3,19},{19,3},{4,20},{20... | collective-permute-start | bytes 3145736 | tf_op jit(solution)/shard_map/ppermute | solution.py:45
  144.2 4.8 %shard_map.79 = (bf16[2,4,32,1024]{3,2,1,0:T(8,128)(2,1)S(1)}, bf16[2,4,32,1024]{3,2,1,0:T(8,128)(2,1)S(1)}) custom-call(s32[4]{0:T(128)S(1)} %pad_add_fusion.pos, bf16[2,64,2048]{2,1,0:T(8,128)(2,1)S(1)} %pad_maximum_fusion.9.near_same, bf16[2,64,2048]{2,1,0:T(8,128)(2,1)S(1)} %collective-permute-done.40.wide_same, ...), custom_call_target="tpu_custom_call" | custom-call | flops 2147483648 | bytes 7340032 | tf_op jit(solution)/shard_map/pallas_call | solution.py:183
  149.1 4.8 %shard_map.78 = (bf16[2,4,32,1024]{3,2,1,0:T(8,128)(2,1)S(1)}, bf16[2,4,32,1024]{3,2,1,0:T(8,128)(2,1)S(1)}) custom-call(s32[4]{0:T(128)S(1)} %pad_add_fusion.pos, bf16[2,64,2048]{2,1,0:T(8,128)(2,1)S(1)} %pad_maximum_fusion.8.near_same, bf16[2,64,2048]{2,1,0:T(8,128)(2,1)S(1)} %collective-permute-done.32.wide_same, ...), custom_call_target="tpu_custom_call" | custom-call | flops 2147483648 | bytes 7340032 | tf_op jit(solution)/shard_map/pallas_call | solution.py:183
  153.9 3.0 %collective-permute-start.34 = (bf16[2,4,32,1024]{3,2,1,0:T(8,128)(2,1)S(1)}, bf16[2,4,32,1024]{3,2,1,0:T(8,128)(2,1)}, u32[]{:S(2)}, u32[]{:S(2)}) collective-permute-start(bf16[2,4,32,1024]{3,2,1,0:T(8,128)(2,1)S(1)} %get-tuple-element.35), channel_id=1, source_target_pairs={{0,1},{1,0},{2,3},{3,2},{16,19},{17,18},{18,17},{19,16},{4,5},{5,4... | collective-permute-start | bytes 1572872 | tf_op jit(solution)/shard_map/ppermute | solution.py:29
  156.9 4.8 %shard_map.77 = (bf16[2,4,32,1024]{3,2,1,0:T(8,128)(2,1)S(1)}, bf16[2,4,32,1024]{3,2,1,0:T(8,128)(2,1)S(1)}) custom-call(s32[4]{0:T(128)S(1)} %pad_add_fusion.pos, bf16[2,64,2048]{2,1,0:T(8,128)(2,1)S(1)} %pad_maximum_fusion.7.near_same, bf16[2,64,2048]{2,1,0:T(8,128)(2,1)S(1)} %collective-permute-done.22.wide_same, ...), custom_call_target="tpu_custom_call" | custom-call | flops 2147483648 | bytes 7340032 | tf_op jit(solution)/shard_map/pallas_call | solution.py:183
  167.3 7.2 %collective-permute-done.24 = bf16[2,4,32,1024]{3,2,1,0:T(8,128)(2,1)} collective-permute-done((bf16[2,4,32,1024]{3,2,1,0:T(8,128)(2,1)S(1)}, bf16[2,4,32,1024]{3,2,1,0:T(8,128)(2,1)}, u32[]{:S(2)}, u32[]{:S(2)}) %collective-permute-start.24) | collective-permute-done | bytes 524320 | tf_op jit(solution)/shard_map/ppermute | solution.py:29
  191.7 5.4 %collective-permute-done.27 = bf16[1,32,1024]{2,1,0:T(8,128)(2,1)S(1)} collective-permute-done((bf16[1,32,1024]{2,1,0:T(8,128)(2,1)S(1)}, bf16[1,32,1024]{2,1,0:T(8,128)(2,1)S(1)}, u32[]{:S(2)}, u32[]{:S(2)}) %collective-permute-start.27) | collective-permute-done | bytes 65568 | tf_op jit(solution)/shard_map/ppermute | solution.py:37
  (172 shorter events, 83.6 us)
Async XLA Ops:
  12.3 12.9 %collective-permute-start.4 = (bf16[8,8,1024]{2,0,1:T(8,128)(2,1)S(1)}, bf16[8,8,1024]{2,0,1:T(8,128)(2,1)S(1)}, u32[]{:S(2)}, u32[]{:S(2)}) collective-permute-start(bf16[8,8,1024]{2,0,1:T(8,128)(2,1)S(1)} %slice.265), channel_id=1, source_target_pairs={{0,140},{4,136},{8,132},{12,128},{128,12},{132,8},{136,4},{140,0},... | collective-permute-start | bytes 393224 | tf_op jit(solution)/shard_map/ppermute | solution.py:41
  42.2 10.0 %collective-permute-start.17 = (bf16[2,8,16,1024]{3,2,1,0:T(8,128)(2,1)S(1)}, bf16[2,8,16,1024]{3,2,1,0:T(8,128)(2,1)S(1)}, u32[]{:S(2)}, u32[]{:S(2)}) collective-permute-start(bf16[2,8,16,1024]{3,2,1,0:T(8,128)(2,1)S(1)} %pad_maximum_fusion.6.near_pair), channel_id=1, source_target_pairs={{0,3},{1,2},{2,1},{3,0},{16,17},{17,16},{18,19},{19,18},{4,7},{5,6... | collective-permute-start | bytes 1572872 | tf_op jit(solution)/shard_map/ppermute | solution.py:29
  46.7 21.7 %collective-permute-start.12 = (bf16[2,8,16,1024]{3,2,1,0:T(8,128)(2,1)S(1)}, bf16[2,8,16,1024]{3,2,1,0:T(8,128)(2,1)S(1)}, u32[]{:S(2)}, u32[]{:S(2)}) collective-permute-start(bf16[2,8,16,1024]{3,2,1,0:T(8,128)(2,1)S(1)} %pad_maximum_fusion.5.near_pair), channel_id=1, source_target_pairs={{0,1},{1,0},{2,3},{3,2},{16,19},{17,18},{18,17},{19,16},{4,5},{5,4... | collective-permute-start | bytes 1572872 | tf_op jit(solution)/shard_map/ppermute | solution.py:29
  47.4 20.7 %collective-permute-start.7 = (bf16[8,16,1024]{2,1,0:T(8,128)(2,1)S(1)}, bf16[8,16,1024]{2,1,0:T(8,128)(2,1)S(1)}, u32[]{:S(2)}, u32[]{:S(2)}) collective-permute-start(bf16[8,16,1024]{2,1,0:T(8,128)(2,1)S(1)} %get-tuple-element.64), channel_id=1, source_target_pairs={{0,1},{1,0},{2,3},{3,2},{16,19},{17,18},{18,17},{19,16},{4,5},{5,4... | collective-permute-start | bytes 786440 | tf_op jit(solution)/shard_map/ppermute | solution.py:29
  56.9 28.0 %collective-permute-start.36 = (bf16[4,64,2048]{2,1,0:T(8,128)(2,1)S(1)}, bf16[4,64,2048]{2,1,0:T(8,128)(2,1)S(1)}, u32[]{:S(2)}, u32[]{:S(2)}) collective-permute-start(bf16[4,64,2048]{2,1,0:T(8,128)(2,1)S(1)} %get-tuple-element.37), channel_id=1, source_target_pairs={{0,16},{16,0},{1,17},{17,1},{2,18},{18,2},{3,19},{19,3},{4,20},{20... | collective-permute-start | bytes 3145736 | tf_op jit(solution)/shard_map/ppermute | solution.py:45
  73.1 14.2 %collective-permute-start.28 = (bf16[4,64,2048]{2,1,0:T(8,128)(2,1)S(1)}, bf16[4,64,2048]{2,1,0:T(8,128)(2,1)S(1)}, u32[]{:S(2)}, u32[]{:S(2)}) collective-permute-start(bf16[4,64,2048]{2,1,0:T(8,128)(2,1)S(1)} %get-tuple-element.32), channel_id=1, source_target_pairs={{0,16},{16,0},{1,17},{17,1},{2,18},{18,2},{3,19},{19,3},{4,20},{20... | collective-permute-start | bytes 3145736 | tf_op jit(solution)/shard_map/ppermute | solution.py:45
  85.1 12.2 %collective-permute-start.37 = (bf16[2,64,2048]{2,1,0:T(8,128)(2,1)S(1)}, bf16[2,64,2048]{2,1,0:T(8,128)(2,1)S(1)}, u32[]{:S(2)}, u32[]{:S(2)}) collective-permute-start(bf16[2,64,2048]{2,1,0:T(8,128)(2,1)S(1)} %add_convert_fusion), channel_id=1, source_target_pairs={{0,96},{32,64},{64,32},{96,0},{16,48},{48,16},{80,112},{112,80},{1... | collective-permute-start | bytes 1572872 | tf_op jit(solution)/shard_map/ppermute | solution.py:28
  87.4 15.3 %collective-permute-start.29 = (bf16[2,64,2048]{2,1,0:T(8,128)(2,1)S(1)}, bf16[2,64,2048]{2,1,0:T(8,128)(2,1)S(1)}, u32[]{:S(2)}, u32[]{:S(2)}) collective-permute-start(bf16[2,64,2048]{2,1,0:T(8,128)(2,1)S(1)} %add_convert_fusion.1), channel_id=1, source_target_pairs={{0,32},{32,0},{64,96},{96,64},{16,112},{48,80},{80,48},{112,16},{1... | collective-permute-start | bytes 1572872 | tf_op jit(solution)/shard_map/ppermute | solution.py:28
  88.6 22.9 %collective-permute-start.19 = (bf16[2,64,2048]{2,1,0:T(8,128)(2,1)S(1)}, bf16[2,64,2048]{2,1,0:T(8,128)(2,1)S(1)}, u32[]{:S(2)}, u32[]{:S(2)}) collective-permute-start(bf16[2,64,2048]{2,1,0:T(8,128)(2,1)S(1)} %add_convert_fusion.2), channel_id=1, source_target_pairs={{0,96},{32,64},{64,32},{96,0},{16,48},{48,16},{80,112},{112,80},{1... | collective-permute-start | bytes 1572872 | tf_op jit(solution)/shard_map/ppermute | solution.py:28
  97.4 11.2 %collective-permute-start.38 = (bf16[64,2048]{1,0:T(8,128)(2,1)S(1)}, bf16[64,2048]{1,0:T(8,128)(2,1)S(1)}, u32[]{:S(2)}, u32[]{:S(2)}) collective-permute-start(bf16[64,2048]{1,0:T(8,128)(2,1)S(1)} %fusion.17), channel_id=1, source_target_pairs={{0,32},{32,0},{64,96},{96,64},{16,112},{48,80},{80,48},{112,16},{1... | collective-permute-start | bytes 786440 | tf_op jit(solution)/shard_map/ppermute | solution.py:28
  102.8 8.9 %collective-permute-start.30 = (bf16[64,2048]{1,0:T(8,128)(2,1)S(1)}, bf16[64,2048]{1,0:T(8,128)(2,1)S(1)}, u32[]{:S(2)}, u32[]{:S(2)}) collective-permute-start(bf16[64,2048]{1,0:T(8,128)(2,1)S(1)} %fusion.15), channel_id=1, source_target_pairs={{0,96},{32,64},{64,32},{96,0},{16,48},{48,16},{80,112},{112,80},{1... | collective-permute-start | bytes 786440 | tf_op jit(solution)/shard_map/ppermute | solution.py:28
  111.9 9.8 %collective-permute-start.31 = (bf16[64,2048]{1,0:T(8,128)(2,1)S(1)}, bf16[64,2048]{1,0:T(8,128)(2,1)S(1)}, u32[]{:S(2)}, u32[]{:S(2)}) collective-permute-start(bf16[64,2048]{1,0:T(8,128)(2,1)S(1)} %fusion.5), channel_id=1, source_target_pairs={{0,96},{32,64},{64,32},{96,0},{16,48},{48,16},{80,112},{112,80},{1... | collective-permute-start | bytes 786440 | tf_op jit(solution)/shard_map/ppermute | solution.py:28
  115.3 13.1 %collective-permute-start.40 = (bf16[2,64,2048]{2,1,0:T(8,128)(2,1)S(1)}, bf16[2,64,2048]{2,1,0:T(8,128)(2,1)S(1)}, u32[]{:S(2)}, u32[]{:S(2)}) collective-permute-start(bf16[2,64,2048]{2,1,0:T(8,128)(2,1)S(1)} %pad_maximum_fusion.9.near_same), channel_id=1, source_target_pairs={{0,96},{32,64},{64,32},{96,0},{16,48},{48,16},{80,112},{112,80},{1... | collective-permute-start | bytes 1572872 | tf_op jit(solution)/shard_map/ppermute | solution.py:28
  119.3 9.0 %collective-permute-start.21 = (bf16[64,2048]{1,0:T(8,128)(2,1)S(1)}, bf16[64,2048]{1,0:T(8,128)(2,1)S(1)}, u32[]{:S(2)}, u32[]{:S(2)}) collective-permute-start(bf16[64,2048]{1,0:T(8,128)(2,1)S(1)} %fusion.7), channel_id=1, source_target_pairs={{0,32},{32,0},{64,96},{96,64},{16,112},{48,80},{80,48},{112,16},{1... | collective-permute-start | bytes 786440 | tf_op jit(solution)/shard_map/ppermute | solution.py:28
  121.8 15.3 %collective-permute-start.32 = (bf16[2,64,2048]{2,1,0:T(8,128)(2,1)S(1)}, bf16[2,64,2048]{2,1,0:T(8,128)(2,1)S(1)}, u32[]{:S(2)}, u32[]{:S(2)}) collective-permute-start(bf16[2,64,2048]{2,1,0:T(8,128)(2,1)S(1)} %pad_maximum_fusion.8.near_same), channel_id=1, source_target_pairs={{0,32},{32,0},{64,96},{96,64},{16,112},{48,80},{80,48},{112,16},{1... | collective-permute-start | bytes 1572872 | tf_op jit(solution)/shard_map/ppermute | solution.py:28
  128.4 13.8 %collective-permute-start.22 = (bf16[2,64,2048]{2,1,0:T(8,128)(2,1)S(1)}, bf16[2,64,2048]{2,1,0:T(8,128)(2,1)S(1)}, u32[]{:S(2)}, u32[]{:S(2)}) collective-permute-start(bf16[2,64,2048]{2,1,0:T(8,128)(2,1)S(1)} %pad_maximum_fusion.7.near_same), channel_id=1, source_target_pairs={{0,96},{32,64},{64,32},{96,0},{16,48},{48,16},{80,112},{112,80},{1... | collective-permute-start | bytes 1572872 | tf_op jit(solution)/shard_map/ppermute | solution.py:28
  128.6 15.6 %collective-permute-start.41 = (bf16[4,64,2048]{2,1,0:T(8,128)(2,1)S(1)}, bf16[4,64,2048]{2,1,0:T(8,128)(2,1)S(1)}, u32[]{:S(2)}, u32[]{:S(2)}) collective-permute-start(bf16[4,64,2048]{2,1,0:T(8,128)(2,1)S(1)} %pad_maximum_fusion.3), channel_id=1, source_target_pairs={{0,16},{16,0},{1,17},{17,1},{2,18},{18,2},{3,19},{19,3},{4,20},{20... | collective-permute-start | bytes 3145736 | tf_op jit(solution)/shard_map/ppermute | solution.py:45
  137.2 11.9 %collective-permute-start.33 = (bf16[4,64,2048]{2,1,0:T(8,128)(2,1)S(1)}, bf16[4,64,2048]{2,1,0:T(8,128)(2,1)S(1)}, u32[]{:S(2)}, u32[]{:S(2)}) collective-permute-start(bf16[4,64,2048]{2,1,0:T(8,128)(2,1)S(1)} %pad_maximum_fusion.2), channel_id=1, source_target_pairs={{0,16},{16,0},{1,17},{17,1},{2,18},{18,2},{3,19},{19,3},{4,20},{20... | collective-permute-start | bytes 3145736 | tf_op jit(solution)/shard_map/ppermute | solution.py:45
  142.3 14.6 %collective-permute-start.23 = (bf16[4,64,2048]{2,1,0:T(8,128)(2,1)S(1)}, bf16[4,64,2048]{2,1,0:T(8,128)(2,1)S(1)}, u32[]{:S(2)}, u32[]{:S(2)}) collective-permute-start(bf16[4,64,2048]{2,1,0:T(8,128)(2,1)S(1)} %pad_maximum_fusion.1), channel_id=1, source_target_pairs={{0,16},{16,0},{1,17},{17,1},{2,18},{18,2},{3,19},{19,3},{4,20},{20... | collective-permute-start | bytes 3145736 | tf_op jit(solution)/shard_map/ppermute | solution.py:45
  149.0 15.5 %collective-permute-start.42 = (bf16[2,4,32,1024]{3,2,1,0:T(8,128)(2,1)S(1)}, bf16[2,4,32,1024]{3,2,1,0:T(8,128)(2,1)}, u32[]{:S(2)}, u32[]{:S(2)}) collective-permute-start(bf16[2,4,32,1024]{3,2,1,0:T(8,128)(2,1)S(1)} %get-tuple-element.40), channel_id=1, source_target_pairs={{0,3},{1,2},{2,1},{3,0},{16,17},{17,16},{18,19},{19,18},{4,7},{5,6... | collective-permute-start | bytes 1572872 | tf_op jit(solution)/shard_map/ppermute | solution.py:29
  153.9 12.3 %collective-permute-start.34 = (bf16[2,4,32,1024]{3,2,1,0:T(8,128)(2,1)S(1)}, bf16[2,4,32,1024]{3,2,1,0:T(8,128)(2,1)}, u32[]{:S(2)}, u32[]{:S(2)}) collective-permute-start(bf16[2,4,32,1024]{3,2,1,0:T(8,128)(2,1)S(1)} %get-tuple-element.35), channel_id=1, source_target_pairs={{0,1},{1,0},{2,3},{3,2},{16,19},{17,18},{18,17},{19,16},{4,5},{5,4... | collective-permute-start | bytes 1572872 | tf_op jit(solution)/shard_map/ppermute | solution.py:29
  161.7 12.8 %collective-permute-start.24 = (bf16[2,4,32,1024]{3,2,1,0:T(8,128)(2,1)S(1)}, bf16[2,4,32,1024]{3,2,1,0:T(8,128)(2,1)}, u32[]{:S(2)}, u32[]{:S(2)}) collective-permute-start(bf16[2,4,32,1024]{3,2,1,0:T(8,128)(2,1)S(1)} %get-tuple-element.30), channel_id=1, source_target_pairs={{0,3},{1,2},{2,1},{3,0},{16,17},{17,16},{18,19},{19,18},{4,7},{5,6... | collective-permute-start | bytes 1572872 | tf_op jit(solution)/shard_map/ppermute | solution.py:29
  165.5 10.2 %collective-permute-start.43 = (bf16[4,32,1024]{2,1,0:T(8,128)(2,1)S(1)}, bf16[4,32,1024]{2,1,0:T(8,128)(2,1)S(1)}, u32[]{:S(2)}, u32[]{:S(2)}) collective-permute-start(bf16[4,32,1024]{2,1,0:T(8,128)(2,1)S(1)} %fusion.18), channel_id=1, source_target_pairs={{0,1},{1,0},{2,3},{3,2},{16,19},{17,18},{18,17},{19,16},{4,5},{5,4... | collective-permute-start | bytes 786440 | tf_op jit(solution)/shard_map/ppermute | solution.py:29
  167.2 10.0 %collective-permute-start.35 = (bf16[4,32,1024]{2,1,0:T(8,128)(2,1)S(1)}, bf16[4,32,1024]{2,1,0:T(8,128)(2,1)S(1)}, u32[]{:S(2)}, u32[]{:S(2)}) collective-permute-start(bf16[4,32,1024]{2,1,0:T(8,128)(2,1)S(1)} %fusion.16), channel_id=1, source_target_pairs={{0,3},{1,2},{2,1},{3,0},{16,17},{17,16},{18,19},{19,18},{4,7},{5,6... | collective-permute-start | bytes 786440 | tf_op jit(solution)/shard_map/ppermute | solution.py:29
  (31 other events, 268.6 us)

commit v2 on v1

--- a/solution.py
+++ b/solution.py
@@ -52,6 +52,11 @@
 def ring_order(chunk, core):
     first, second = flips(chunk)
     return 0, first(core), second(core), 2
+
+
+def ring_flip(chunk, core, index):
+    _, first, second, _ = ring_order(chunk, core)
+    return jnp.where(index == 0, 0, jnp.where(index == 1, first, jnp.where(index == 2, second, 2)))
 
 
 def gelu_slope(u):
@@ -101,13 +106,14 @@
 
     @pl.when(pl.program_id(0) == 0)
     def _():
-        for c_rel in range(2):
-            core = jnp.bitwise_xor(c, c_rel)
-            for j, flip in enumerate(ring_order(chunk, core)):
-                source = 2 * jnp.bitwise_xor(y, flip) + core
-                for x_rel, x_flip in enumerate(ring_order(chunk, c)):
-                    ref = near_pair if x_rel < 2 else wide_pair
-                    lhs[4 * c_rel + j, jnp.bitwise_xor(x, x_flip)] = ref[x_rel % 2, source]
+        @pl.loop(0, 8)
+        def _(to):
+            core = jnp.bitwise_xor(c, to // 4)
+            source = 2 * jnp.bitwise_xor(y, ring_flip(chunk, core, lax.rem(to, 4))) + core
+            for x_rel, x_flip in enumerate(ring_order(chunk, c)):
+                ref = near_pair if x_rel < 2 else wide_pair
+                lhs[to, jnp.bitwise_xor(x, x_flip)] = ref[x_rel % 2, source]
+
         source = 2 * z + x // 2
         for x_rel, x_flip in enumerate(ring_order(chunk, c)):
             ref = near_pair if x_rel < 2 else wide_pair
@@ -145,22 +151,22 @@
             jax.ShapeDtypeStruct((4, 8, depth), F32),
         ],
         scratch_shapes=[pltpu.VMEM((8, 4, 16, depth), BF)],
-        compiler_params=pltpu.CompilerParams(vmem_limit_bytes=16 * 2**20),
+        compiler_params=pltpu.CompilerParams(vmem_limit_bytes=13 * 2**20),
         cost_estimate=pl.CostEstimate(
             flops=2 * 512 * width * depth, bytes_accessed=2 * (width * depth + 512 * (width + depth)), transcendentals=0
         ),
     )(pos, near_pair, wide_pair, weight)
 
 
-def feature_kernel(chunk, pos, near_same, wide_same, other, weight, keep, send, lhs, result):
+def feature_kernel(chunk, pos, same, other, weight, keep, send, lhs, result):
     x, y, z, c = pos[0], pos[1], pos[2], pos[3]
 
     @pl.when(pl.program_id(0) == 0)
     def _():
-        for j, flip in enumerate(ring_order(chunk, c)):
-            lhs[2 * jnp.bitwise_xor(y, flip) + c] = (near_same if j < 2 else wide_same)[j % 2]
-        for j, flip in enumerate(ring_order(chunk, 1 - c)):
-            lhs[2 * jnp.bitwise_xor(y, flip) + 1 - c] = other[j]
+        @pl.loop(0, 4)
+        def _(j):
+            lhs[2 * jnp.bitwise_xor(y, ring_flip(chunk, c, j)) + c] = same[j]
+            lhs[2 * jnp.bitwise_xor(y, ring_flip(chunk, 1 - c, j)) + 1 - c] = other[j]
 
 
     @pl.loop(0, 2)
@@ -187,7 +193,7 @@
         out_specs=[out_block, out_block],
         out_shape=[jax.ShapeDtypeStruct((2, 4, 32, width), BF)] * 2,
         scratch_shapes=[pltpu.VMEM((8, 64, depth), BF), pltpu.VMEM((8, 4, 2, 8, tile), F32)],
-        compiler_params=pltpu.CompilerParams(vmem_limit_bytes=20 * 2**20),
+        compiler_params=pltpu.CompilerParams(vmem_limit_bytes=14 * 2**20),
         cost_estimate=pl.CostEstimate(
             flops=2 * 512 * width * depth, bytes_accessed=2 * (width * depth + 512 * (width + depth)), transcendentals=0
         ),
@@ -223,7 +229,8 @@
     return jnp.concatenate(sort_flips(pieces, y)).transpose(1, 0, 2)
 
 
-def gather_rows(chunk, a3, z):
+def gather_rows(chunk, part, z):
+    a3 = move_mirror(part)
     a1 = move_z(a3, 2)
     a2, a0 = move_z(jnp.stack([a3, a1]), 1)
     own = jnp.concatenate(sort_flips((a0, a1, a2, a3), z)).transpose(1, 0, 2)
@@ -289,15 +296,14 @@
     spread = by_chunk(inverse_spread_per_position[0])
     gain = layernorm_multiplier[0]
 
-    rows = [move_mirror(rows[: 2 * ROWS]), move_mirror(rows[2 * ROWS :])]
-    rows = [rows[0][:ROWS], rows[0][ROWS:], rows[1]]
     mine, totals = [], []
     for k in range(CHUNKS):
-        gathered = gather_rows(k, rows[k], z)
+        gathered = gather_rows(k, rows[ROWS * k : ROWS * (k + 1)], z)
         keep, send, own_rows = hidden_product(k, pos, *gathered, contraction_factor[0])
         block = (reduce_hidden(k, keep, send) * slope[k]).astype(BF)
         near_pair, wide_pair = gather_ring(k, block, "y")
-        pairs = (near_pair, wide_pair, move_core(jnp.concatenate([near_pair, wide_pair])))
+        same = jnp.concatenate([near_pair, wide_pair])
+        pairs = (same, move_core(same))
         keep, send = feature_product(k, pos, pairs, expansion_factor[0])
         mine.append(own_rows.reshape(32, -1))
         totals.append(reduce_x(k, keep, send))

time: 210 us -> 208 us (level)
    ppermute x12, waiting for transfers between devices: 12.1 us -> 20.4 us  [move_ring(): lax.ppermute(array, ('core', axis), [(4 * c + i, 4 * d + j) for c, i, d,...]
    ppermute x2 -> x3, waiting for transfers between devices: 8.21 us -> 0.01 us  [move_mirror(): return lax.ppermute(array, ('section', 'z'), [(i, 7 - i) for i in range(8)])]
    ppermute x10, waiting for transfers between devices: 20.4 us -> 14.9 us  [move_z(): return lax.ppermute(array, 'z', [(z, z ^ flip) for z in range(4)])]
    ppermute x12, starting transfers between devices: 16.5 us -> 12.2 us  [move_ring(): lax.ppermute(array, ('y', 'core'), [(2 * i + c, 2 * j + d) for c, i, d, j...]
    ppermute x8, starting transfers between devices: 37.2 us -> 40.2 us  [move_core(): return lax.ppermute(array, 'core', [(0, 1), (1, 0)])]
    ppermute x2 -> x3, starting transfers between devices: 4.61 us -> 7.18 us  [move_mirror(): return lax.ppermute(array, ('section', 'z'), [(i, 7 - i) for i in range(8)])]
    ppermute x12, waiting for transfers between devices: 25.7 us -> 28.2 us  [move_ring(): lax.ppermute(array, ('y', 'core'), [(2 * i + c, 2 * j + d) for c, i, d, j...]
  transfers between devices with their start and end apart: 49 -> 50, of which waited for: 27 -> 27; matrix products, arithmetic and copies ran while one was open for 6% -> 6% of each run, Pallas kernels for 14% -> 15%
where the time goes in v2:
time: 208 us; the launch traced here: 206 us
  starting transfers between devices  84.9 us (41%)
  waiting for transfers between devices  74 us (36%)
  Pallas kernels  30.8 us (15%)
  other arithmetic  11.2 us (5%)
  local copies, waits for them, and re-layouts  4.85 us (2%)
    ppermute x8, starting transfers between devices, move_core(): return lax.ppermute(array, 'core', [(0, 1), (1, 0)])  40.2 us
    ppermute x12, waiting for transfers between devices, move_ring(): lax.ppermute(array, ('y', 'core'), [(2 * i + c, 2 * j + d) for c, i, d, j...  28.2 us
    ppermute x12, waiting for transfers between devices, move_ring(): lax.ppermute(array, ('core', axis), [(4 * c + i, 4 * d + j) for c, i, d,...  20.4 us
    ppermute x10, waiting for transfers between devices, move_z(): return lax.ppermute(array, 'z', [(z, z ^ flip) for z in range(4)])  14.9 us
    pallas_call x3, Pallas kernels, feature_product(): pl.pallas_call(functools.partial(feature_kernel, chunk), grid=(width // t...  14.8 us
    pallas_call x3, Pallas kernels, hidden_product(): pl.pallas_call(functools.partial(hidden_kernel, chunk), grid=(width // ti...  14.6 us
    ppermute x12, starting transfers between devices, move_ring(): lax.ppermute(array, ('y', 'core'), [(2 * i + c, 2 * j + d) for c, i, d, j...  12.2 us
    ppermute x10, starting transfers between devices, move_z(): return lax.ppermute(array, 'z', [(z, z ^ flip) for z in range(4)])  11.3 us
  transfers between devices with their start and end apart: 50, of which 27 were waited for; matrix products, arithmetic and copies ran while one was open for 6% of the time, Pallas kernels for 15%

profile of v2, /device:TPU:1, one launch (start us, length us, event | category | flops | bytes accessed | tf_op | source)
XLA Modules:
  0.0 206.3 jit_solution(10442820402555015776)
XLA Ops:
  1.0 3.3 %collective-permute-start = (bf16[4,12,1024]{2,1,0:T(8,128)(2,1)S(1)}, bf16[4,12,1024]{2,1,0:T(8,128)(2,1)S(1)}, u32[]{:S(2)}, u32[]{:S(2)}) collective-permute-start(bf16[4,12,1024]{2,1,0:T(8,128)(2,1)S(1)} %broadcast_select_fusion), channel_id=1, source_target_pairs={{0,16},{16,0},{1,17},{17,1},{2,18},{18,2},{3,19},{19,3},{4,20},{20... | collective-permute-start | bytes 294920 | tf_op jit(solution)/shard_map/ppermute | solution.py:45
  12.3 4.5 %collective-permute-start.14 = (bf16[4,8,1024]{2,0,1:T(4,128)(2,1)S(1)}, bf16[4,8,1024]{2,0,1:T(4,128)(2,1)S(1)}, u32[]{:S(2)}, u32[]{:S(2)}) collective-permute-start(bf16[4,8,1024]{2,0,1:T(4,128)(2,1)S(1)} %get-tuple-element.54), channel_id=1, source_target_pairs={{0,140},{4,136},{8,132},{12,128},{128,12},{132,8},{136,4},{140,0},... | collective-permute-start | bytes 196616 | tf_op jit(solution)/shard_map/ppermute | solution.py:41
  19.5 3.9 %collective-permute-start.15 = (bf16[4,8,1024]{2,0,1:T(4,128)(2,1)S(1)}, bf16[4,8,1024]{2,0,1:T(4,128)(2,1)S(1)}, u32[]{:S(2)}, u32[]{:S(2)}) collective-permute-start(bf16[4,8,1024]{2,0,1:T(4,128)(2,1)S(1)} %collective-permute-done.14), channel_id=1, source_target_pairs={{0,8},{4,12},{8,0},{12,4},{1,9},{5,13},{9,1},{13,5},{2,10},{6,14},... | collective-permute-start | bytes 196616 | tf_op jit(solution)/shard_map/ppermute | solution.py:37
  29.5 2.8 %collective-permute-done.5 = bf16[4,8,1024]{2,0,1:T(4,128)(2,1)S(1)} collective-permute-done((bf16[4,8,1024]{2,0,1:T(4,128)(2,1)S(1)}, bf16[4,8,1024]{2,0,1:T(4,128)(2,1)S(1)}, u32[]{:S(2)}, u32[]{:S(2)}) %collective-permute-start.5) | collective-permute-done | bytes 65568 | tf_op jit(solution)/shard_map/ppermute | solution.py:37
  36.3 3.0 %collective-permute-done.17 = bf16[8,16,1024]{2,1,0:T(8,128)(2,1)S(1)} collective-permute-done((bf16[8,16,1024]{2,1,0:T(8,128)(2,1)S(1)}, bf16[8,16,1024]{2,1,0:T(8,128)(2,1)S(1)}, u32[]{:S(2)}, u32[]{:S(2)}) %collective-permute-start.17) | collective-permute-done | bytes 262176 | tf_op jit(solution)/shard_map/ppermute | solution.py:29
  45.7 3.7 %collective-permute-done.18.wide_pair = bf16[2,8,16,1024]{3,2,1,0:T(8,128)(2,1)S(1)} collective-permute-done((bf16[2,8,16,1024]{3,2,1,0:T(8,128)(2,1)S(1)}, bf16[2,8,16,1024]{3,2,1,0:T(8,128)(2,1)S(1)}, u32[]{:S(2)}, u32[]{:S(2)}) %collective-permute-start.18) | collective-permute-done | bytes 524320 | tf_op jit(solution)/shard_map/ppermute | solution.py:29
  49.4 4.8 %shard_map.75 = (bf16[4,64,2048]{2,1,0:T(8,128)(2,1)S(1)}, bf16[4,64,2048]{2,1,0:T(8,128)(2,1)S(1)}, f32[4,8,1024]{2,1,0:T(8,128)S(1)}) custom-call(s32[4]{0:T(128)S(1)} %pad_add_fusion.pos, bf16[2,8,16,1024]{3,2,1,0:T(8,128)(2,1)S(1)} %pad_maximum_fusion.6.near_pair, bf16[2,8,16,1024]{3,2,1,0:T(8,128)(2,1)S(1)} %collective-permute-done.18.wide_pair, ...), custom_call_target="tpu_custom_call" | custom-call | flops 2147483648 | bytes 7340032 | tf_op jit(solution)/shard_map/pallas_call | solution.py:138
  54.3 11.6 %collective-permute-start.37 = (bf16[4,64,2048]{2,1,0:T(8,128)(2,1)S(1)}, bf16[4,64,2048]{2,1,0:T(8,128)(2,1)S(1)}, u32[]{:S(2)}, u32[]{:S(2)}) collective-permute-start(bf16[4,64,2048]{2,1,0:T(8,128)(2,1)S(1)} %get-tuple-element.37), channel_id=1, source_target_pairs={{0,16},{16,0},{1,17},{17,1},{2,18},{18,2},{3,19},{19,3},{4,20},{20... | collective-permute-start | bytes 3145736 | tf_op jit(solution)/shard_map/ppermute | solution.py:45
  66.1 4.9 %shard_map.74 = (bf16[4,64,2048]{2,1,0:T(8,128)(2,1)S(1)}, bf16[4,64,2048]{2,1,0:T(8,128)(2,1)S(1)}, f32[4,8,1024]{2,1,0:T(8,128)S(1)}) custom-call(s32[4]{0:T(128)S(1)} %pad_add_fusion.pos, bf16[2,8,16,1024]{3,2,1,0:T(8,128)(2,1)S(1)} %pad_maximum_fusion.5.near_pair, bf16[2,8,16,1024]{3,2,1,0:T(8,128)(2,1)S(1)} %collective-permute-done.13.wide_pair, ...), custom_call_target="tpu_custom_call" | custom-call | flops 2147483648 | bytes 7340032 | tf_op jit(solution)/shard_map/pallas_call | solution.py:138
  71.0 2.7 %collective-permute-start.29 = (bf16[4,64,2048]{2,1,0:T(8,128)(2,1)S(1)}, bf16[4,64,2048]{2,1,0:T(8,128)(2,1)S(1)}, u32[]{:S(2)}, u32[]{:S(2)}) collective-permute-start(bf16[4,64,2048]{2,1,0:T(8,128)(2,1)S(1)} %get-tuple-element.32), channel_id=1, source_target_pairs={{0,16},{16,0},{1,17},{17,1},{2,18},{18,2},{3,19},{19,3},{4,20},{20... | collective-permute-start | bytes 3145736 | tf_op jit(solution)/shard_map/ppermute | solution.py:45
  74.4 4.8 %shard_map.73 = (bf16[4,64,2048]{2,1,0:T(8,128)(2,1)S(1)}, bf16[4,64,2048]{2,1,0:T(8,128)(2,1)S(1)}, f32[4,8,1024]{2,1,0:T(8,128)S(1)}) custom-call(s32[4]{0:T(128)S(1)} %pad_add_fusion.pos, bf16[2,8,16,1024]{3,2,1,0:T(8,128)(2,1)S(1)} %pad_maximum_fusion.4.near_pair, bf16[2,8,16,1024]{3,2,1,0:T(8,128)(2,1)S(1)} %collective-permute-done.8.wide_pair, ...), custom_call_target="tpu_custom_call" | custom-call | flops 2147483648 | bytes 7340032 | tf_op jit(solution)/shard_map/pallas_call | solution.py:138
  86.4 10.1 %collective-permute-done.38 = bf16[2,64,2048]{2,1,0:T(8,128)(2,1)S(1)} collective-permute-done((bf16[2,64,2048]{2,1,0:T(8,128)(2,1)S(1)}, bf16[2,64,2048]{2,1,0:T(8,128)(2,1)S(1)}, u32[]{:S(2)}, u32[]{:S(2)}) %collective-permute-start.38) | collective-permute-done | bytes 524320 | tf_op jit(solution)/shard_map/ppermute | solution.py:28
  97.5 3.4 %collective-permute-done.30 = bf16[2,64,2048]{2,1,0:T(8,128)(2,1)S(1)} collective-permute-done((bf16[2,64,2048]{2,1,0:T(8,128)(2,1)S(1)}, bf16[2,64,2048]{2,1,0:T(8,128)(2,1)S(1)}, u32[]{:S(2)}, u32[]{:S(2)}) %collective-permute-start.30) | collective-permute-done | bytes 524320 | tf_op jit(solution)/shard_map/ppermute | solution.py:28
  101.1 4.3 %collective-permute-done.20 = bf16[2,64,2048]{2,1,0:T(8,128)(2,1)S(1)} collective-permute-done((bf16[2,64,2048]{2,1,0:T(8,128)(2,1)S(1)}, bf16[2,64,2048]{2,1,0:T(8,128)(2,1)S(1)}, u32[]{:S(2)}, u32[]{:S(2)}) %collective-permute-start.20) | collective-permute-done | bytes 524320 | tf_op jit(solution)/shard_map/ppermute | solution.py:28
  110.9 4.4 %collective-permute-done.40 = bf16[64,2048]{1,0:T(8,128)(2,1)S(1)} collective-permute-done((bf16[64,2048]{1,0:T(8,128)(2,1)S(1)}, bf16[64,2048]{1,0:T(8,128)(2,1)S(1)}, u32[]{:S(2)}, u32[]{:S(2)}) %collective-permute-start.40) | collective-permute-done | bytes 262176 | tf_op jit(solution)/shard_map/ppermute | solution.py:28
  120.1 3.6 %collective-permute-done.22 = bf16[64,2048]{1,0:T(8,128)(2,1)S(1)} collective-permute-done((bf16[64,2048]{1,0:T(8,128)(2,1)S(1)}, bf16[64,2048]{1,0:T(8,128)(2,1)S(1)}, u32[]{:S(2)}, u32[]{:S(2)}) %collective-permute-start.22) | collective-permute-done | bytes 262176 | tf_op jit(solution)/shard_map/ppermute | solution.py:28
  124.7 11.3 %collective-permute-start.42 = (bf16[4,64,2048]{2,1,0:T(8,128)(2,1)S(1)}, bf16[4,64,2048]{2,1,0:T(8,128)(2,1)S(1)}, u32[]{:S(2)}, u32[]{:S(2)}) collective-permute-start(bf16[4,64,2048]{2,1,0:T(8,128)(2,1)S(1)} %pad_maximum_fusion.3.same), channel_id=1, source_target_pairs={{0,16},{16,0},{1,17},{17,1},{2,18},{18,2},{3,19},{19,3},{4,20},{20... | collective-permute-start | bytes 3145736 | tf_op jit(solution)/shard_map/ppermute | solution.py:45
  136.2 5.0 %collective-permute-start.34 = (bf16[4,64,2048]{2,1,0:T(8,128)(2,1)S(1)}, bf16[4,64,2048]{2,1,0:T(8,128)(2,1)S(1)}, u32[]{:S(2)}, u32[]{:S(2)}) collective-permute-start(bf16[4,64,2048]{2,1,0:T(8,128)(2,1)S(1)} %pad_maximum_fusion.2.same), channel_id=1, source_target_pairs={{0,16},{16,0},{1,17},{17,1},{2,18},{18,2},{3,19},{19,3},{4,20},{20... | collective-permute-start | bytes 3145736 | tf_op jit(solution)/shard_map/ppermute | solution.py:45
  143.5 4.9 %shard_map.79 = (bf16[2,4,32,1024]{3,2,1,0:T(8,128)(2,1)S(1)}, bf16[2,4,32,1024]{3,2,1,0:T(8,128)(2,1)S(1)}) custom-call(s32[4]{0:T(128)S(1)} %pad_add_fusion.pos, bf16[4,64,2048]{2,1,0:T(8,128)(2,1)S(1)} %pad_maximum_fusion.3.same, bf16[4,64,2048]{2,1,0:T(8,128)(2,1)S(1)} %collective-permute-done.42.other, bf16[1024,2048]{1,0:T(8,128)(2,1)S(1)} %bitcast.248), custom_call_target="tpu_custom_call" | custom-call | flops 2147483648 | bytes 7340032 | tf_op jit(solution)/shard_map/pallas_call | solution.py:189
  148.5 4.9 %shard_map.78 = (bf16[2,4,32,1024]{3,2,1,0:T(8,128)(2,1)S(1)}, bf16[2,4,32,1024]{3,2,1,0:T(8,128)(2,1)S(1)}) custom-call(s32[4]{0:T(128)S(1)} %pad_add_fusion.pos, bf16[4,64,2048]{2,1,0:T(8,128)(2,1)S(1)} %pad_maximum_fusion.2.same, bf16[4,64,2048]{2,1,0:T(8,128)(2,1)S(1)} %collective-permute-done.34.other, bf16[1024,2048]{1,0:T(8,128)(2,1)S(1)} %bitcast.249), custom_call_target="tpu_custom_call" | custom-call | flops 2147483648 | bytes 7340032 | tf_op jit(solution)/shard_map/pallas_call | solution.py:189
  156.0 4.9 %shard_map.77 = (bf16[2,4,32,1024]{3,2,1,0:T(8,128)(2,1)S(1)}, bf16[2,4,32,1024]{3,2,1,0:T(8,128)(2,1)S(1)}) custom-call(s32[4]{0:T(128)S(1)} %pad_add_fusion.pos, bf16[4,64,2048]{2,1,0:T(8,128)(2,1)S(1)} %pad_maximum_fusion.1.same, bf16[4,64,2048]{2,1,0:T(8,128)(2,1)S(1)} %collective-permute-done.24.other, bf16[1024,2048]{1,0:T(8,128)(2,1)S(1)} %bitcast.250), custom_call_target="tpu_custom_call" | custom-call | flops 2147483648 | bytes 7340032 | tf_op jit(solution)/shard_map/pallas_call | solution.py:189
  166.6 6.9 %collective-permute-done.25 = bf16[2,4,32,1024]{3,2,1,0:T(8,128)(2,1)} collective-permute-done((bf16[2,4,32,1024]{3,2,1,0:T(8,128)(2,1)S(1)}, bf16[2,4,32,1024]{3,2,1,0:T(8,128)(2,1)}, u32[]{:S(2)}, u32[]{:S(2)}) %collective-permute-start.25) | collective-permute-done | bytes 524320 | tf_op jit(solution)/shard_map/ppermute | solution.py:29
  178.0 3.1 %collective-permute-done.26 = bf16[4,32,1024]{2,1,0:T(8,128)(2,1)S(1)} collective-permute-done((bf16[4,32,1024]{2,1,0:T(8,128)(2,1)S(1)}, bf16[4,32,1024]{2,1,0:T(8,128)(2,1)S(1)}, u32[]{:S(2)}, u32[]{:S(2)}) %collective-permute-start.26) | collective-permute-done | bytes 262176 | tf_op jit(solution)/shard_map/ppermute | solution.py:29
  190.1 5.3 %collective-permute-done.28 = bf16[1,32,1024]{2,1,0:T(8,128)(2,1)S(1)} collective-permute-done((bf16[1,32,1024]{2,1,0:T(8,128)(2,1)S(1)}, bf16[1,32,1024]{2,1,0:T(8,128)(2,1)S(1)}, u32[]{:S(2)}, u32[]{:S(2)}) %collective-permute-start.28) | collective-permute-done | bytes 65568 | tf_op jit(solution)/shard_map/ppermute | solution.py:37
  (172 shorter events, 83.4 us)
Async XLA Ops:
  39.4 10.0 %collective-permute-start.18 = (bf16[2,8,16,1024]{3,2,1,0:T(8,128)(2,1)S(1)}, bf16[2,8,16,1024]{3,2,1,0:T(8,128)(2,1)S(1)}, u32[]{:S(2)}, u32[]{:S(2)}) collective-permute-start(bf16[2,8,16,1024]{3,2,1,0:T(8,128)(2,1)S(1)} %pad_maximum_fusion.6.near_pair), channel_id=1, source_target_pairs={{0,3},{1,2},{2,1},{3,0},{16,17},{17,16},{18,19},{19,18},{4,7},{5,6... | collective-permute-start | bytes 1572872 | tf_op jit(solution)/shard_map/ppermute | solution.py:29
  42.5 23.5 %collective-permute-start.13 = (bf16[2,8,16,1024]{3,2,1,0:T(8,128)(2,1)S(1)}, bf16[2,8,16,1024]{3,2,1,0:T(8,128)(2,1)S(1)}, u32[]{:S(2)}, u32[]{:S(2)}) collective-permute-start(bf16[2,8,16,1024]{3,2,1,0:T(8,128)(2,1)S(1)} %pad_maximum_fusion.5.near_pair), channel_id=1, source_target_pairs={{0,1},{1,0},{2,3},{3,2},{16,19},{17,18},{18,17},{19,16},{4,5},{5,4... | collective-permute-start | bytes 1572872 | tf_op jit(solution)/shard_map/ppermute | solution.py:29
  43.9 22.0 %collective-permute-start.7 = (bf16[8,16,1024]{2,1,0:T(8,128)(2,1)S(1)}, bf16[8,16,1024]{2,1,0:T(8,128)(2,1)S(1)}, u32[]{:S(2)}, u32[]{:S(2)}) collective-permute-start(bf16[8,16,1024]{2,1,0:T(8,128)(2,1)S(1)} %get-tuple-element.63), channel_id=1, source_target_pairs={{0,1},{1,0},{2,3},{3,2},{16,19},{17,18},{18,17},{19,16},{4,5},{5,4... | collective-permute-start | bytes 786440 | tf_op jit(solution)/shard_map/ppermute | solution.py:29
  54.3 28.6 %collective-permute-start.37 = (bf16[4,64,2048]{2,1,0:T(8,128)(2,1)S(1)}, bf16[4,64,2048]{2,1,0:T(8,128)(2,1)S(1)}, u32[]{:S(2)}, u32[]{:S(2)}) collective-permute-start(bf16[4,64,2048]{2,1,0:T(8,128)(2,1)S(1)} %get-tuple-element.37), channel_id=1, source_target_pairs={{0,16},{16,0},{1,17},{17,1},{2,18},{18,2},{3,19},{19,3},{4,20},{20... | collective-permute-start | bytes 3145736 | tf_op jit(solution)/shard_map/ppermute | solution.py:45
  65.9 8.4 %collective-permute-start.8 = (bf16[2,8,16,1024]{3,2,1,0:T(8,128)(2,1)S(1)}, bf16[2,8,16,1024]{3,2,1,0:T(8,128)(2,1)S(1)}, u32[]{:S(2)}, u32[]{:S(2)}) collective-permute-start(bf16[2,8,16,1024]{3,2,1,0:T(8,128)(2,1)S(1)} %pad_maximum_fusion.4.near_pair), channel_id=1, source_target_pairs={{0,3},{1,2},{2,1},{3,0},{16,17},{17,16},{18,19},{19,18},{4,7},{5,6... | collective-permute-start | bytes 1572872 | tf_op jit(solution)/shard_map/ppermute | solution.py:29
  71.0 14.5 %collective-permute-start.29 = (bf16[4,64,2048]{2,1,0:T(8,128)(2,1)S(1)}, bf16[4,64,2048]{2,1,0:T(8,128)(2,1)S(1)}, u32[]{:S(2)}, u32[]{:S(2)}) collective-permute-start(bf16[4,64,2048]{2,1,0:T(8,128)(2,1)S(1)} %get-tuple-element.32), channel_id=1, source_target_pairs={{0,16},{16,0},{1,17},{17,1},{2,18},{18,2},{3,19},{19,3},{4,20},{20... | collective-permute-start | bytes 3145736 | tf_op jit(solution)/shard_map/ppermute | solution.py:45
  83.0 13.5 %collective-permute-start.38 = (bf16[2,64,2048]{2,1,0:T(8,128)(2,1)S(1)}, bf16[2,64,2048]{2,1,0:T(8,128)(2,1)S(1)}, u32[]{:S(2)}, u32[]{:S(2)}) collective-permute-start(bf16[2,64,2048]{2,1,0:T(8,128)(2,1)S(1)} %add_convert_fusion), channel_id=1, source_target_pairs={{0,96},{32,64},{64,32},{96,0},{16,48},{48,16},{80,112},{112,80},{1... | collective-permute-start | bytes 1572872 | tf_op jit(solution)/shard_map/ppermute | solution.py:28
  85.6 15.3 %collective-permute-start.30 = (bf16[2,64,2048]{2,1,0:T(8,128)(2,1)S(1)}, bf16[2,64,2048]{2,1,0:T(8,128)(2,1)S(1)}, u32[]{:S(2)}, u32[]{:S(2)}) collective-permute-start(bf16[2,64,2048]{2,1,0:T(8,128)(2,1)S(1)} %add_convert_fusion.1), channel_id=1, source_target_pairs={{0,32},{32,0},{64,96},{96,64},{16,112},{48,80},{80,48},{112,16},{1... | collective-permute-start | bytes 1572872 | tf_op jit(solution)/shard_map/ppermute | solution.py:28
  85.9 19.6 %collective-permute-start.20 = (bf16[2,64,2048]{2,1,0:T(8,128)(2,1)S(1)}, bf16[2,64,2048]{2,1,0:T(8,128)(2,1)S(1)}, u32[]{:S(2)}, u32[]{:S(2)}) collective-permute-start(bf16[2,64,2048]{2,1,0:T(8,128)(2,1)S(1)} %add_convert_fusion.2), channel_id=1, source_target_pairs={{0,96},{32,64},{64,32},{96,0},{16,48},{48,16},{80,112},{112,80},{1... | collective-permute-start | bytes 1572872 | tf_op jit(solution)/shard_map/ppermute | solution.py:28
  96.6 9.9 %collective-permute-start.39 = (bf16[64,2048]{1,0:T(8,128)(2,1)S(1)}, bf16[64,2048]{1,0:T(8,128)(2,1)S(1)}, u32[]{:S(2)}, u32[]{:S(2)}) collective-permute-start(bf16[64,2048]{1,0:T(8,128)(2,1)S(1)} %fusion.17), channel_id=1, source_target_pairs={{0,32},{32,0},{64,96},{96,64},{16,112},{48,80},{80,48},{112,16},{1... | collective-permute-start | bytes 786440 | tf_op jit(solution)/shard_map/ppermute | solution.py:28
  105.5 11.6 %collective-permute-start.21 = (bf16[64,2048]{1,0:T(8,128)(2,1)S(1)}, bf16[64,2048]{1,0:T(8,128)(2,1)S(1)}, u32[]{:S(2)}, u32[]{:S(2)}) collective-permute-start(bf16[64,2048]{1,0:T(8,128)(2,1)S(1)} %fusion.13), channel_id=1, source_target_pairs={{0,32},{32,0},{64,96},{96,64},{16,112},{48,80},{80,48},{112,16},{1... | collective-permute-start | bytes 786440 | tf_op jit(solution)/shard_map/ppermute | solution.py:28
  106.7 8.6 %collective-permute-start.40 = (bf16[64,2048]{1,0:T(8,128)(2,1)S(1)}, bf16[64,2048]{1,0:T(8,128)(2,1)S(1)}, u32[]{:S(2)}, u32[]{:S(2)}) collective-permute-start(bf16[64,2048]{1,0:T(8,128)(2,1)S(1)} %fusion.2), channel_id=1, source_target_pairs={{0,32},{32,0},{64,96},{96,64},{16,112},{48,80},{80,48},{112,16},{1... | collective-permute-start | bytes 786440 | tf_op jit(solution)/shard_map/ppermute | solution.py:28
  109.4 8.6 %collective-permute-start.32 = (bf16[64,2048]{1,0:T(8,128)(2,1)S(1)}, bf16[64,2048]{1,0:T(8,128)(2,1)S(1)}, u32[]{:S(2)}, u32[]{:S(2)}) collective-permute-start(bf16[64,2048]{1,0:T(8,128)(2,1)S(1)} %fusion.5), channel_id=1, source_target_pairs={{0,96},{32,64},{64,32},{96,0},{16,48},{48,16},{80,112},{112,80},{1... | collective-permute-start | bytes 786440 | tf_op jit(solution)/shard_map/ppermute | solution.py:28
  115.3 9.3 %collective-permute-start.41 = (bf16[2,64,2048]{2,1,0:T(8,128)(2,1)S(1)}, bf16[2,64,2048]{2,1,0:T(8,128)(2,1)S(1)}, u32[]{:S(2)}, u32[]{:S(2)}) collective-permute-start(bf16[2,64,2048]{2,1,0:T(8,128)(2,1)S(1)} %pad_maximum_fusion.9), channel_id=1, source_target_pairs={{0,96},{32,64},{64,32},{96,0},{16,48},{48,16},{80,112},{112,80},{1... | collective-permute-start | bytes 1572872 | tf_op jit(solution)/shard_map/ppermute | solution.py:28
  118.0 18.1 %collective-permute-start.33 = (bf16[2,64,2048]{2,1,0:T(8,128)(2,1)S(1)}, bf16[2,64,2048]{2,1,0:T(8,128)(2,1)S(1)}, u32[]{:S(2)}, u32[]{:S(2)}) collective-permute-start(bf16[2,64,2048]{2,1,0:T(8,128)(2,1)S(1)} %pad_maximum_fusion.8), channel_id=1, source_target_pairs={{0,32},{32,0},{64,96},{96,64},{16,112},{48,80},{80,48},{112,16},{1... | collective-permute-start | bytes 1572872 | tf_op jit(solution)/shard_map/ppermute | solution.py:28
  123.8 17.4 %collective-permute-start.23 = (bf16[2,64,2048]{2,1,0:T(8,128)(2,1)S(1)}, bf16[2,64,2048]{2,1,0:T(8,128)(2,1)S(1)}, u32[]{:S(2)}, u32[]{:S(2)}) collective-permute-start(bf16[2,64,2048]{2,1,0:T(8,128)(2,1)S(1)} %pad_maximum_fusion.7), channel_id=1, source_target_pairs={{0,96},{32,64},{64,32},{96,0},{16,48},{48,16},{80,112},{112,80},{1... | collective-permute-start | bytes 1572872 | tf_op jit(solution)/shard_map/ppermute | solution.py:28
  124.7 18.7 %collective-permute-start.42 = (bf16[4,64,2048]{2,1,0:T(8,128)(2,1)S(1)}, bf16[4,64,2048]{2,1,0:T(8,128)(2,1)S(1)}, u32[]{:S(2)}, u32[]{:S(2)}) collective-permute-start(bf16[4,64,2048]{2,1,0:T(8,128)(2,1)S(1)} %pad_maximum_fusion.3.same), channel_id=1, source_target_pairs={{0,16},{16,0},{1,17},{17,1},{2,18},{18,2},{3,19},{19,3},{4,20},{20... | collective-permute-start | bytes 3145736 | tf_op jit(solution)/shard_map/ppermute | solution.py:45
  136.2 12.3 %collective-permute-start.34 = (bf16[4,64,2048]{2,1,0:T(8,128)(2,1)S(1)}, bf16[4,64,2048]{2,1,0:T(8,128)(2,1)S(1)}, u32[]{:S(2)}, u32[]{:S(2)}) collective-permute-start(bf16[4,64,2048]{2,1,0:T(8,128)(2,1)S(1)} %pad_maximum_fusion.2.same), channel_id=1, source_target_pairs={{0,16},{16,0},{1,17},{17,1},{2,18},{18,2},{3,19},{19,3},{4,20},{20... | collective-permute-start | bytes 3145736 | tf_op jit(solution)/shard_map/ppermute | solution.py:45
  141.3 14.7 %collective-permute-start.24 = (bf16[4,64,2048]{2,1,0:T(8,128)(2,1)S(1)}, bf16[4,64,2048]{2,1,0:T(8,128)(2,1)S(1)}, u32[]{:S(2)}, u32[]{:S(2)}) collective-permute-start(bf16[4,64,2048]{2,1,0:T(8,128)(2,1)S(1)} %pad_maximum_fusion.1.same), channel_id=1, source_target_pairs={{0,16},{16,0},{1,17},{17,1},{2,18},{18,2},{3,19},{19,3},{4,20},{20... | collective-permute-start | bytes 3145736 | tf_op jit(solution)/shard_map/ppermute | solution.py:45
  148.4 15.3 %collective-permute-start.43 = (bf16[2,4,32,1024]{3,2,1,0:T(8,128)(2,1)S(1)}, bf16[2,4,32,1024]{3,2,1,0:T(8,128)(2,1)}, u32[]{:S(2)}, u32[]{:S(2)}) collective-permute-start(bf16[2,4,32,1024]{3,2,1,0:T(8,128)(2,1)S(1)} %get-tuple-element.40), channel_id=1, source_target_pairs={{0,3},{1,2},{2,1},{3,0},{16,17},{17,16},{18,19},{19,18},{4,7},{5,6... | collective-permute-start | bytes 1572872 | tf_op jit(solution)/shard_map/ppermute | solution.py:29
  153.5 12.0 %collective-permute-start.35 = (bf16[2,4,32,1024]{3,2,1,0:T(8,128)(2,1)S(1)}, bf16[2,4,32,1024]{3,2,1,0:T(8,128)(2,1)}, u32[]{:S(2)}, u32[]{:S(2)}) collective-permute-start(bf16[2,4,32,1024]{3,2,1,0:T(8,128)(2,1)S(1)} %get-tuple-element.35), channel_id=1, source_target_pairs={{0,1},{1,0},{2,3},{3,2},{16,19},{17,18},{18,17},{19,16},{4,5},{5,4... | collective-permute-start | bytes 1572872 | tf_op jit(solution)/shard_map/ppermute | solution.py:29
  160.9 12.5 %collective-permute-start.25 = (bf16[2,4,32,1024]{3,2,1,0:T(8,128)(2,1)S(1)}, bf16[2,4,32,1024]{3,2,1,0:T(8,128)(2,1)}, u32[]{:S(2)}, u32[]{:S(2)}) collective-permute-start(bf16[2,4,32,1024]{3,2,1,0:T(8,128)(2,1)S(1)} %get-tuple-element.30), channel_id=1, source_target_pairs={{0,3},{1,2},{2,1},{3,0},{16,17},{17,16},{18,19},{19,18},{4,7},{5,6... | collective-permute-start | bytes 1572872 | tf_op jit(solution)/shard_map/ppermute | solution.py:29
  164.7 9.9 %collective-permute-start.44 = (bf16[4,32,1024]{2,1,0:T(8,128)(2,1)S(1)}, bf16[4,32,1024]{2,1,0:T(8,128)(2,1)S(1)}, u32[]{:S(2)}, u32[]{:S(2)}) collective-permute-start(bf16[4,32,1024]{2,1,0:T(8,128)(2,1)S(1)} %fusion.18), channel_id=1, source_target_pairs={{0,1},{1,0},{2,3},{3,2},{16,19},{17,18},{18,17},{19,16},{4,5},{5,4... | collective-permute-start | bytes 786440 | tf_op jit(solution)/shard_map/ppermute | solution.py:29
  166.5 9.8 %collective-permute-start.36 = (bf16[4,32,1024]{2,1,0:T(8,128)(2,1)S(1)}, bf16[4,32,1024]{2,1,0:T(8,128)(2,1)S(1)}, u32[]{:S(2)}, u32[]{:S(2)}) collective-permute-start(bf16[4,32,1024]{2,1,0:T(8,128)(2,1)S(1)} %fusion.16), channel_id=1, source_target_pairs={{0,3},{1,2},{2,1},{3,0},{16,17},{17,16},{18,19},{19,18},{4,7},{5,6... | collective-permute-start | bytes 786440 | tf_op jit(solution)/shard_map/ppermute | solution.py:29
  (32 other events, 280.3 us)

commit v3 on v2

--- a/solution.py
+++ b/solution.py
@@ -169,11 +169,8 @@
             lhs[2 * jnp.bitwise_xor(y, ring_flip(chunk, 1 - c, j)) + 1 - c] = other[j]
 
 
-    @pl.loop(0, 2)
-    def _(index):
-        part = pl.ds(4 * index, 4)
-        result[part] = nt_dot(lhs[part].reshape(256, -1), weight[...]).reshape(4, *result.shape[1:])
-
+    rows = lhs[...].reshape(512, -1)
+    result[...] = nt_dot(rows, weight[...]).reshape(result.shape)
     for x_rel, x_flip in enumerate(ring_order(chunk, c)):
         to = jnp.bitwise_xor(x, x_flip)
         out = keep if x_rel < 2 else send
@@ -229,12 +226,13 @@
     return jnp.concatenate(sort_flips(pieces, y)).transpose(1, 0, 2)
 
 
-def gather_rows(chunk, part, z):
-    a3 = move_mirror(part)
+def gather_z(rows, z):
+    a3 = move_mirror(rows)
     a1 = move_z(a3, 2)
     a2, a0 = move_z(jnp.stack([a3, a1]), 1)
-    own = jnp.concatenate(sort_flips((a0, a1, a2, a3), z)).transpose(1, 0, 2)
-    return gather_ring(chunk, own, "x")
+    pieces = sort_flips((a0, a1, a2, a3), z)
+    starts = range(0, rows.shape[0], ROWS)
+    return [jnp.concatenate([piece[at : at + ROWS] for piece in pieces]).transpose(1, 0, 2) for at in starts]
 
 
 def gather_ring(chunk, block, axis):
@@ -243,26 +241,21 @@
     return pair, move_ring(pair, axis, second)
 
 
-def reduce_hidden(chunk, keep, send):
+def reduce_hidden(chunk, keep, other):
     second, first = flips(chunk)
-    other = move_core(send)
     far = move_ring(add(keep[2:], other[2:]).astype(BF), "y", first)
     last = move_ring(add(keep[1], other[1], far[1]).astype(BF), "y", second)
     return add(keep[0], other[0], far[0], last)
 
 
-def reduce_x(chunk, keep, send):
+def reduce_features(chunk, keep, send):
     second, first = flips(chunk)
     far = move_ring(send, "x", first)
     last = move_ring(add(keep[1], far[1]).astype(BF), "x", second)
-    return add(keep[0], far[0], last)
-
-
-def reduce_z(totals):
-    total = jnp.stack(totals, axis=1)
+    total = add(keep[0], far[0], last)
     far = move_z(total[2:].astype(BF), 1)
     last = move_z(add(total[1], far[1]).astype(BF), 2)
-    return list(add(total[0], far[0], last))
+    return add(total[0], far[0], last)
 
 
 def sum_over_dp(array):
@@ -296,18 +289,22 @@
     spread = by_chunk(inverse_spread_per_position[0])
     gain = layernorm_multiplier[0]
 
-    mine, totals = [], []
+    parts = gather_z(rows[: 2 * ROWS], z) + gather_z(rows[2 * ROWS :], z)
+    mine, keeps, others = [], [], []
     for k in range(CHUNKS):
-        gathered = gather_rows(k, rows[ROWS * k : ROWS * (k + 1)], z)
-        keep, send, own_rows = hidden_product(k, pos, *gathered, contraction_factor[0])
-        block = (reduce_hidden(k, keep, send) * slope[k]).astype(BF)
+        keep, send, own_rows = hidden_product(k, pos, *gather_ring(k, parts[k], "x"), contraction_factor[0])
+        mine.append(own_rows.reshape(32, -1))
+        keeps.append(keep)
+        others.append(move_core(send))
+    others = lax.optimization_barrier(others)
+    scaled = []
+    for k in range(CHUNKS):
+        block = (reduce_hidden(k, keeps[k], others[k]) * slope[k]).astype(BF)
         near_pair, wide_pair = gather_ring(k, block, "y")
         same = jnp.concatenate([near_pair, wide_pair])
         pairs = (same, move_core(same))
         keep, send = feature_product(k, pos, pairs, expansion_factor[0])
-        mine.append(own_rows.reshape(32, -1))
-        totals.append(reduce_x(k, keep, send))
-    scaled = [gain * total for total in reduce_z(totals[:1]) + reduce_z(totals[1:])]
+        scaled.append(gain * reduce_features(k, keep, send))
     scaled = jnp.stack(scaled)
     upstream = jnp.stack(mine)
     sums = sum_over_dp(jnp.stack([jnp.sum(scaled, axis=2), jnp.sum(scaled * entry, axis=2)]))

time: 208 us -> 203 us (0.976)
  waiting for transfers between devices: 74 us -> 94.5 us
  starting transfers between devices: 84.9 us -> 68.9 us
  other arithmetic: 11.2 us -> 4.84 us
  Pallas kernels: 30.8 us -> 28.2 us
    ppermute x8, starting transfers between devices: 40.2 us -> 31.9 us  [move_core(): return lax.ppermute(array, 'core', [(0, 1), (1, 0)])]
    ppermute x3 -> x2, waiting for transfers between devices: 0.01 us -> 7.91 us  [move_mirror(): return lax.ppermute(array, ('section', 'z'), [(i, 7 - i) for i in range(8)])]
    ppermute x12, starting transfers between devices: 12.2 us -> 5.35 us  [move_ring(): lax.ppermute(array, ('y', 'core'), [(2 * i + c, 2 * j + d) for c, i, d, j...]
    ppermute x12, waiting for transfers between devices: 28.2 us -> 34.8 us  [move_ring(): lax.ppermute(array, ('y', 'core'), [(2 * i + c, 2 * j + d) for c, i, d, j...]
    ppermute x10, waiting for transfers between devices: 14.9 us -> 21.1 us  [move_z(): return lax.ppermute(array, 'z', [(z, z ^ flip) for z in range(4)])]
    ppermute x10, starting transfers between devices: 11.3 us -> 6.34 us  [move_z(): return lax.ppermute(array, 'z', [(z, z ^ flip) for z in range(4)])]
    ppermute x12, starting transfers between devices: 11.2 us -> 14.9 us  [move_ring(): lax.ppermute(array, ('core', axis), [(4 * c + i, 4 * d + j) for c, i, d,...]
    convert_element_type x8 -> x9, other arithmetic: 3.64 us -> 0.75 us  [the longest x3 0.5 us: per_device(): block = (reduce_hidden(k, keeps[k], others[k]) * slope[k]).astype(BF)]
  transfers between devices with their start and end apart: 50 -> 49, of which waited for: 27 -> 32; matrix products, arithmetic and copies ran while one was open for 6% -> 2% of each run, Pallas kernels for 15% -> 14%
where the time goes in v3:
time: 203 us; the launch traced here: 202 us
  waiting for transfers between devices  94.5 us (47%)
  starting transfers between devices  68.9 us (34%)
  Pallas kernels  28.2 us (14%)
  local copies, waits for them, and re-layouts  5.47 us (3%)
  other arithmetic  4.84 us (2%)
    ppermute x12, waiting for transfers between devices, move_ring(): lax.ppermute(array, ('y', 'core'), [(2 * i + c, 2 * j + d) for c, i, d, j...  34.8 us
    ppermute x8, starting transfers between devices, move_core(): return lax.ppermute(array, 'core', [(0, 1), (1, 0)])  31.9 us
    ppermute x12, waiting for transfers between devices, move_ring(): lax.ppermute(array, ('core', axis), [(4 * c + i, 4 * d + j) for c, i, d,...  22.3 us
    ppermute x10, waiting for transfers between devices, move_z(): return lax.ppermute(array, 'z', [(z, z ^ flip) for z in range(4)])  21.1 us
    ppermute x12, starting transfers between devices, move_ring(): lax.ppermute(array, ('core', axis), [(4 * c + i, 4 * d + j) for c, i, d,...  14.9 us
    pallas_call x3, Pallas kernels, hidden_product(): pl.pallas_call(functools.partial(hidden_kernel, chunk), grid=(width // ti...  14.6 us
    pallas_call x3, Pallas kernels, feature_product(): pl.pallas_call(functools.partial(feature_kernel, chunk), grid=(width // t...  12.2 us
    ppermute x2, waiting for transfers between devices, move_mirror(): return lax.ppermute(array, ('section', 'z'), [(i, 7 - i) for i in range(8)])  7.91 us
  transfers between devices with their start and end apart: 49, of which 32 were waited for; matrix products, arithmetic and copies ran while one was open for 2% of the time, Pallas kernels for 14%

profile of v3, /device:TPU:1, one launch (start us, length us, event | category | flops | bytes accessed | tf_op | source)
XLA Modules:
  0.0 202.5 jit_solution(10245786897656726430)
XLA Ops:
  1.0 3.3 %collective-permute-start = (bf16[4,12,1024]{2,1,0:T(8,128)(2,1)S(1)}, bf16[4,12,1024]{2,1,0:T(8,128)(2,1)S(1)}, u32[]{:S(2)}, u32[]{:S(2)}) collective-permute-start(bf16[4,12,1024]{2,1,0:T(8,128)(2,1)S(1)} %broadcast_select_fusion), channel_id=1, source_target_pairs={{0,16},{16,0},{1,17},{17,1},{2,18},{18,2},{3,19},{19,3},{4,20},{20... | collective-permute-start | bytes 294920 | tf_op jit(solution)/shard_map/ppermute | solution.py:45
  11.8 5.1 %collective-permute-start.4 = (bf16[8,8,1024]{2,0,1:T(8,128)(2,1)S(1)}, bf16[8,8,1024]{2,0,1:T(8,128)(2,1)S(1)}, u32[]{:S(2)}, u32[]{:S(2)}) collective-permute-start(bf16[8,8,1024]{2,0,1:T(8,128)(2,1)S(1)} %slice.307), channel_id=1, source_target_pairs={{0,140},{4,136},{8,132},{12,128},{128,12},{132,8},{136,4},{140,0},... | collective-permute-start | bytes 393224 | tf_op jit(solution)/shard_map/ppermute | solution.py:41
  17.0 7.9 %collective-permute-done.11 = bf16[4,8,1024]{2,0,1:T(4,128)(2,1)S(1)} collective-permute-done((bf16[4,8,1024]{2,0,1:T(4,128)(2,1)S(1)}, bf16[4,8,1024]{2,0,1:T(4,128)(2,1)S(1)}, u32[]{:S(2)}, u32[]{:S(2)}) %collective-permute-start.11) | collective-permute-done | bytes 65568 | tf_op jit(solution)/shard_map/ppermute | solution.py:41
  29.5 4.9 %collective-permute-done.5 = bf16[8,8,1024]{2,0,1:T(8,128)(2,1)S(1)} collective-permute-done((bf16[8,8,1024]{2,0,1:T(8,128)(2,1)S(1)}, bf16[8,8,1024]{2,0,1:T(8,128)(2,1)S(1)}, u32[]{:S(2)}, u32[]{:S(2)}) %collective-permute-start.5) | collective-permute-done | bytes 131104 | tf_op jit(solution)/shard_map/ppermute | solution.py:37
  37.5 4.5 %collective-permute-done.6 = bf16[2,8,8,1024]{3,1,2,0:T(8,128)(2,1)S(1)} collective-permute-done((bf16[2,8,8,1024]{3,1,2,0:T(8,128)(2,1)S(1)}, bf16[2,8,8,1024]{3,1,2,0:T(8,128)(2,1)S(1)}, u32[]{:S(2)}, u32[]{:S(2)}) %collective-permute-start.6) | collective-permute-done | bytes 262176 | tf_op jit(solution)/shard_map/ppermute | solution.py:37
  46.8 3.5 %collective-permute-done.9 = bf16[8,16,1024]{2,1,0:T(8,128)(2,1)S(1)} collective-permute-done((bf16[8,16,1024]{2,1,0:T(8,128)(2,1)S(1)}, bf16[8,16,1024]{2,1,0:T(8,128)(2,1)S(1)}, u32[]{:S(2)}, u32[]{:S(2)}) %collective-permute-start.9) | collective-permute-done | bytes 262176 | tf_op jit(solution)/shard_map/ppermute | solution.py:29
  58.1 4.9 %shard_map.75 = (bf16[4,64,2048]{2,1,0:T(8,128)(2,1)S(1)}, bf16[4,64,2048]{2,1,0:T(8,128)(2,1)S(1)}, f32[4,8,1024]{2,1,0:T(8,128)S(1)}) custom-call(s32[4]{0:T(128)S(1)} %pad_add_fusion.pos, bf16[2,8,16,1024]{3,2,1,0:T(8,128)(2,1)S(1)} %pad_maximum_fusion.5.near_pair, bf16[2,8,16,1024]{3,2,1,0:T(8,128)(2,1)S(1)} %collective-permute-done.15.wide_pair, ...), custom_call_target="tpu_custom_call" | custom-call | flops 2147483648 | bytes 7340032 | tf_op jit(solution)/shard_map/pallas_call | solution.py:138
  63.0 10.2 %collective-permute-start.18 = (bf16[4,64,2048]{2,1,0:T(8,128)(2,1)S(1)}, bf16[4,64,2048]{2,1,0:T(8,128)(2,1)S(1)}, u32[]{:S(2)}, u32[]{:S(2)}) collective-permute-start(bf16[4,64,2048]{2,1,0:T(8,128)(2,1)S(1)} %get-tuple-element.32), channel_id=1, source_target_pairs={{0,16},{16,0},{1,17},{17,1},{2,18},{18,2},{3,19},{19,3},{4,20},{20... | collective-permute-start | bytes 3145736 | tf_op jit(solution)/shard_map/ppermute | solution.py:45
  73.2 4.9 %shard_map.74 = (bf16[4,64,2048]{2,1,0:T(8,128)(2,1)S(1)}, bf16[4,64,2048]{2,1,0:T(8,128)(2,1)S(1)}, f32[4,8,1024]{2,1,0:T(8,128)S(1)}) custom-call(s32[4]{0:T(128)S(1)} %pad_add_fusion.pos, bf16[2,8,16,1024]{3,2,1,0:T(8,128)(2,1)S(1)} %pad_maximum_fusion.4.near_pair, bf16[2,8,16,1024]{3,2,1,0:T(8,128)(2,1)S(1)} %collective-permute-done.10.wide_pair, ...), custom_call_target="tpu_custom_call" | custom-call | flops 2147483648 | bytes 7340032 | tf_op jit(solution)/shard_map/pallas_call | solution.py:138
  78.3 4.9 %shard_map.73 = (bf16[4,64,2048]{2,1,0:T(8,128)(2,1)S(1)}, bf16[4,64,2048]{2,1,0:T(8,128)(2,1)S(1)}, f32[4,8,1024]{2,1,0:T(8,128)S(1)}) custom-call(s32[4]{0:T(128)S(1)} %pad_add_fusion.pos, bf16[2,8,16,1024]{3,2,1,0:T(8,128)(2,1)S(1)} %pad_maximum_fusion.3.near_pair, bf16[2,8,16,1024]{3,2,1,0:T(8,128)(2,1)S(1)} %collective-permute-done.8.wide_pair, ...), custom_call_target="tpu_custom_call" | custom-call | flops 2147483648 | bytes 7340032 | tf_op jit(solution)/shard_map/pallas_call | solution.py:138
  88.2 10.9 %collective-permute-done.19 = bf16[2,64,2048]{2,1,0:T(8,128)(2,1)S(1)} collective-permute-done((bf16[2,64,2048]{2,1,0:T(8,128)(2,1)S(1)}, bf16[2,64,2048]{2,1,0:T(8,128)(2,1)S(1)}, u32[]{:S(2)}, u32[]{:S(2)}) %collective-permute-start.19) | collective-permute-done | bytes 524320 | tf_op jit(solution)/shard_map/ppermute | solution.py:28
  102.1 4.0 %collective-permute-done.37 = bf16[2,64,2048]{2,1,0:T(8,128)(2,1)S(1)} collective-permute-done((bf16[2,64,2048]{2,1,0:T(8,128)(2,1)S(1)}, bf16[2,64,2048]{2,1,0:T(8,128)(2,1)S(1)}, u32[]{:S(2)}, u32[]{:S(2)}) %collective-permute-start.37) | collective-permute-done | bytes 524320 | tf_op jit(solution)/shard_map/ppermute | solution.py:28
  111.7 6.5 %collective-permute-done.21 = bf16[64,2048]{1,0:T(8,128)(2,1)S(1)} collective-permute-done((bf16[64,2048]{1,0:T(8,128)(2,1)S(1)}, bf16[64,2048]{1,0:T(8,128)(2,1)S(1)}, u32[]{:S(2)}, u32[]{:S(2)}) %collective-permute-start.21) | collective-permute-done | bytes 262176 | tf_op jit(solution)/shard_map/ppermute | solution.py:28
  121.4 4.3 %collective-permute-done.39 = bf16[64,2048]{1,0:T(8,128)(2,1)S(1)} collective-permute-done((bf16[64,2048]{1,0:T(8,128)(2,1)S(1)}, bf16[64,2048]{1,0:T(8,128)(2,1)S(1)}, u32[]{:S(2)}, u32[]{:S(2)}) %collective-permute-start.39) | collective-permute-done | bytes 262176 | tf_op jit(solution)/shard_map/ppermute | solution.py:28
  127.7 10.2 %collective-permute-start.23 = (bf16[4,64,2048]{2,1,0:T(8,128)(2,1)S(1)}, bf16[4,64,2048]{2,1,0:T(8,128)(2,1)S(1)}, u32[]{:S(2)}, u32[]{:S(2)}) collective-permute-start(bf16[4,64,2048]{2,1,0:T(8,128)(2,1)S(1)} %pad_maximum_fusion.same), channel_id=1, source_target_pairs={{0,16},{16,0},{1,17},{17,1},{2,18},{18,2},{3,19},{19,3},{4,20},{20... | collective-permute-start | bytes 3145736 | tf_op jit(solution)/shard_map/ppermute | solution.py:45
  138.0 4.9 %collective-permute-start.32 = (bf16[4,64,2048]{2,1,0:T(8,128)(2,1)S(1)}, bf16[4,64,2048]{2,1,0:T(8,128)(2,1)S(1)}, u32[]{:S(2)}, u32[]{:S(2)}) collective-permute-start(bf16[4,64,2048]{2,1,0:T(8,128)(2,1)S(1)} %pad_maximum_fusion.1.same), channel_id=1, source_target_pairs={{0,16},{16,0},{1,17},{17,1},{2,18},{18,2},{3,19},{19,3},{4,20},{20... | collective-permute-start | bytes 3145736 | tf_op jit(solution)/shard_map/ppermute | solution.py:45
  144.7 4.0 %shard_map.77 = (bf16[2,4,32,1024]{3,2,1,0:T(8,128)(2,1)S(1)}, bf16[2,4,32,1024]{3,2,1,0:T(8,128)(2,1)S(1)}) custom-call(s32[4]{0:T(128)S(1)} %pad_add_fusion.pos, bf16[4,64,2048]{2,1,0:T(8,128)(2,1)S(1)} %pad_maximum_fusion.same, bf16[4,64,2048]{2,1,0:T(8,128)(2,1)S(1)} %collective-permute-done.23.other, bf16[1024,2048]{1,0:T(8,128)(2,1)S(1)} %bitcast.210), custom_call_target="tpu_custom_call" | custom-call | flops 2147483648 | bytes 7340032 | tf_op jit(solution)/shard_map/pallas_call | solution.py:186
  149.1 4.1 %shard_map.78 = (bf16[2,4,32,1024]{3,2,1,0:T(8,128)(2,1)S(1)}, bf16[2,4,32,1024]{3,2,1,0:T(8,128)(2,1)S(1)}) custom-call(s32[4]{0:T(128)S(1)} %pad_add_fusion.pos, bf16[4,64,2048]{2,1,0:T(8,128)(2,1)S(1)} %pad_maximum_fusion.1.same, bf16[4,64,2048]{2,1,0:T(8,128)(2,1)S(1)} %collective-permute-done.32.other, bf16[1024,2048]{1,0:T(8,128)(2,1)S(1)} %bitcast.211), custom_call_target="tpu_custom_call" | custom-call | flops 2147483648 | bytes 7340032 | tf_op jit(solution)/shard_map/pallas_call | solution.py:186
  155.9 4.0 %shard_map.79 = (bf16[2,4,32,1024]{3,2,1,0:T(8,128)(2,1)S(1)}, bf16[2,4,32,1024]{3,2,1,0:T(8,128)(2,1)S(1)}) custom-call(s32[4]{0:T(128)S(1)} %pad_add_fusion.pos, bf16[4,64,2048]{2,1,0:T(8,128)(2,1)S(1)} %pad_maximum_fusion.2.same, bf16[4,64,2048]{2,1,0:T(8,128)(2,1)S(1)} %collective-permute-done.41.other, bf16[1024,2048]{1,0:T(8,128)(2,1)S(1)} %bitcast.212), custom_call_target="tpu_custom_call" | custom-call | flops 2147483648 | bytes 7340032 | tf_op jit(solution)/shard_map/pallas_call | solution.py:186
  161.7 4.8 %collective-permute-done.33 = bf16[2,4,32,1024]{3,2,1,0:T(8,128)(2,1)S(1)} collective-permute-done((bf16[2,4,32,1024]{3,2,1,0:T(8,128)(2,1)S(1)}, bf16[2,4,32,1024]{3,2,1,0:T(8,128)(2,1)S(1)}, u32[]{:S(2)}, u32[]{:S(2)}) %collective-permute-start.33) | collective-permute-done | bytes 524320 | tf_op jit(solution)/shard_map/ppermute | solution.py:29
  166.6 6.8 %collective-permute-done.42 = bf16[2,4,32,1024]{3,2,1,0:T(8,128)(2,1)S(1)} collective-permute-done((bf16[2,4,32,1024]{3,2,1,0:T(8,128)(2,1)S(1)}, bf16[2,4,32,1024]{3,2,1,0:T(8,128)(2,1)S(1)}, u32[]{:S(2)}, u32[]{:S(2)}) %collective-permute-start.42) | collective-permute-done | bytes 524320 | tf_op jit(solution)/shard_map/ppermute | solution.py:29
  176.7 3.3 %collective-permute-done.43 = bf16[4,32,1024]{2,1,0:T(8,128)(2,1)S(1)} collective-permute-done((bf16[4,32,1024]{2,1,0:T(8,128)(2,1)S(1)}, bf16[4,32,1024]{2,1,0:T(8,128)(2,1)S(1)}, u32[]{:S(2)}, u32[]{:S(2)}) %collective-permute-start.43) | collective-permute-done | bytes 262176 | tf_op jit(solution)/shard_map/ppermute | solution.py:29
  183.4 3.2 %collective-permute-done.44 = bf16[2,32,1024]{2,1,0:T(8,128)(2,1)S(1)} collective-permute-done((bf16[2,32,1024]{2,1,0:T(8,128)(2,1)S(1)}, bf16[2,32,1024]{2,1,0:T(8,128)(2,1)S(1)}, u32[]{:S(2)}, u32[]{:S(2)}) %collective-permute-start.44) | collective-permute-done | bytes 131104 | tf_op jit(solution)/shard_map/ppermute | solution.py:37
  186.9 4.0 %collective-permute-done.36 = bf16[32,1024]{1,0:T(8,128)(2,1)S(1)} collective-permute-done((bf16[32,1024]{1,0:T(8,128)(2,1)S(1)}, bf16[32,1024]{1,0:T(8,128)(2,1)S(1)}, u32[]{:S(2)}, u32[]{:S(2)}) %collective-permute-start.36) | collective-permute-done | bytes 65568 | tf_op jit(solution)/shard_map/ppermute | solution.py:37
  (172 shorter events, 72.9 us)
Async XLA Ops:
  11.8 13.5 %collective-permute-start.4 = (bf16[8,8,1024]{2,0,1:T(8,128)(2,1)S(1)}, bf16[8,8,1024]{2,0,1:T(8,128)(2,1)S(1)}, u32[]{:S(2)}, u32[]{:S(2)}) collective-permute-start(bf16[8,8,1024]{2,0,1:T(8,128)(2,1)S(1)} %slice.307), channel_id=1, source_target_pairs={{0,140},{4,136},{8,132},{12,128},{128,12},{132,8},{136,4},{140,0},... | collective-permute-start | bytes 393224 | tf_op jit(solution)/shard_map/ppermute | solution.py:41
  25.3 9.1 %collective-permute-start.5 = (bf16[8,8,1024]{2,0,1:T(8,128)(2,1)S(1)}, bf16[8,8,1024]{2,0,1:T(8,128)(2,1)S(1)}, u32[]{:S(2)}, u32[]{:S(2)}) collective-permute-start(bf16[8,8,1024]{2,0,1:T(8,128)(2,1)S(1)} %collective-permute-done.4), channel_id=1, source_target_pairs={{0,8},{4,12},{8,0},{12,4},{1,9},{5,13},{9,1},{13,5},{2,10},{6,14},... | collective-permute-start | bytes 393224 | tf_op jit(solution)/shard_map/ppermute | solution.py:37
  43.7 12.2 %collective-permute-start.15 = (bf16[2,8,16,1024]{3,2,1,0:T(8,128)(2,1)S(1)}, bf16[2,8,16,1024]{3,2,1,0:T(8,128)(2,1)S(1)}, u32[]{:S(2)}, u32[]{:S(2)}) collective-permute-start(bf16[2,8,16,1024]{3,2,1,0:T(8,128)(2,1)S(1)} %pad_maximum_fusion.5.near_pair), channel_id=1, source_target_pairs={{0,3},{1,2},{2,1},{3,0},{16,17},{17,16},{18,19},{19,18},{4,7},{5,6... | collective-permute-start | bytes 1572872 | tf_op jit(solution)/shard_map/ppermute | solution.py:29
  50.4 22.8 %collective-permute-start.10 = (bf16[2,8,16,1024]{3,2,1,0:T(8,128)(2,1)S(1)}, bf16[2,8,16,1024]{3,2,1,0:T(8,128)(2,1)S(1)}, u32[]{:S(2)}, u32[]{:S(2)}) collective-permute-start(bf16[2,8,16,1024]{3,2,1,0:T(8,128)(2,1)S(1)} %pad_maximum_fusion.4.near_pair), channel_id=1, source_target_pairs={{0,1},{1,0},{2,3},{3,2},{16,19},{17,18},{18,17},{19,16},{4,5},{5,4... | collective-permute-start | bytes 1572872 | tf_op jit(solution)/shard_map/ppermute | solution.py:29
  53.0 25.3 %collective-permute-start.8 = (bf16[2,8,16,1024]{3,2,1,0:T(8,128)(2,1)S(1)}, bf16[2,8,16,1024]{3,2,1,0:T(8,128)(2,1)S(1)}, u32[]{:S(2)}, u32[]{:S(2)}) collective-permute-start(bf16[2,8,16,1024]{3,2,1,0:T(8,128)(2,1)S(1)} %pad_maximum_fusion.3.near_pair), channel_id=1, source_target_pairs={{0,3},{1,2},{2,1},{3,0},{16,17},{17,16},{18,19},{19,18},{4,7},{5,6... | collective-permute-start | bytes 1572872 | tf_op jit(solution)/shard_map/ppermute | solution.py:29
  63.0 22.2 %collective-permute-start.18 = (bf16[4,64,2048]{2,1,0:T(8,128)(2,1)S(1)}, bf16[4,64,2048]{2,1,0:T(8,128)(2,1)S(1)}, u32[]{:S(2)}, u32[]{:S(2)}) collective-permute-start(bf16[4,64,2048]{2,1,0:T(8,128)(2,1)S(1)} %get-tuple-element.32), channel_id=1, source_target_pairs={{0,16},{16,0},{1,17},{17,1},{2,18},{18,2},{3,19},{19,3},{4,20},{20... | collective-permute-start | bytes 3145736 | tf_op jit(solution)/shard_map/ppermute | solution.py:45
  86.2 12.9 %collective-permute-start.19 = (bf16[2,64,2048]{2,1,0:T(8,128)(2,1)S(1)}, bf16[2,64,2048]{2,1,0:T(8,128)(2,1)S(1)}, u32[]{:S(2)}, u32[]{:S(2)}) collective-permute-start(bf16[2,64,2048]{2,1,0:T(8,128)(2,1)S(1)} %add_convert_fusion.2), channel_id=1, source_target_pairs={{0,96},{32,64},{64,32},{96,0},{16,48},{48,16},{80,112},{112,80},{1... | collective-permute-start | bytes 1572872 | tf_op jit(solution)/shard_map/ppermute | solution.py:28
  86.4 14.7 %collective-permute-start.28 = (bf16[2,64,2048]{2,1,0:T(8,128)(2,1)S(1)}, bf16[2,64,2048]{2,1,0:T(8,128)(2,1)S(1)}, u32[]{:S(2)}, u32[]{:S(2)}) collective-permute-start(bf16[2,64,2048]{2,1,0:T(8,128)(2,1)S(1)} %add_convert_fusion.1), channel_id=1, source_target_pairs={{0,32},{32,0},{64,96},{96,64},{16,112},{48,80},{80,48},{112,16},{1... | collective-permute-start | bytes 1572872 | tf_op jit(solution)/shard_map/ppermute | solution.py:28
  87.2 19.0 %collective-permute-start.37 = (bf16[2,64,2048]{2,1,0:T(8,128)(2,1)S(1)}, bf16[2,64,2048]{2,1,0:T(8,128)(2,1)S(1)}, u32[]{:S(2)}, u32[]{:S(2)}) collective-permute-start(bf16[2,64,2048]{2,1,0:T(8,128)(2,1)S(1)} %add_convert_fusion), channel_id=1, source_target_pairs={{0,96},{32,64},{64,32},{96,0},{16,48},{48,16},{80,112},{112,80},{1... | collective-permute-start | bytes 1572872 | tf_op jit(solution)/shard_map/ppermute | solution.py:28
  99.1 9.7 %collective-permute-start.20 = (bf16[64,2048]{1,0:T(8,128)(2,1)S(1)}, bf16[64,2048]{1,0:T(8,128)(2,1)S(1)}, u32[]{:S(2)}, u32[]{:S(2)}) collective-permute-start(bf16[64,2048]{1,0:T(8,128)(2,1)S(1)} %fusion.11), channel_id=1, source_target_pairs={{0,32},{32,0},{64,96},{96,64},{16,112},{48,80},{80,48},{112,16},{1... | collective-permute-start | bytes 786440 | tf_op jit(solution)/shard_map/ppermute | solution.py:28
  101.2 10.2 %collective-permute-start.29 = (bf16[64,2048]{1,0:T(8,128)(2,1)S(1)}, bf16[64,2048]{1,0:T(8,128)(2,1)S(1)}, u32[]{:S(2)}, u32[]{:S(2)}) collective-permute-start(bf16[64,2048]{1,0:T(8,128)(2,1)S(1)} %fusion.13), channel_id=1, source_target_pairs={{0,96},{32,64},{64,32},{96,0},{16,48},{48,16},{80,112},{112,80},{1... | collective-permute-start | bytes 786440 | tf_op jit(solution)/shard_map/ppermute | solution.py:28
  106.3 12.1 %collective-permute-start.38 = (bf16[64,2048]{1,0:T(8,128)(2,1)S(1)}, bf16[64,2048]{1,0:T(8,128)(2,1)S(1)}, u32[]{:S(2)}, u32[]{:S(2)}) collective-permute-start(bf16[64,2048]{1,0:T(8,128)(2,1)S(1)} %fusion.15), channel_id=1, source_target_pairs={{0,32},{32,0},{64,96},{96,64},{16,112},{48,80},{80,48},{112,16},{1... | collective-permute-start | bytes 786440 | tf_op jit(solution)/shard_map/ppermute | solution.py:28
  109.0 9.2 %collective-permute-start.21 = (bf16[64,2048]{1,0:T(8,128)(2,1)S(1)}, bf16[64,2048]{1,0:T(8,128)(2,1)S(1)}, u32[]{:S(2)}, u32[]{:S(2)}) collective-permute-start(bf16[64,2048]{1,0:T(8,128)(2,1)S(1)} %fusion.5), channel_id=1, source_target_pairs={{0,32},{32,0},{64,96},{96,64},{16,112},{48,80},{80,48},{112,16},{1... | collective-permute-start | bytes 786440 | tf_op jit(solution)/shard_map/ppermute | solution.py:28
  118.3 9.3 %collective-permute-start.22 = (bf16[2,64,2048]{2,1,0:T(8,128)(2,1)S(1)}, bf16[2,64,2048]{2,1,0:T(8,128)(2,1)S(1)}, u32[]{:S(2)}, u32[]{:S(2)}) collective-permute-start(bf16[2,64,2048]{2,1,0:T(8,128)(2,1)S(1)} %pad_maximum_fusion.6), channel_id=1, source_target_pairs={{0,96},{32,64},{64,32},{96,0},{16,48},{48,16},{80,112},{112,80},{1... | collective-permute-start | bytes 1572872 | tf_op jit(solution)/shard_map/ppermute | solution.py:28
  120.0 17.9 %collective-permute-start.31 = (bf16[2,64,2048]{2,1,0:T(8,128)(2,1)S(1)}, bf16[2,64,2048]{2,1,0:T(8,128)(2,1)S(1)}, u32[]{:S(2)}, u32[]{:S(2)}) collective-permute-start(bf16[2,64,2048]{2,1,0:T(8,128)(2,1)S(1)} %pad_maximum_fusion.7), channel_id=1, source_target_pairs={{0,32},{32,0},{64,96},{96,64},{16,112},{48,80},{80,48},{112,16},{1... | collective-permute-start | bytes 1572872 | tf_op jit(solution)/shard_map/ppermute | solution.py:28
  125.8 17.1 %collective-permute-start.40 = (bf16[2,64,2048]{2,1,0:T(8,128)(2,1)S(1)}, bf16[2,64,2048]{2,1,0:T(8,128)(2,1)S(1)}, u32[]{:S(2)}, u32[]{:S(2)}) collective-permute-start(bf16[2,64,2048]{2,1,0:T(8,128)(2,1)S(1)} %pad_maximum_fusion.8), channel_id=1, source_target_pairs={{0,96},{32,64},{64,32},{96,0},{16,48},{48,16},{80,112},{112,80},{1... | collective-permute-start | bytes 1572872 | tf_op jit(solution)/shard_map/ppermute | solution.py:28
  127.7 17.0 %collective-permute-start.23 = (bf16[4,64,2048]{2,1,0:T(8,128)(2,1)S(1)}, bf16[4,64,2048]{2,1,0:T(8,128)(2,1)S(1)}, u32[]{:S(2)}, u32[]{:S(2)}) collective-permute-start(bf16[4,64,2048]{2,1,0:T(8,128)(2,1)S(1)} %pad_maximum_fusion.same), channel_id=1, source_target_pairs={{0,16},{16,0},{1,17},{17,1},{2,18},{18,2},{3,19},{19,3},{4,20},{20... | collective-permute-start | bytes 3145736 | tf_op jit(solution)/shard_map/ppermute | solution.py:45
  138.0 11.1 %collective-permute-start.32 = (bf16[4,64,2048]{2,1,0:T(8,128)(2,1)S(1)}, bf16[4,64,2048]{2,1,0:T(8,128)(2,1)S(1)}, u32[]{:S(2)}, u32[]{:S(2)}) collective-permute-start(bf16[4,64,2048]{2,1,0:T(8,128)(2,1)S(1)} %pad_maximum_fusion.1.same), channel_id=1, source_target_pairs={{0,16},{16,0},{1,17},{17,1},{2,18},{18,2},{3,19},{19,3},{4,20},{20... | collective-permute-start | bytes 3145736 | tf_op jit(solution)/shard_map/ppermute | solution.py:45
  143.0 12.9 %collective-permute-start.41 = (bf16[4,64,2048]{2,1,0:T(8,128)(2,1)S(1)}, bf16[4,64,2048]{2,1,0:T(8,128)(2,1)S(1)}, u32[]{:S(2)}, u32[]{:S(2)}) collective-permute-start(bf16[4,64,2048]{2,1,0:T(8,128)(2,1)S(1)} %pad_maximum_fusion.2.same), channel_id=1, source_target_pairs={{0,16},{16,0},{1,17},{17,1},{2,18},{18,2},{3,19},{19,3},{4,20},{20... | collective-permute-start | bytes 3145736 | tf_op jit(solution)/shard_map/ppermute | solution.py:45
  148.8 12.1 %collective-permute-start.24 = (bf16[2,4,32,1024]{3,2,1,0:T(8,128)(2,1)S(1)}, bf16[2,4,32,1024]{3,2,1,0:T(8,128)(2,1)S(1)}, u32[]{:S(2)}, u32[]{:S(2)}) collective-permute-start(bf16[2,4,32,1024]{3,2,1,0:T(8,128)(2,1)S(1)} %get-tuple-element.36), channel_id=1, source_target_pairs={{0,3},{1,2},{2,1},{3,0},{16,17},{17,16},{18,19},{19,18},{4,7},{5,6... | collective-permute-start | bytes 1572872 | tf_op jit(solution)/shard_map/ppermute | solution.py:29
  153.2 13.3 %collective-permute-start.33 = (bf16[2,4,32,1024]{3,2,1,0:T(8,128)(2,1)S(1)}, bf16[2,4,32,1024]{3,2,1,0:T(8,128)(2,1)S(1)}, u32[]{:S(2)}, u32[]{:S(2)}) collective-permute-start(bf16[2,4,32,1024]{3,2,1,0:T(8,128)(2,1)S(1)} %get-tuple-element.41), channel_id=1, source_target_pairs={{0,1},{1,0},{2,3},{3,2},{16,19},{17,18},{18,17},{19,16},{4,5},{5,4... | collective-permute-start | bytes 1572872 | tf_op jit(solution)/shard_map/ppermute | solution.py:29
  160.0 13.4 %collective-permute-start.42 = (bf16[2,4,32,1024]{3,2,1,0:T(8,128)(2,1)S(1)}, bf16[2,4,32,1024]{3,2,1,0:T(8,128)(2,1)S(1)}, u32[]{:S(2)}, u32[]{:S(2)}) collective-permute-start(bf16[2,4,32,1024]{3,2,1,0:T(8,128)(2,1)S(1)} %get-tuple-element.46), channel_id=1, source_target_pairs={{0,3},{1,2},{2,1},{3,0},{16,17},{17,16},{18,19},{19,18},{4,7},{5,6... | collective-permute-start | bytes 1572872 | tf_op jit(solution)/shard_map/ppermute | solution.py:29
  160.9 13.3 %collective-permute-start.25 = (bf16[4,32,1024]{2,1,0:T(8,128)(2,1)S(1)}, bf16[4,32,1024]{2,1,0:T(8,128)(2,1)S(1)}, u32[]{:S(2)}, u32[]{:S(2)}) collective-permute-start(bf16[4,32,1024]{2,1,0:T(8,128)(2,1)S(1)} %fusion.12), channel_id=1, source_target_pairs={{0,1},{1,0},{2,3},{3,2},{16,19},{17,18},{18,17},{19,16},{4,5},{5,4... | collective-permute-start | bytes 786440 | tf_op jit(solution)/shard_map/ppermute | solution.py:29
  166.5 9.5 %collective-permute-start.34 = (bf16[4,32,1024]{2,1,0:T(8,128)(2,1)S(1)}, bf16[4,32,1024]{2,1,0:T(8,128)(2,1)S(1)}, u32[]{:S(2)}, u32[]{:S(2)}) collective-permute-start(bf16[4,32,1024]{2,1,0:T(8,128)(2,1)S(1)} %fusion.14), channel_id=1, source_target_pairs={{0,3},{1,2},{2,1},{3,0},{16,17},{17,16},{18,19},{19,18},{4,7},{5,6... | collective-permute-start | bytes 786440 | tf_op jit(solution)/shard_map/ppermute | solution.py:29
  (32 other events, 280.2 us)

commit v4 on v3

--- a/solution.py
+++ b/solution.py
@@ -290,9 +290,12 @@
     gain = layernorm_multiplier[0]
 
     parts = gather_z(rows[: 2 * ROWS], z) + gather_z(rows[2 * ROWS :], z)
+    moved = lax.optimization_barrier([move_ring(parts[k], "x", flips(k)[0]) for k in range(CHUNKS)])
     mine, keeps, others = [], [], []
     for k in range(CHUNKS):
-        keep, send, own_rows = hidden_product(k, pos, *gather_ring(k, parts[k], "x"), contraction_factor[0])
+        near_pair = jnp.stack([parts[k], moved[k]])
+        wide_pair = move_ring(near_pair, "x", flips(k)[1])
+        keep, send, own_rows = hidden_product(k, pos, near_pair, wide_pair, contraction_factor[0])
         mine.append(own_rows.reshape(32, -1))
         keeps.append(keep)
         others.append(move_core(send))

time: 203 us -> 205 us (level)
    ppermute x12, waiting for transfers between devices: 22.3 us -> 26.9 us  [move_ring(): lax.ppermute(array, ('core', axis), [(4 * c + i, 4 * d + j) for c, i, d,...]
    ppermute x10, starting transfers between devices: 6.34 us -> 8.94 us  [move_z(): return lax.ppermute(array, 'z', [(z, z ^ flip) for z in range(4)])]
    ppermute x10, waiting for transfers between devices: 21.1 us -> 18.6 us  [move_z(): return lax.ppermute(array, 'z', [(z, z ^ flip) for z in range(4)])]
    ppermute x8, starting transfers between devices: 31.9 us -> 29.5 us  [move_core(): return lax.ppermute(array, 'core', [(0, 1), (1, 0)])]
where the time goes in v4:
time: 205 us; the launch traced here: 204 us
  waiting for transfers between devices  96.3 us (47%)
  starting transfers between devices  68.5 us (33%)
  Pallas kernels  28.1 us (14%)
  local copies, waits for them, and re-layouts  5.47 us (3%)
  other arithmetic  4.84 us (2%)
    ppermute x12, waiting for transfers between devices, move_ring(): lax.ppermute(array, ('y', 'core'), [(2 * i + c, 2 * j + d) for c, i, d, j...  34.9 us
    ppermute x8, starting transfers between devices, move_core(): return lax.ppermute(array, 'core', [(0, 1), (1, 0)])  29.5 us
    ppermute x12, waiting for transfers between devices, move_ring(): lax.ppermute(array, ('core', axis), [(4 * c + i, 4 * d + j) for c, i, d,...  26.9 us
    ppermute x10, waiting for transfers between devices, move_z(): return lax.ppermute(array, 'z', [(z, z ^ flip) for z in range(4)])  18.6 us
    pallas_call x3, Pallas kernels, hidden_product(): pl.pallas_call(functools.partial(hidden_kernel, chunk), grid=(width // ti...  14.5 us
    ppermute x12, starting transfers between devices, move_ring(): lax.ppermute(array, ('core', axis), [(4 * c + i, 4 * d + j) for c, i, d,...  13.4 us
    pallas_call x3, Pallas kernels, feature_product(): pl.pallas_call(functools.partial(feature_kernel, chunk), grid=(width // t...  12.1 us
    ppermute x10, starting transfers between devices, move_z(): return lax.ppermute(array, 'z', [(z, z ^ flip) for z in range(4)])  8.94 us
  transfers between devices with their start and end apart: 49, of which 32 were waited for; matrix products, arithmetic and copies ran while one was open for 2% of the time, Pallas kernels for 14%

profile of v4, /device:TPU:1, one launch (start us, length us, event | category | flops | bytes accessed | tf_op | source)
XLA Modules:
  0.0 203.8 jit_solution(13793025397406683624)
XLA Ops:
  1.0 3.3 %collective-permute-start = (bf16[4,12,1024]{2,1,0:T(8,128)(2,1)S(1)}, bf16[4,12,1024]{2,1,0:T(8,128)(2,1)S(1)}, u32[]{:S(2)}, u32[]{:S(2)}) collective-permute-start(bf16[4,12,1024]{2,1,0:T(8,128)(2,1)S(1)} %broadcast_select_fusion), channel_id=1, source_target_pairs={{0,16},{16,0},{1,17},{17,1},{2,18},{18,2},{3,19},{19,3},{4,20},{20... | collective-permute-start | bytes 294920 | tf_op jit(solution)/shard_map/ppermute | solution.py:45
  11.8 5.1 %collective-permute-start.4 = (bf16[8,8,1024]{2,0,1:T(8,128)(2,1)S(1)}, bf16[8,8,1024]{2,0,1:T(8,128)(2,1)S(1)}, u32[]{:S(2)}, u32[]{:S(2)}) collective-permute-start(bf16[8,8,1024]{2,0,1:T(8,128)(2,1)S(1)} %slice.307), channel_id=1, source_target_pairs={{0,140},{4,136},{8,132},{12,128},{128,12},{132,8},{136,4},{140,0},... | collective-permute-start | bytes 393224 | tf_op jit(solution)/shard_map/ppermute | solution.py:41
  17.0 7.9 %collective-permute-done.9 = bf16[4,8,1024]{2,0,1:T(4,128)(2,1)S(1)} collective-permute-done((bf16[4,8,1024]{2,0,1:T(4,128)(2,1)S(1)}, bf16[4,8,1024]{2,0,1:T(4,128)(2,1)S(1)}, u32[]{:S(2)}, u32[]{:S(2)}) %collective-permute-start.9) | collective-permute-done | bytes 65568 | tf_op jit(solution)/shard_map/ppermute | solution.py:41
  29.5 4.9 %collective-permute-done.5 = bf16[8,8,1024]{2,0,1:T(8,128)(2,1)S(1)} collective-permute-done((bf16[8,8,1024]{2,0,1:T(8,128)(2,1)S(1)}, bf16[8,8,1024]{2,0,1:T(8,128)(2,1)S(1)}, u32[]{:S(2)}, u32[]{:S(2)}) %collective-permute-start.5) | collective-permute-done | bytes 131104 | tf_op jit(solution)/shard_map/ppermute | solution.py:37
  37.5 4.5 %collective-permute-done.6 = bf16[2,8,8,1024]{3,1,2,0:T(8,128)(2,1)S(1)} collective-permute-done((bf16[2,8,8,1024]{3,1,2,0:T(8,128)(2,1)S(1)}, bf16[2,8,8,1024]{3,1,2,0:T(8,128)(2,1)S(1)}, u32[]{:S(2)}, u32[]{:S(2)}) %collective-permute-start.6) | collective-permute-done | bytes 262176 | tf_op jit(solution)/shard_map/ppermute | solution.py:37
  45.8 4.6 %collective-permute-done.8 = bf16[8,16,1024]{2,1,0:T(8,128)(2,1)S(1)} collective-permute-done((bf16[8,16,1024]{2,1,0:T(8,128)(2,1)S(1)}, bf16[8,16,1024]{2,1,0:T(8,128)(2,1)S(1)}, u32[]{:S(2)}, u32[]{:S(2)}) %collective-permute-start.8) | collective-permute-done | bytes 262176 | tf_op jit(solution)/shard_map/ppermute | solution.py:29
  54.6 6.2 %collective-permute-done.15.wide_pair = bf16[2,8,16,1024]{3,2,1,0:T(8,128)(2,1)S(1)} collective-permute-done((bf16[2,8,16,1024]{3,2,1,0:T(8,128)(2,1)S(1)}, bf16[2,8,16,1024]{3,2,1,0:T(8,128)(2,1)S(1)}, u32[]{:S(2)}, u32[]{:S(2)}) %collective-permute-start.15) | collective-permute-done | bytes 524320 | tf_op jit(solution)/shard_map/ppermute | solution.py:29
  62.9 4.9 %shard_map.75 = (bf16[4,64,2048]{2,1,0:T(8,128)(2,1)S(1)}, bf16[4,64,2048]{2,1,0:T(8,128)(2,1)S(1)}, f32[4,8,1024]{2,1,0:T(8,128)S(1)}) custom-call(s32[4]{0:T(128)S(1)} %pad_add_fusion.pos, bf16[2,8,16,1024]{3,2,1,0:T(8,128)(2,1)S(1)} %pad_maximum_fusion.5.near_pair, bf16[2,8,16,1024]{3,2,1,0:T(8,128)(2,1)S(1)} %collective-permute-done.15.wide_pair, ...), custom_call_target="tpu_custom_call" | custom-call | flops 2147483648 | bytes 7340032 | tf_op jit(solution)/shard_map/pallas_call | solution.py:138
  67.8 7.0 %collective-permute-start.18 = (bf16[4,64,2048]{2,1,0:T(8,128)(2,1)S(1)}, bf16[4,64,2048]{2,1,0:T(8,128)(2,1)S(1)}, u32[]{:S(2)}, u32[]{:S(2)}) collective-permute-start(bf16[4,64,2048]{2,1,0:T(8,128)(2,1)S(1)} %get-tuple-element.38), channel_id=1, source_target_pairs={{0,16},{16,0},{1,17},{17,1},{2,18},{18,2},{3,19},{19,3},{4,20},{20... | collective-permute-start | bytes 3145736 | tf_op jit(solution)/shard_map/ppermute | solution.py:45
  74.8 4.8 %shard_map.74 = (bf16[4,64,2048]{2,1,0:T(8,128)(2,1)S(1)}, bf16[4,64,2048]{2,1,0:T(8,128)(2,1)S(1)}, f32[4,8,1024]{2,1,0:T(8,128)S(1)}) custom-call(s32[4]{0:T(128)S(1)} %pad_add_fusion.pos, bf16[2,8,16,1024]{3,2,1,0:T(8,128)(2,1)S(1)} %pad_maximum_fusion.4.near_pair, bf16[2,8,16,1024]{3,2,1,0:T(8,128)(2,1)S(1)} %collective-permute-done.14.wide_pair, ...), custom_call_target="tpu_custom_call" | custom-call | flops 2147483648 | bytes 7340032 | tf_op jit(solution)/shard_map/pallas_call | solution.py:138
  80.0 4.8 %shard_map.73 = (bf16[4,64,2048]{2,1,0:T(8,128)(2,1)S(1)}, bf16[4,64,2048]{2,1,0:T(8,128)(2,1)S(1)}, f32[4,8,1024]{2,1,0:T(8,128)S(1)}) custom-call(s32[4]{0:T(128)S(1)} %pad_add_fusion.pos, bf16[2,8,16,1024]{3,2,1,0:T(8,128)(2,1)S(1)} %pad_maximum_fusion.3.near_pair, bf16[2,8,16,1024]{3,2,1,0:T(8,128)(2,1)S(1)} %collective-permute-done.13.wide_pair, ...), custom_call_target="tpu_custom_call" | custom-call | flops 2147483648 | bytes 7340032 | tf_op jit(solution)/shard_map/pallas_call | solution.py:138
  89.8 10.9 %collective-permute-done.19 = bf16[2,64,2048]{2,1,0:T(8,128)(2,1)S(1)} collective-permute-done((bf16[2,64,2048]{2,1,0:T(8,128)(2,1)S(1)}, bf16[2,64,2048]{2,1,0:T(8,128)(2,1)S(1)}, u32[]{:S(2)}, u32[]{:S(2)}) %collective-permute-start.19) | collective-permute-done | bytes 524320 | tf_op jit(solution)/shard_map/ppermute | solution.py:28
  103.7 4.0 %collective-permute-done.37 = bf16[2,64,2048]{2,1,0:T(8,128)(2,1)S(1)} collective-permute-done((bf16[2,64,2048]{2,1,0:T(8,128)(2,1)S(1)}, bf16[2,64,2048]{2,1,0:T(8,128)(2,1)S(1)}, u32[]{:S(2)}, u32[]{:S(2)}) %collective-permute-start.37) | collective-permute-done | bytes 524320 | tf_op jit(solution)/shard_map/ppermute | solution.py:28
  113.3 6.5 %collective-permute-done.21 = bf16[64,2048]{1,0:T(8,128)(2,1)S(1)} collective-permute-done((bf16[64,2048]{1,0:T(8,128)(2,1)S(1)}, bf16[64,2048]{1,0:T(8,128)(2,1)S(1)}, u32[]{:S(2)}, u32[]{:S(2)}) %collective-permute-start.21) | collective-permute-done | bytes 262176 | tf_op jit(solution)/shard_map/ppermute | solution.py:28
  123.1 4.3 %collective-permute-done.39 = bf16[64,2048]{1,0:T(8,128)(2,1)S(1)} collective-permute-done((bf16[64,2048]{1,0:T(8,128)(2,1)S(1)}, bf16[64,2048]{1,0:T(8,128)(2,1)S(1)}, u32[]{:S(2)}, u32[]{:S(2)}) %collective-permute-start.39) | collective-permute-done | bytes 262176 | tf_op jit(solution)/shard_map/ppermute | solution.py:28
  129.3 10.2 %collective-permute-start.23 = (bf16[4,64,2048]{2,1,0:T(8,128)(2,1)S(1)}, bf16[4,64,2048]{2,1,0:T(8,128)(2,1)S(1)}, u32[]{:S(2)}, u32[]{:S(2)}) collective-permute-start(bf16[4,64,2048]{2,1,0:T(8,128)(2,1)S(1)} %pad_maximum_fusion.same), channel_id=1, source_target_pairs={{0,16},{16,0},{1,17},{17,1},{2,18},{18,2},{3,19},{19,3},{4,20},{20... | collective-permute-start | bytes 3145736 | tf_op jit(solution)/shard_map/ppermute | solution.py:45
  139.6 4.7 %collective-permute-start.32 = (bf16[4,64,2048]{2,1,0:T(8,128)(2,1)S(1)}, bf16[4,64,2048]{2,1,0:T(8,128)(2,1)S(1)}, u32[]{:S(2)}, u32[]{:S(2)}) collective-permute-start(bf16[4,64,2048]{2,1,0:T(8,128)(2,1)S(1)} %pad_maximum_fusion.1.same), channel_id=1, source_target_pairs={{0,16},{16,0},{1,17},{17,1},{2,18},{18,2},{3,19},{19,3},{4,20},{20... | collective-permute-start | bytes 3145736 | tf_op jit(solution)/shard_map/ppermute | solution.py:45
  145.9 4.0 %shard_map.77 = (bf16[2,4,32,1024]{3,2,1,0:T(8,128)(2,1)S(1)}, bf16[2,4,32,1024]{3,2,1,0:T(8,128)(2,1)S(1)}) custom-call(s32[4]{0:T(128)S(1)} %pad_add_fusion.pos, bf16[4,64,2048]{2,1,0:T(8,128)(2,1)S(1)} %pad_maximum_fusion.same, bf16[4,64,2048]{2,1,0:T(8,128)(2,1)S(1)} %collective-permute-done.23.other, bf16[1024,2048]{1,0:T(8,128)(2,1)S(1)} %bitcast.210), custom_call_target="tpu_custom_call" | custom-call | flops 2147483648 | bytes 7340032 | tf_op jit(solution)/shard_map/pallas_call | solution.py:186
  150.3 4.0 %shard_map.78 = (bf16[2,4,32,1024]{3,2,1,0:T(8,128)(2,1)S(1)}, bf16[2,4,32,1024]{3,2,1,0:T(8,128)(2,1)S(1)}) custom-call(s32[4]{0:T(128)S(1)} %pad_add_fusion.pos, bf16[4,64,2048]{2,1,0:T(8,128)(2,1)S(1)} %pad_maximum_fusion.1.same, bf16[4,64,2048]{2,1,0:T(8,128)(2,1)S(1)} %collective-permute-done.32.other, bf16[1024,2048]{1,0:T(8,128)(2,1)S(1)} %bitcast.211), custom_call_target="tpu_custom_call" | custom-call | flops 2147483648 | bytes 7340032 | tf_op jit(solution)/shard_map/pallas_call | solution.py:186
  156.2 4.0 %shard_map.79 = (bf16[2,4,32,1024]{3,2,1,0:T(8,128)(2,1)S(1)}, bf16[2,4,32,1024]{3,2,1,0:T(8,128)(2,1)S(1)}) custom-call(s32[4]{0:T(128)S(1)} %pad_add_fusion.pos, bf16[4,64,2048]{2,1,0:T(8,128)(2,1)S(1)} %pad_maximum_fusion.2.same, bf16[4,64,2048]{2,1,0:T(8,128)(2,1)S(1)} %collective-permute-done.41.other, bf16[1024,2048]{1,0:T(8,128)(2,1)S(1)} %bitcast.212), custom_call_target="tpu_custom_call" | custom-call | flops 2147483648 | bytes 7340032 | tf_op jit(solution)/shard_map/pallas_call | solution.py:186
  162.3 4.4 %collective-permute-done.33 = bf16[2,4,32,1024]{3,2,1,0:T(8,128)(2,1)S(1)} collective-permute-done((bf16[2,4,32,1024]{3,2,1,0:T(8,128)(2,1)S(1)}, bf16[2,4,32,1024]{3,2,1,0:T(8,128)(2,1)S(1)}, u32[]{:S(2)}, u32[]{:S(2)}) %collective-permute-start.33) | collective-permute-done | bytes 524320 | tf_op jit(solution)/shard_map/ppermute | solution.py:29
  166.8 6.9 %collective-permute-done.42 = bf16[2,4,32,1024]{3,2,1,0:T(8,128)(2,1)S(1)} collective-permute-done((bf16[2,4,32,1024]{3,2,1,0:T(8,128)(2,1)S(1)}, bf16[2,4,32,1024]{3,2,1,0:T(8,128)(2,1)S(1)}, u32[]{:S(2)}, u32[]{:S(2)}) %collective-permute-start.42) | collective-permute-done | bytes 524320 | tf_op jit(solution)/shard_map/ppermute | solution.py:29
  186.2 4.6 %collective-permute-done.36 = bf16[32,1024]{1,0:T(8,128)(2,1)S(1)} collective-permute-done((bf16[32,1024]{1,0:T(8,128)(2,1)S(1)}, bf16[32,1024]{1,0:T(8,128)(2,1)S(1)}, u32[]{:S(2)}, u32[]{:S(2)}) %collective-permute-start.36) | collective-permute-done | bytes 65568 | tf_op jit(solution)/shard_map/ppermute | solution.py:37
  198.1 2.9 %collective-permute-start.48 = (f32[2,3,32]{2,1,0:T(4,128)S(1)}, f32[2,3,32]{2,1,0:T(4,128)S(1)}, u32[]{:S(2)}, u32[]{:S(2)}) collective-permute-start(f32[2,3,32]{2,1,0:T(4,128)S(1)} %fusion.53), channel_id=1, source_target_pairs={{0,96},{32,64},{64,32},{96,0},{1,97},{33,65},{65,33},{97,1},{2,98}... | collective-permute-start | bytes 2312 | tf_op jit(solution)/shard_map/ppermute | solution.py:33
  (172 shorter events, 73.6 us)
Async XLA Ops:
  11.8 13.5 %collective-permute-start.4 = (bf16[8,8,1024]{2,0,1:T(8,128)(2,1)S(1)}, bf16[8,8,1024]{2,0,1:T(8,128)(2,1)S(1)}, u32[]{:S(2)}, u32[]{:S(2)}) collective-permute-start(bf16[8,8,1024]{2,0,1:T(8,128)(2,1)S(1)} %slice.307), channel_id=1, source_target_pairs={{0,140},{4,136},{8,132},{12,128},{128,12},{132,8},{136,4},{140,0},... | collective-permute-start | bytes 393224 | tf_op jit(solution)/shard_map/ppermute | solution.py:41
  25.3 9.1 %collective-permute-start.5 = (bf16[8,8,1024]{2,0,1:T(8,128)(2,1)S(1)}, bf16[8,8,1024]{2,0,1:T(8,128)(2,1)S(1)}, u32[]{:S(2)}, u32[]{:S(2)}) collective-permute-start(bf16[8,8,1024]{2,0,1:T(8,128)(2,1)S(1)} %collective-permute-done.4), channel_id=1, source_target_pairs={{0,8},{4,12},{8,0},{12,4},{1,9},{5,13},{9,1},{13,5},{2,10},{6,14},... | collective-permute-start | bytes 393224 | tf_op jit(solution)/shard_map/ppermute | solution.py:37
  35.0 10.8 %collective-permute-start.12 = (bf16[8,16,1024]{2,1,0:T(8,128)(2,1)S(1)}, bf16[8,16,1024]{2,1,0:T(8,128)(2,1)S(1)}, u32[]{:S(2)}, u32[]{:S(2)}) collective-permute-start(bf16[8,16,1024]{2,1,0:T(8,128)(2,1)S(1)} %get-tuple-element.62), channel_id=1, source_target_pairs={{0,1},{1,0},{2,3},{3,2},{16,19},{17,18},{18,17},{19,16},{4,5},{5,4... | collective-permute-start | bytes 786440 | tf_op jit(solution)/shard_map/ppermute | solution.py:29
  52.0 22.8 %collective-permute-start.14 = (bf16[2,8,16,1024]{3,2,1,0:T(8,128)(2,1)S(1)}, bf16[2,8,16,1024]{3,2,1,0:T(8,128)(2,1)S(1)}, u32[]{:S(2)}, u32[]{:S(2)}) collective-permute-start(bf16[2,8,16,1024]{3,2,1,0:T(8,128)(2,1)S(1)} %pad_maximum_fusion.4.near_pair), channel_id=1, source_target_pairs={{0,1},{1,0},{2,3},{3,2},{16,19},{17,18},{18,17},{19,16},{4,5},{5,4... | collective-permute-start | bytes 1572872 | tf_op jit(solution)/shard_map/ppermute | solution.py:29
  54.1 25.9 %collective-permute-start.13 = (bf16[2,8,16,1024]{3,2,1,0:T(8,128)(2,1)S(1)}, bf16[2,8,16,1024]{3,2,1,0:T(8,128)(2,1)S(1)}, u32[]{:S(2)}, u32[]{:S(2)}) collective-permute-start(bf16[2,8,16,1024]{3,2,1,0:T(8,128)(2,1)S(1)} %pad_maximum_fusion.3.near_pair), channel_id=1, source_target_pairs={{0,3},{1,2},{2,1},{3,0},{16,17},{17,16},{18,19},{19,18},{4,7},{5,6... | collective-permute-start | bytes 1572872 | tf_op jit(solution)/shard_map/ppermute | solution.py:29
  67.8 19.0 %collective-permute-start.18 = (bf16[4,64,2048]{2,1,0:T(8,128)(2,1)S(1)}, bf16[4,64,2048]{2,1,0:T(8,128)(2,1)S(1)}, u32[]{:S(2)}, u32[]{:S(2)}) collective-permute-start(bf16[4,64,2048]{2,1,0:T(8,128)(2,1)S(1)} %get-tuple-element.38), channel_id=1, source_target_pairs={{0,16},{16,0},{1,17},{17,1},{2,18},{18,2},{3,19},{19,3},{4,20},{20... | collective-permute-start | bytes 3145736 | tf_op jit(solution)/shard_map/ppermute | solution.py:45
  87.8 13.0 %collective-permute-start.19 = (bf16[2,64,2048]{2,1,0:T(8,128)(2,1)S(1)}, bf16[2,64,2048]{2,1,0:T(8,128)(2,1)S(1)}, u32[]{:S(2)}, u32[]{:S(2)}) collective-permute-start(bf16[2,64,2048]{2,1,0:T(8,128)(2,1)S(1)} %add_convert_fusion.2), channel_id=1, source_target_pairs={{0,96},{32,64},{64,32},{96,0},{16,48},{48,16},{80,112},{112,80},{1... | collective-permute-start | bytes 1572872 | tf_op jit(solution)/shard_map/ppermute | solution.py:28
  88.0 14.7 %collective-permute-start.28 = (bf16[2,64,2048]{2,1,0:T(8,128)(2,1)S(1)}, bf16[2,64,2048]{2,1,0:T(8,128)(2,1)S(1)}, u32[]{:S(2)}, u32[]{:S(2)}) collective-permute-start(bf16[2,64,2048]{2,1,0:T(8,128)(2,1)S(1)} %add_convert_fusion.1), channel_id=1, source_target_pairs={{0,32},{32,0},{64,96},{96,64},{16,112},{48,80},{80,48},{112,16},{1... | collective-permute-start | bytes 1572872 | tf_op jit(solution)/shard_map/ppermute | solution.py:28
  88.7 19.1 %collective-permute-start.37 = (bf16[2,64,2048]{2,1,0:T(8,128)(2,1)S(1)}, bf16[2,64,2048]{2,1,0:T(8,128)(2,1)S(1)}, u32[]{:S(2)}, u32[]{:S(2)}) collective-permute-start(bf16[2,64,2048]{2,1,0:T(8,128)(2,1)S(1)} %add_convert_fusion), channel_id=1, source_target_pairs={{0,96},{32,64},{64,32},{96,0},{16,48},{48,16},{80,112},{112,80},{1... | collective-permute-start | bytes 1572872 | tf_op jit(solution)/shard_map/ppermute | solution.py:28
  100.8 9.7 %collective-permute-start.20 = (bf16[64,2048]{1,0:T(8,128)(2,1)S(1)}, bf16[64,2048]{1,0:T(8,128)(2,1)S(1)}, u32[]{:S(2)}, u32[]{:S(2)}) collective-permute-start(bf16[64,2048]{1,0:T(8,128)(2,1)S(1)} %fusion.11), channel_id=1, source_target_pairs={{0,32},{32,0},{64,96},{96,64},{16,112},{48,80},{80,48},{112,16},{1... | collective-permute-start | bytes 786440 | tf_op jit(solution)/shard_map/ppermute | solution.py:28
  102.8 10.2 %collective-permute-start.29 = (bf16[64,2048]{1,0:T(8,128)(2,1)S(1)}, bf16[64,2048]{1,0:T(8,128)(2,1)S(1)}, u32[]{:S(2)}, u32[]{:S(2)}) collective-permute-start(bf16[64,2048]{1,0:T(8,128)(2,1)S(1)} %fusion.13), channel_id=1, source_target_pairs={{0,96},{32,64},{64,32},{96,0},{16,48},{48,16},{80,112},{112,80},{1... | collective-permute-start | bytes 786440 | tf_op jit(solution)/shard_map/ppermute | solution.py:28
  107.9 12.1 %collective-permute-start.38 = (bf16[64,2048]{1,0:T(8,128)(2,1)S(1)}, bf16[64,2048]{1,0:T(8,128)(2,1)S(1)}, u32[]{:S(2)}, u32[]{:S(2)}) collective-permute-start(bf16[64,2048]{1,0:T(8,128)(2,1)S(1)} %fusion.15), channel_id=1, source_target_pairs={{0,32},{32,0},{64,96},{96,64},{16,112},{48,80},{80,48},{112,16},{1... | collective-permute-start | bytes 786440 | tf_op jit(solution)/shard_map/ppermute | solution.py:28
  110.7 9.1 %collective-permute-start.21 = (bf16[64,2048]{1,0:T(8,128)(2,1)S(1)}, bf16[64,2048]{1,0:T(8,128)(2,1)S(1)}, u32[]{:S(2)}, u32[]{:S(2)}) collective-permute-start(bf16[64,2048]{1,0:T(8,128)(2,1)S(1)} %fusion.5), channel_id=1, source_target_pairs={{0,32},{32,0},{64,96},{96,64},{16,112},{48,80},{80,48},{112,16},{1... | collective-permute-start | bytes 786440 | tf_op jit(solution)/shard_map/ppermute | solution.py:28
  119.9 9.3 %collective-permute-start.22 = (bf16[2,64,2048]{2,1,0:T(8,128)(2,1)S(1)}, bf16[2,64,2048]{2,1,0:T(8,128)(2,1)S(1)}, u32[]{:S(2)}, u32[]{:S(2)}) collective-permute-start(bf16[2,64,2048]{2,1,0:T(8,128)(2,1)S(1)} %pad_maximum_fusion.6), channel_id=1, source_target_pairs={{0,96},{32,64},{64,32},{96,0},{16,48},{48,16},{80,112},{112,80},{1... | collective-permute-start | bytes 1572872 | tf_op jit(solution)/shard_map/ppermute | solution.py:28
  121.6 17.9 %collective-permute-start.31 = (bf16[2,64,2048]{2,1,0:T(8,128)(2,1)S(1)}, bf16[2,64,2048]{2,1,0:T(8,128)(2,1)S(1)}, u32[]{:S(2)}, u32[]{:S(2)}) collective-permute-start(bf16[2,64,2048]{2,1,0:T(8,128)(2,1)S(1)} %pad_maximum_fusion.7), channel_id=1, source_target_pairs={{0,32},{32,0},{64,96},{96,64},{16,112},{48,80},{80,48},{112,16},{1... | collective-permute-start | bytes 1572872 | tf_op jit(solution)/shard_map/ppermute | solution.py:28
  127.4 16.9 %collective-permute-start.40 = (bf16[2,64,2048]{2,1,0:T(8,128)(2,1)S(1)}, bf16[2,64,2048]{2,1,0:T(8,128)(2,1)S(1)}, u32[]{:S(2)}, u32[]{:S(2)}) collective-permute-start(bf16[2,64,2048]{2,1,0:T(8,128)(2,1)S(1)} %pad_maximum_fusion.8), channel_id=1, source_target_pairs={{0,96},{32,64},{64,32},{96,0},{16,48},{48,16},{80,112},{112,80},{1... | collective-permute-start | bytes 1572872 | tf_op jit(solution)/shard_map/ppermute | solution.py:28
  129.3 16.6 %collective-permute-start.23 = (bf16[4,64,2048]{2,1,0:T(8,128)(2,1)S(1)}, bf16[4,64,2048]{2,1,0:T(8,128)(2,1)S(1)}, u32[]{:S(2)}, u32[]{:S(2)}) collective-permute-start(bf16[4,64,2048]{2,1,0:T(8,128)(2,1)S(1)} %pad_maximum_fusion.same), channel_id=1, source_target_pairs={{0,16},{16,0},{1,17},{17,1},{2,18},{18,2},{3,19},{19,3},{4,20},{20... | collective-permute-start | bytes 3145736 | tf_op jit(solution)/shard_map/ppermute | solution.py:45
  139.6 10.7 %collective-permute-start.32 = (bf16[4,64,2048]{2,1,0:T(8,128)(2,1)S(1)}, bf16[4,64,2048]{2,1,0:T(8,128)(2,1)S(1)}, u32[]{:S(2)}, u32[]{:S(2)}) collective-permute-start(bf16[4,64,2048]{2,1,0:T(8,128)(2,1)S(1)} %pad_maximum_fusion.1.same), channel_id=1, source_target_pairs={{0,16},{16,0},{1,17},{17,1},{2,18},{18,2},{3,19},{19,3},{4,20},{20... | collective-permute-start | bytes 3145736 | tf_op jit(solution)/shard_map/ppermute | solution.py:45
  144.4 11.8 %collective-permute-start.41 = (bf16[4,64,2048]{2,1,0:T(8,128)(2,1)S(1)}, bf16[4,64,2048]{2,1,0:T(8,128)(2,1)S(1)}, u32[]{:S(2)}, u32[]{:S(2)}) collective-permute-start(bf16[4,64,2048]{2,1,0:T(8,128)(2,1)S(1)} %pad_maximum_fusion.2.same), channel_id=1, source_target_pairs={{0,16},{16,0},{1,17},{17,1},{2,18},{18,2},{3,19},{19,3},{4,20},{20... | collective-permute-start | bytes 3145736 | tf_op jit(solution)/shard_map/ppermute | solution.py:45
  149.9 11.3 %collective-permute-start.24 = (bf16[2,4,32,1024]{3,2,1,0:T(8,128)(2,1)S(1)}, bf16[2,4,32,1024]{3,2,1,0:T(8,128)(2,1)S(1)}, u32[]{:S(2)}, u32[]{:S(2)}) collective-permute-start(bf16[2,4,32,1024]{3,2,1,0:T(8,128)(2,1)S(1)} %get-tuple-element.42), channel_id=1, source_target_pairs={{0,3},{1,2},{2,1},{3,0},{16,17},{17,16},{18,19},{19,18},{4,7},{5,6... | collective-permute-start | bytes 1572872 | tf_op jit(solution)/shard_map/ppermute | solution.py:29
  154.4 12.3 %collective-permute-start.33 = (bf16[2,4,32,1024]{3,2,1,0:T(8,128)(2,1)S(1)}, bf16[2,4,32,1024]{3,2,1,0:T(8,128)(2,1)S(1)}, u32[]{:S(2)}, u32[]{:S(2)}) collective-permute-start(bf16[2,4,32,1024]{3,2,1,0:T(8,128)(2,1)S(1)} %get-tuple-element.47), channel_id=1, source_target_pairs={{0,1},{1,0},{2,3},{3,2},{16,19},{17,18},{18,17},{19,16},{4,5},{5,4... | collective-permute-start | bytes 1572872 | tf_op jit(solution)/shard_map/ppermute | solution.py:29
  160.3 13.4 %collective-permute-start.42 = (bf16[2,4,32,1024]{3,2,1,0:T(8,128)(2,1)S(1)}, bf16[2,4,32,1024]{3,2,1,0:T(8,128)(2,1)S(1)}, u32[]{:S(2)}, u32[]{:S(2)}) collective-permute-start(bf16[2,4,32,1024]{3,2,1,0:T(8,128)(2,1)S(1)} %get-tuple-element.52), channel_id=1, source_target_pairs={{0,3},{1,2},{2,1},{3,0},{16,17},{17,16},{18,19},{19,18},{4,7},{5,6... | collective-permute-start | bytes 1572872 | tf_op jit(solution)/shard_map/ppermute | solution.py:29
  161.3 13.5 %collective-permute-start.25 = (bf16[4,32,1024]{2,1,0:T(8,128)(2,1)S(1)}, bf16[4,32,1024]{2,1,0:T(8,128)(2,1)S(1)}, u32[]{:S(2)}, u32[]{:S(2)}) collective-permute-start(bf16[4,32,1024]{2,1,0:T(8,128)(2,1)S(1)} %fusion.12), channel_id=1, source_target_pairs={{0,1},{1,0},{2,3},{3,2},{16,19},{17,18},{18,17},{19,16},{4,5},{5,4... | collective-permute-start | bytes 786440 | tf_op jit(solution)/shard_map/ppermute | solution.py:29
  166.7 9.8 %collective-permute-start.34 = (bf16[4,32,1024]{2,1,0:T(8,128)(2,1)S(1)}, bf16[4,32,1024]{2,1,0:T(8,128)(2,1)S(1)}, u32[]{:S(2)}, u32[]{:S(2)}) collective-permute-start(bf16[4,32,1024]{2,1,0:T(8,128)(2,1)S(1)} %fusion.14), channel_id=1, source_target_pairs={{0,3},{1,2},{2,1},{3,0},{16,17},{17,16},{18,19},{19,18},{4,7},{5,6... | collective-permute-start | bytes 786440 | tf_op jit(solution)/shard_map/ppermute | solution.py:29
  (32 other events, 274.2 us)
